TPU v7x, 32 devices: a whole 2x2x4 slice. The times are simulated.
32 devices in a mesh: dp: 32 (over z, y, x, core).
Axes of the slice: x: 2, y: 2, z: 4, core: 2. Of those that a mesh axis runs over, the one named last changes fastest.
Arguments:
- view_a: bfloat16 [4096, 4096], P('dp'), may hold values from -120 to 120
- view_b: bfloat16 [4096, 4096], P('dp'), may hold values from -120 to 120
Outputs:
- loss: float32 [], replicated
- grad_a: bfloat16 [4096, 4096], P('dp')
- grad_b: bfloat16 [4096, 4096], P('dp')
All inputs are finite; a program needn't handle non-finite values.
Results may differ from a plain program's by a relative error of at most 0.0034.
Values may be sent and summed in bfloat16 or wider, within the bound.
No kernel may reach another device: no remote copies, remote signals or barrier semaphores. Data moves between devices by JAX's collectives and lax.ppermute only.
A program may use at most 192 MiB of HBM per device.

v0:
```python
import jax
import jax.numpy as jnp
from jax import lax
from jax.sharding import PartitionSpec as P

lam = 0.0051
eps = 1e-05


def shards(view_a, view_b):
    rows = view_a.shape[0]
    width = view_a.shape[1]
    devices = lax.axis_size("dp")
    count = rows * devices
    full_a = view_a.astype(jnp.float32)
    full_b = view_b.astype(jnp.float32)
    sums = lax.psum(
        (
            jnp.sum(full_a, axis=0),
            jnp.sum(full_a * full_a, axis=0),
            jnp.sum(full_b, axis=0),
            jnp.sum(full_b * full_b, axis=0),
        ),
        "dp",
    )
    mean_a = sums[0] / count
    mean_b = sums[2] / count
    inv_a = 1.0 / jnp.sqrt(sums[1] / count - mean_a * mean_a + eps)
    inv_b = 1.0 / jnp.sqrt(sums[3] / count - mean_b * mean_b + eps)
    flat_a = (full_a - mean_a) * inv_a
    flat_b = (full_b - mean_b) * inv_b
    norm_a = flat_a.astype(jnp.bfloat16)
    norm_b = flat_b.astype(jnp.bfloat16)
    owned = width // devices
    block = norm_a
    corr = (
        lax.psum_scatter(
            lax.dot_general(
                block, norm_b, (((0,), (0,)), ((), ())), preferred_element_type=jnp.float32
            ),
            "dp",
            scatter_dimension=0,
            tiled=True,
        )
        / count
    )
    first = lax.axis_index("dp") * owned
    diag_mask = lax.broadcasted_iota(jnp.int32, (owned, width), 0) + first == lax.broadcasted_iota(
        jnp.int32, (owned, width), 1
    )
    diag_sq = jnp.where(diag_mask, corr * corr, 0.0)
    diag_miss = jnp.where(diag_mask, (1.0 - corr) ** 2, 0.0)
    loss_part = jnp.sum(diag_miss) + lam * (jnp.sum(corr * corr) - jnp.sum(diag_sq))
    loss = lax.psum(loss_part, "dp")
    gcorr = jnp.where(diag_mask, 2.0 * (corr - 1.0), 2.0 * lam * corr).astype(jnp.bfloat16)
    piece = lax.all_gather(gcorr, "dp", axis=0, tiled=True)
    cross = lax.dot_general(
        norm_b, piece, (((1,), (1,)), ((), ())), preferred_element_type=jnp.float32
    )
    block = norm_a
    grad_nb = jnp.dot(block, piece, preferred_element_type=jnp.float32)
    stats = lax.psum(
        (
            jnp.sum(cross, axis=0),
            jnp.sum(cross * flat_a, axis=0),
            jnp.sum(grad_nb, axis=0),
            jnp.sum(grad_nb * flat_b, axis=0),
        ),
        "dp",
    )
    grad_a = (inv_a * (cross - stats[0] / count - flat_a * (stats[1] / count))).astype(jnp.bfloat16)
    grad_b = (inv_b * (grad_nb - stats[2] / count - flat_b * (stats[3] / count))).astype(
        jnp.bfloat16
    )
    return (loss, grad_a, grad_b)


def solution(mesh):
    return jax.shard_map(
        shards,
        mesh=mesh,
        in_specs=(P("dp", None), P("dp", None)),
        out_specs=(P(), P("dp", None), P("dp", None)),
        check_vma=False,
    )
```

profile of v0, /device:TPU:0, one launch (start us, length us, event | category | flops | bytes accessed | tf_op | source)
XLA Modules:
  0.0 1156.7 jit_solution(5889201687892482890)
XLA Ops:
  7.2 0.0 copy-start
  7.2 0.0 copy-start.1
  7.2 0.0 all-reduce.5.cloned.1.call-start
  7.2 2.3 convert_reduce_fusion.1
  9.5 2.2 convert_reduce_fusion
  11.7 0.0 all-reduce.5.cloned.1.call-update
  11.7 0.0 reduce-scatter.2.cloned.1.call-start
  11.8 124.8 %all-reduce.5.cloned.1.call-done = (f32[4096]{0:T(1024)}, f32[4096]{0:T(1024)}, f32[4096]{0:T(1024)}, f32[4096]{0:T(1024)}) async-done(((f32[4096]{0:T(1024)}, f32[4096]{0:T(1024)}, f32[4096]{0:T(1024)}, f32[4096]{0:T(1024)}), (f32[4096]{0:T(1024)}, f32[4096]{0:T(1024)}, f32[4096]{0:T(1024)}, f32[4096]{0:T(1024)})) %all-reduce.5.cloned.1.call-update) | async-done | bytes 65552 | tf_op jit(solution)/shard_map/psum | solution.py:17
  136.6 0.8 broadcast_multiply_fusion.4
  137.3 0.0 copy-done
  137.4 0.0 copy-done.1
  137.4 23.2 %fusion.20 = f32[4096,4096]{1,0:T(8,128)} fusion(bf16[128,4096]{1,0:T(8,128)(2,1)S(1)} %copy-done.1, f32[4096]{0:T(1024)S(1)} %get-tuple-element.27, f32[4096]{0:T(1024)S(1)} %get-tuple-element.26, bf16[128,4096]{1,0:T(8,128)(2,1)S(1)} %copy-done, f32[4096]{0:T(1024)S(1)} %get-tuple-element.30, f32[4096]{0:T(1024)S(1)} %get-tuple-element.31), kind=kOutput, calls=%fused_computation.30 | convolution fusion | flops 4299161600 | bytes 69271552 | tf_op jit(solution)/shard_map/dot_general | solution.py:38
  160.6 0.0 reduce-scatter.2.cloned.1.call-update
  160.6 0.2 all-gather.2.cloned.1.call-start
  160.8 703.7 %reduce-scatter.2.cloned.1.call-done = f32[128,4096]{1,0:T(8,128)} async-done(((f32[4096,4096]{1,0:T(8,128)}), f32[128,4096]{1,0:T(8,128)}) %reduce-scatter.2.cloned.1.call-update) | async-done | bytes 2097168 | tf_op jit(solution)/shard_map/reduce_scatter | solution.py:37
  864.5 4.2 select_reduce_fusion
  868.8 0.0 all-gather.2.cloned.1.call-update
  870.8 200.7 %all-gather.2.cloned.1.call-done = bf16[4096,4096]{1,0:T(8,128)(2,1)} async-done(((bf16[128,4096]{1,0:T(8,128)(2,1)}), bf16[4096,4096]{1,0:T(8,128)(2,1)}) %all-gather.2.cloned.1.call-update) | async-done | bytes 33554448 | tf_op jit(solution)/shard_map/all_gather | solution.py:56
  1071.4 16.8 %fusion.25 = (f32[4096]{0:T(1024)S(1)}, f32[4096]{0:T(1024)S(1)}, f32[128,4096]{1,0:T(8,128)}) fusion(f32[4096]{0:T(1024)S(1)} %get-tuple-element.27, f32[4096]{0:T(1024)S(1)} %get-tuple-element.26, bf16[128,4096]{1,0:T(8,128)(2,1)S(1)} %copy-done.1, bf16[4096,4096]{1,0:T(8,128)(2,1)} %all-gather.2.cloned.1.call-done, bf16[128,4096]{1,0:T(8,128)(2,1)S(1)} %copy-done, ...), kind=kOutput, calls=%fused_computation.41 | convolution fusion | flops 4300201984 | bytes 37847040 | tf_op jit(solution)/shard_map/dot_general | solution.py:61
  1088.2 17.6 %fusion.26 = (f32[4096]{0:T(1024)S(1)}, f32[4096]{0:T(1024)S(1)}, f32[128,4096]{1,0:T(8,128)}) fusion(f32[4096]{0:T(1024)S(1)} %get-tuple-element.30, f32[4096]{0:T(1024)S(1)} %get-tuple-element.31, bf16[128,4096]{1,0:T(8,128)(2,1)S(1)} %copy-done, bf16[4096,4096]{1,0:T(8,128)(2,1)} %all-gather.2.cloned.1.call-done, bf16[128,4096]{1,0:T(8,128)(2,1)S(1)} %copy-done.1, ...), kind=kOutput, calls=%fused_computation.42 | convolution fusion | flops 4300201984 | bytes 37847040 | tf_op jit(solution)/shard_map/dot_general | solution.py:57
  1105.9 39.5 %all-reduce.6 = (f32[]{:T(128)}, f32[4096]{0:T(1024)S(1)}, f32[4096]{0:T(1024)S(1)}, f32[4096]{0:T(1024)S(1)}, f32[4096]{0:T(1024)S(1)}) all-reduce(f32[]{:T(128)S(6)} %add.41, f32[4096]{0:T(1024)S(1)} %get-tuple-element.8, f32[4096]{0:T(1024)S(1)} %get-tuple-element.7, ...), channel_id=1, replica_groups=mesh['dp'=32] {'dp'}, use_global_device_ids=true, to_apply=%region_12.13 | all-reduce | flops 16385 | bytes 131080 | tf_op jit(solution)/shard_map/psum | solution.py:54
  1145.4 0.0 copy-start.2
  1145.4 3.2 fusion.16
  1148.6 0.0 copy-done.2
  1148.6 1.5 fusion.7
  (5 shorter events, 0.0 us)
Async XLA Ops:
  7.2 130.2 %copy-start = (bf16[128,4096]{1,0:T(8,128)(2,1)S(1)}, bf16[128,4096]{1,0:T(8,128)(2,1)}, u32[]{:S(2)}) copy-start(bf16[128,4096]{1,0:T(8,128)(2,1)} %param.2) | copy-start | bytes 3145732
  7.2 130.2 %copy-start.1 = (bf16[128,4096]{1,0:T(8,128)(2,1)S(1)}, bf16[128,4096]{1,0:T(8,128)(2,1)}, u32[]{:S(2)}) copy-start(bf16[128,4096]{1,0:T(8,128)(2,1)} %param.3) | copy-start | bytes 3145732
  7.2 129.4 %all-reduce.5.cloned.1.call-start = ((), (), s32[]{:S(2)}) async-start(), calls=%async_computation.3 | async-start | bytes 131072 | tf_op jit(solution)/shard_map/psum | solution.py:17
  11.7 852.8 %reduce-scatter.2.cloned.1.call-start = ((), (), s32[]{:S(2)}) async-start(), calls=%async_computation.1 | async-start | bytes 69206016 | tf_op jit(solution)/shard_map/reduce_scatter | solution.py:37
  160.6 910.8 %all-gather.2.cloned.1.call-start = ((), (), s32[]{:S(2)}) async-start(), calls=%async_computation.2 | async-start | bytes 34603008 | tf_op jit(solution)/shard_map/all_gather | solution.py:56
  1145.4 3.2 copy-start.2
Sparse Core Ops, SparseCore 0:
  14.7 121.7 all-reduce.4
  160.7 703.7 reduce-scatter.1
  868.9 202.4 all-gather.1
where the time goes:
time: 1160 us
  waiting for transfers between devices  1030 us (89%)
  matrix products  57.6 us (5%)
  blocking collectives  39.5 us (3%)
  between operations  15.8 us (1%)
  other arithmetic  14.2 us (1%)
    reduce_scatter x1, waiting for transfers between devices, shards(): lax.psum_scatter(lax.dot_general(block, norm_b, (((0,), (0,)), ((), ())),...  704 us
    all_gather x1, waiting for transfers between devices, shards(): piece = lax.all_gather(gcorr, 'dp', axis=0, tiled=True)  201 us
    psum x1, waiting for transfers between devices, shards(): lax.psum((jnp.sum(full_a, axis=0), jnp.sum(full_a * full_a, axis=0), jnp....  125 us
    psum x1, blocking collectives, shards(): loss = lax.psum(loss_part, 'dp')  39.5 us
  transfers between devices with their start and end apart: 3, of which 3 were waited for; matrix products, arithmetic and copies ran while one was open for 0% of the time, Pallas kernels for 0%

commit v1 on v0

v1 whole, which is shorter than its diff:
```python
import jax
import jax.numpy as jnp
from jax import lax
from jax.sharding import PartitionSpec as P

lam = 0.0051
eps = 1e-05

cube = 8
orders = ((4, 2, 1), (2, 1, 4), (1, 4, 2))


def offset(order, place):
    return sum(bit for step, bit in enumerate(order) if place >> step & 1)


def places(order):
    return [offset(order, place) for place in range(cube)]


def cuts(rows):
    part = -(-rows // 48) * 16
    return (0, part, 2 * part, rows)


def shards(view_a, view_b):
    f32, bf16 = jnp.float32, jnp.bfloat16
    rows, width = view_a.shape
    devices = lax.axis_size("dp")
    count = rows * devices
    cubes = devices // (2 * cube)
    index = lax.axis_index("dp")
    c, k, h = index % 2, index // 2 % cube, index // (2 * cube)
    wide, half, narrow = width // cubes, width // cubes // 2, width // cube

    def swap(x, mask):
        return lax.ppermute(x, "dp", [(i, i ^ mask) for i in range(devices)])

    def swap_k(x, bit):
        return swap(x, 2 * bit)

    def turn(x, step):
        return lax.ppermute(
            x, "dp", [(i, (i + 2 * cube * step) % devices) for i in range(devices)]
        )

    def columns(x, start, size):
        return lax.dynamic_slice_in_dim(x, start, size, axis=1)

    def pair(mine, other, axis):
        return jnp.where(
            c == 0,
            jnp.concatenate([mine, other], axis),
            jnp.concatenate([other, mine], axis),
        )

    def doubled(x, order, axis):
        for bit in order[:-1]:
            x = jnp.concatenate([x, swap_k(x, bit)], axis)
        return [x, swap_k(x, order[-1])]

    full_a, full_b = view_a.astype(f32), view_b.astype(f32)
    sums = jnp.stack(
        [
            jnp.sum(full_a, axis=0),
            jnp.sum(full_a * full_a, axis=0),
            jnp.sum(full_b, axis=0),
            jnp.sum(full_b * full_b, axis=0),
        ]
    )
    mask = 1
    while mask < devices:
        sums = sums + swap(sums, mask)
        mask *= 2
    means = sums / count
    mean_a, mean_b = means[0:1], means[2:3]
    inv_a = 1.0 / jnp.sqrt(means[1:2] - mean_a * mean_a + eps)
    inv_b = 1.0 / jnp.sqrt(means[3:4] - mean_b * mean_b + eps)

    def flat(x, mean, inv):
        return (x.astype(f32) - mean) * inv

    def norm(x, mean, inv):
        return flat(x, mean, inv).astype(bf16)

    rows_b = [view_b] + [turn(view_b, s) for s in range(1, cubes)]
    far_a = [
        turn(columns(view_a, (h + s) % cubes * wide, wide), s) for s in range(1, cubes)
    ]
    near_a = columns(view_a, h * wide, wide)
    pair_b = jnp.concatenate(rows_b, 0)
    pair_a = jnp.concatenate([near_a] + far_a, 0)

    edges = cuts(rows)
    parts = list(zip(edges, edges[1:], orders))
    own_a = [doubled(view_a[lo:hi], order, 0) for lo, hi, order in parts]
    far = jnp.concatenate(far_a, 1)
    other_a = [doubled(far[lo:hi], order, 0) for lo, hi, order in parts]
    eighths = [columns(pair_b, (k ^ r) * narrow, narrow) for r in range(cube)]
    narrow_b = [eighths[0]] + [swap_k(eighths[r], r) for r in range(1, cube)]

    def ordered_b(s):
        return jnp.concatenate(
            [
                narrow_b[r][s * rows + lo : s * rows + hi]
                for lo, hi, order in parts
                for r in places(order)
            ],
            0,
        )

    all_b = jnp.concatenate([pair_b, swap(pair_b, 1)], 0)
    all_a = jnp.concatenate(
        [columns(pair_a, c * half, half), swap(columns(pair_a, (1 - c) * half, half), 1)], 0
    )

    mean_aw, inv_aw = columns(mean_a, h * wide, wide), columns(inv_a, h * wide, wide)
    mean_bn, inv_bn = columns(mean_b, k * narrow, narrow), columns(inv_b, k * narrow, narrow)
    cube_a = norm(jnp.concatenate([x for pieces in own_a for x in pieces], 0), mean_a, inv_a)
    rest_a = jnp.concatenate([x for pieces in other_a for x in pieces], 0)
    left = jnp.concatenate(
        [columns(cube_a, h * wide, wide)]
        + [
            norm(rest_a[:, s * wide : (s + 1) * wide], mean_aw, inv_aw)
            for s in range(cubes - 1)
        ],
        0,
    )
    near_b = ordered_b(0)
    right = norm(
        jnp.concatenate([near_b] + [ordered_b(s) for s in range(1, cubes)], 0), mean_bn, inv_bn
    )
    partial = lax.dot_general(left, right, (((0,), (0,)), ((), ())), preferred_element_type=f32)
    corr = (
        lax.dynamic_slice_in_dim(partial, c * half, half, 0)
        + swap(lax.dynamic_slice_in_dim(partial, (1 - c) * half, half, 0), 1)
    ) / count
    first_i, first_j = h * wide + c * half, k * narrow
    diag = (
        lax.broadcasted_iota(jnp.int32, (half, narrow), 0) + first_i
        == lax.broadcasted_iota(jnp.int32, (half, narrow), 1) + first_j
    )
    loss = jnp.sum(jnp.where(diag, (1.0 - corr) ** 2, lam * corr * corr))
    gcorr = jnp.where(diag, 2.0 * (corr - 1.0), 2.0 * lam * corr).astype(bf16)

    loss = jnp.full((8, 128), loss, f32)
    mask = 1
    while mask < devices:
        loss = loss + swap(loss, mask)
        mask *= 2

    turned = [gcorr] + [turn(gcorr, s) for s in range(1, cubes)]
    across = jnp.zeros((cubes, half, narrow), bf16)
    for s, block in enumerate(turned):
        across = lax.dynamic_update_slice_in_dim(across, block[None], (h - s) % cubes, 0)
    sibling = swap(across, 1)
    rows_g = pair(across, sibling, 1).reshape(width, narrow)
    grad_nb = jnp.dot(cube_a, rows_g, preferred_element_type=f32)
    flat_b = flat(near_b, mean_bn, inv_bn)
    stats_b = jnp.stack([jnp.sum(grad_nb, axis=0), jnp.sum(grad_nb * flat_b, axis=0)])
    stats_b = stats_b + swap(stats_b, 1)
    mask = 2 * cube
    while mask < devices:
        stats_b = stats_b + swap(stats_b, mask)
        mask *= 2
    stats_b = stats_b / count
    out_b = (inv_bn * (grad_nb - stats_b[0:1] - flat_b * stats_b[1:2])).astype(bf16)

    norm_b = norm(all_b, mean_b, inv_b)
    edges_g = cuts(half)
    cross = []
    for lo, hi, order in zip(edges_g, edges_g[1:], orders):
        arranged = jnp.concatenate(
            [columns(norm_b, (k ^ r) * narrow, narrow) for r in places(order)], 1
        )
        pieces = doubled(gcorr[lo:hi], order, 1)
        total = 0.0
        for n, piece in enumerate(pieces):
            total = total + lax.dot_general(
                arranged[:, n * width // 2 : (n + 1) * width // 2],
                piece,
                (((1,), (1,)), ((), ())),
                preferred_element_type=f32,
            )
        cross.append(total)
    cross = jnp.concatenate(cross, 1)
    mean_ah, inv_ah = columns(mean_a, first_i, half), columns(inv_a, first_i, half)
    flat_a = flat(all_a, mean_ah, inv_ah)
    stats_a = jnp.stack([jnp.sum(cross, axis=0), jnp.sum(cross * flat_a, axis=0)])
    for bit in (1, 2, 4):
        stats_a = stats_a + swap_k(stats_a, bit)
    stats_a = stats_a / count
    out_a = (inv_ah * (cross - stats_a[0:1] - flat_a * stats_a[1:2])).astype(bf16)

    start, blocks = 0, {}
    for lo, hi, order in parts:
        for r in places(order):
            blocks.setdefault(r, []).append(out_b[start : start + hi - lo])
            start += hi - lo
    grad_b = jnp.zeros((rows, width), bf16)
    for r in range(cube):
        block = jnp.concatenate(blocks[r], 0)
        block = swap_k(block, r) if r else block
        grad_b = lax.dynamic_update_slice_in_dim(grad_b, block, (k ^ r) * narrow, 1)
    mine = cubes * rows
    both = pair(out_a[:mine], swap(out_a[mine:], 1), 1)
    grad_a = jnp.zeros((rows, width), bf16)
    for s in range(cubes):
        block = both[s * rows : (s + 1) * rows]
        block = turn(block, -s) if s else block
        grad_a = lax.dynamic_update_slice_in_dim(grad_a, block, (h + s) % cubes * wide, 1)
    return (loss[0, 0], grad_a, grad_b)


def solution(mesh):
    return jax.shard_map(
        shards,
        mesh=mesh,
        in_specs=(P("dp", None), P("dp", None)),
        out_specs=(P(), P("dp", None), P("dp", None)),
        check_vma=False,
    )
```

time: 1160 us -> 572 us (0.49)
  waiting for transfers between devices: 1030 us -> 278 us
  local copies, waits for them, and re-layouts: 0.01 us -> 117 us
  starting transfers between devices: 0.3 us -> 79.7 us
  other arithmetic: 14.2 us -> 64.1 us
  blocking collectives: 39.5 us -> 0 us
  matrix products: 57.6 us -> 21.6 us
  between operations: 15.8 us -> 2.16 us
    reduce_scatter x1 -> x0, waiting for transfers between devices: 704 us -> none  [shards(): lax.psum_scatter(lax.dot_general(block, norm_b, (((0,), (0,)), ((), ())),...]
    ppermute x0 -> x65, waiting for transfers between devices: none -> 278 us  [the longest x61 278 us: swap(): return lax.ppermute(x, 'dp', [(i, i ^ mask) for i in range(devices)])]
    all_gather x1 -> x0, waiting for transfers between devices: 201 us -> none  [shards(): piece = lax.all_gather(gcorr, 'dp', axis=0, tiled=True)]
    psum x1 -> x0, waiting for transfers between devices: 125 us -> none  [shards(): lax.psum((jnp.sum(full_a, axis=0), jnp.sum(full_a * full_a, axis=0), jnp....]
    ppermute x0 -> x65, starting transfers between devices: none -> 79.7 us  [the longest x61 68.5 us: swap(): return lax.ppermute(x, 'dp', [(i, i ^ mask) for i in range(devices)])]
    unnamed x6 -> x175, local copies, waits for them, and re-layouts: 0.01 us -> 71.4 us
    psum x1 -> x0, blocking collectives: 39.5 us -> none  [shards(): loss = lax.psum(loss_part, 'dp')]
    dot_general x3 -> x8, matrix products: 57.6 us -> 21.6 us  [the longest x6 9.56 us: shards(): lax.dot_general(arranged[:, n * width // 2:(n + 1) * width // 2], piece,...]
  transfers between devices with their start and end apart: 3 -> 65, of which waited for: 3 -> 34; matrix products, arithmetic and copies ran while one was open for 0% -> 29% of each run, Pallas kernels for 0% -> 0%
where the time goes in v1:
time: 572 us; the launch traced here: 563 us
  waiting for transfers between devices  278 us (49%)
  local copies, waits for them, and re-layouts  117 us (20%)
  starting transfers between devices  79.7 us (14%)
  other arithmetic  64.1 us (11%)
  matrix products  21.6 us (4%)
    ppermute x61, waiting for transfers between devices, swap(): return lax.ppermute(x, 'dp', [(i, i ^ mask) for i in range(devices)])  278 us
    unnamed x175, local copies, waits for them, and re-layouts  71.4 us
    ppermute x61, starting transfers between devices, swap(): return lax.ppermute(x, 'dp', [(i, i ^ mask) for i in range(devices)])  68.5 us
    concatenate x18, other arithmetic, doubled(): x = jnp.concatenate([x, swap_k(x, bit)], axis)  26.2 us
    convert_element_type x3, other arithmetic, norm(): return flat(x, mean, inv).astype(bf16)  15.6 us
    ppermute x7, local copies, waits for them, and re-layouts, swap(): return lax.ppermute(x, 'dp', [(i, i ^ mask) for i in range(devices)])  12.1 us
  transfers between devices with their start and end apart: 65, of which 34 were waited for; matrix products, arithmetic and copies ran while one was open for 29% of the time, Pallas kernels for 0%

profile of v1, /device:TPU:0, one launch (start us, length us, event | category | flops | bytes accessed | tf_op | source)
XLA Modules:
  0.0 562.6 jit_solution(473986026519460416)
XLA Ops:
  5.5 2.9 collective-permute-start.10
  8.4 2.6 collective-permute-start.24
  14.0 2.7 collective-permute-start.14
  19.6 27.6 %collective-permute-done.12 = f32[4,4096]{1,0:T(4,128)S(1)} collective-permute-done((f32[4,4096]{1,0:T(4,128)S(1)}, f32[4,4096]{1,0:T(4,128)S(1)}, u32[]{:S(2)}, u32[]{:S(2)}) %collective-permute-start.12) | collective-permute-done | bytes 65568 | tf_op jit(solution)/shard_map/ppermute | solution.py:37
  47.2 2.4 collective-permute-start.13
  50.7 31.4 %collective-permute-done.13 = f32[4,4096]{1,0:T(4,128)} collective-permute-done((f32[4,4096]{1,0:T(4,128)S(1)}, f32[4,4096]{1,0:T(4,128)}, u32[]{:S(2)}, u32[]{:S(2)}) %collective-permute-start.13) | collective-permute-done | bytes 65568 | tf_op jit(solution)/shard_map/ppermute | solution.py:37
  98.0 11.1 %collective-permute-done.21 = bf16[32,2048]{0,1:T(8,128)(2,1)S(1)} collective-permute-done((bf16[32,2048]{0,1:T(8,128)(2,1)}, bf16[32,2048]{0,1:T(8,128)(2,1)S(1)}, u32[]{:S(2)}, u32[]{:S(2)}) %collective-permute-start.21) | collective-permute-done | bytes 131104 | tf_op jit(solution)/shard_map/ppermute | solution.py:37
  126.1 2.6 pad_maximum_fusion.28
  131.5 2.3 constant_dynamic-update-slice_fusion.24
  133.8 2.8 constant_dynamic-slice_fusion.14
  140.8 2.9 pad_maximum_fusion.16
  146.6 2.9 pad_maximum_fusion.17
  149.6 2.4 copy.14
  163.6 2.5 collective-permute-start.30
  168.9 5.9 %collective-permute-done.28 = bf16[256,512]{1,0:T(8,128)(2,1)S(1)} collective-permute-done((bf16[256,512]{1,0:T(8,128)(2,1)}, bf16[256,512]{1,0:T(8,128)(2,1)S(1)}, u32[]{:S(2)}, u32[]{:S(2)}) %collective-permute-start.28) | collective-permute-done | bytes 262176 | tf_op jit(solution)/shard_map/ppermute | solution.py:37
  175.4 4.3 collective-permute-start.20
  218.0 12.1 %collective-permute-done.2 = bf16[192,4096]{1,0:T(8,128)(2,1)S(1)} collective-permute-done((bf16[192,4096]{1,0:T(8,128)(2,1)S(1)}, bf16[192,4096]{1,0:T(8,128)(2,1)S(1)}, u32[]{:S(2)}, u32[]{:S(2)}) %collective-permute-start.2) | collective-permute-done | bytes 1572896 | tf_op jit(solution)/shard_map/ppermute | solution.py:37
  235.5 5.5 collective-permute-done.3
  248.7 10.3 %collective-permute-done.4 = bf16[96,4096]{1,0:T(8,128)(2,1)} collective-permute-done((bf16[96,4096]{1,0:T(8,128)(2,1)}, bf16[96,4096]{1,0:T(8,128)(2,1)}, u32[]{:S(2)}, u32[]{:S(2)}) %collective-permute-start.4) | collective-permute-done | bytes 786464 | tf_op jit(solution)/shard_map/ppermute | solution.py:37
  267.0 25.9 %collective-permute-done.5 = bf16[192,4096]{1,0:T(8,128)(2,1)S(1)} collective-permute-done((bf16[192,4096]{1,0:T(8,128)(2,1)S(1)}, bf16[192,4096]{1,0:T(8,128)(2,1)S(1)}, u32[]{:S(2)}, u32[]{:S(2)}) %collective-permute-start.5) | collective-permute-done | bytes 1572896 | tf_op jit(solution)/shard_map/ppermute | solution.py:37
  298.1 3.2 collective-permute-done.6
  303.0 7.6 %collective-permute-done.7 = bf16[64,4096]{1,0:T(8,128)(2,1)S(1)} collective-permute-done((bf16[64,4096]{1,0:T(8,128)(2,1)S(1)}, bf16[64,4096]{1,0:T(8,128)(2,1)S(1)}, u32[]{:S(2)}, u32[]{:S(2)}) %collective-permute-start.7) | collective-permute-done | bytes 524320 | tf_op jit(solution)/shard_map/ppermute | solution.py:37
  311.9 3.3 multiply_convert_fusion.2
  316.7 12.7 %collective-permute-done.8 = bf16[128,4096]{1,0:T(8,128)(2,1)S(1)} collective-permute-done((bf16[128,4096]{1,0:T(8,128)(2,1)S(1)}, bf16[128,4096]{1,0:T(8,128)(2,1)S(1)}, u32[]{:S(2)}, u32[]{:S(2)}) %collective-permute-start.8) | collective-permute-done | bytes 1048608 | tf_op jit(solution)/shard_map/ppermute | solution.py:37
  330.5 9.6 %multiply_convert_fusion = bf16[1024,4096]{1,0:T(8,128)(2,1)} fusion(bf16[1024,4096]{1,0:T(8,128)(2,1)} %constant_dynamic-update-slice_fusion, f32[4096]{0:T(1024)S(1)} %bitcast.46, f32[4096]{0:T(1024)S(1)} %bitcast.47), kind=kLoop, calls=%fused_computation | loop fusion | flops 16777216 | bytes 16809984 | tf_op jit(solution)/shard_map/convert_element_type | solution.py:84
  340.2 2.9 constant_dynamic-slice_fusion.24
  344.3 4.8 fusion
  351.7 6.7 %collective-permute-done.32 = f32[1024,512]{1,0:T(8,128)} collective-permute-done((f32[1024,512]{1,0:T(8,128)S(1)}, f32[1024,512]{1,0:T(8,128)}, u32[]{:S(2)}, u32[]{:S(2)}) %collective-permute-start.32) | collective-permute-done | bytes 2097184 | tf_op jit(solution)/shard_map/ppermute | solution.py:37
  358.5 3.7 bitcast_dynamic-update-slice_fusion.1
  366.6 6.5 %collective-permute-done.45 = bf16[320,512]{1,0:T(8,128)(2,1)S(1)} collective-permute-done((bf16[320,512]{1,0:T(8,128)(2,1)S(1)}, bf16[320,512]{1,0:T(8,128)(2,1)S(1)}, u32[]{:S(2)}, u32[]{:S(2)}) %collective-permute-start.45) | collective-permute-done | bytes 327712 | tf_op jit(solution)/shard_map/ppermute | solution.py:37
  382.3 15.7 %collective-permute-done.39 = bf16[352,512]{1,0:T(8,128)(2,1)} collective-permute-done((bf16[352,512]{1,0:T(8,128)(2,1)S(1)}, bf16[352,512]{1,0:T(8,128)(2,1)}, u32[]{:S(2)}, u32[]{:S(2)}) %collective-permute-start.39) | collective-permute-done | bytes 360480 | tf_op jit(solution)/shard_map/ppermute | solution.py:37
  404.8 2.7 multiply_convert_fusion.1
  408.0 3.6 collective-permute-start.54
  411.6 6.6 %collective-permute-done.40 = bf16[352,1024]{1,0:T(8,128)(2,1)S(1)} collective-permute-done((bf16[352,1024]{1,0:T(8,128)(2,1)S(1)}, bf16[352,1024]{1,0:T(8,128)(2,1)S(1)}, u32[]{:S(2)}, u32[]{:S(2)}) %collective-permute-start.40) | collective-permute-done | bytes 720928 | tf_op jit(solution)/shard_map/ppermute | solution.py:37
  421.2 22.5 %collective-permute-done.47 = bf16[320,2048]{1,0:T(8,128)(2,1)S(1)} collective-permute-done((bf16[320,2048]{1,0:T(8,128)(2,1)S(1)}, bf16[320,2048]{1,0:T(8,128)(2,1)S(1)}, u32[]{:S(2)}, u32[]{:S(2)}) %collective-permute-start.47) | collective-permute-done | bytes 1310752 | tf_op jit(solution)/shard_map/ppermute | solution.py:37
  446.8 10.9 %collective-permute-done.44 = bf16[352,2048]{1,0:T(8,128)(2,1)S(1)} collective-permute-done((bf16[352,2048]{1,0:T(8,128)(2,1)S(1)}, bf16[352,2048]{1,0:T(8,128)(2,1)S(1)}, u32[]{:S(2)}, u32[]{:S(2)}) %collective-permute-start.44) | collective-permute-done | bytes 1441824 | tf_op jit(solution)/shard_map/ppermute | solution.py:37
  473.5 3.6 collective-permute-done.51
  477.2 2.4 multiply_convert_fusion.6
  480.4 3.1 fusion.6
  491.1 3.1 collective-permute-done.35
  494.2 3.6 collective-permute-done.36
  497.8 2.4 collective-permute-start.37
  503.1 3.4 maximum_select_fusion
  506.6 7.3 %fusion.75 = (f32[512]{0:T(512)S(1)}, f32[512]{0:T(512)S(1)}, f32[1024,512]{1,0:T(8,128)S(1)}) fusion(f32[512]{0:T(512)S(1)} %bitcast.71, f32[512]{0:T(512)S(1)} %bitcast.74, bf16[1024,512]{1,0:T(8,128)(2,1)S(1)} %copy-done.26, bf16[1024,4096]{1,0:T(8,128)(2,1)} %multiply_convert_fusion, bf16[4096,512]{1,0:T(8,128)(2,1)S(1)} %bitcast.33), kind=kOutput, calls=%fused_computation.268 | convolution fusion | flops 4298112000 | bytes 15736832 | tf_op jit(solution)/shard_map/dot_general | solution.py:158
  515.1 2.4 collective-permute-start.53
  518.3 23.7 %collective-permute-done.57 = f32[2,512]{1,0:T(2,128)S(1)} collective-permute-done((f32[2,512]{1,0:T(2,128)S(1)}, f32[2,512]{1,0:T(2,128)S(1)}, u32[]{:S(2)}, u32[]{:S(2)}) %collective-permute-start.57) | collective-permute-done | bytes 4128 | tf_op jit(solution)/shard_map/ppermute | solution.py:37
  549.9 2.6 collective-permute-done.59
  556.8 2.4 collective-permute-done.63
  (379 shorter events, 214.4 us)
Async XLA Ops:
  8.4 123.1 %collective-permute-start.24 = (bf16[128,4096]{1,0:T(8,128)(2,1)S(1)}, bf16[128,4096]{1,0:T(8,128)(2,1)}, u32[]{:S(2)}, u32[]{:S(2)}) collective-permute-start(bf16[128,4096]{1,0:T(8,128)(2,1)S(1)} %copy-done.3), channel_id=1, source_target_pairs={{0,16},{1,17},{2,18},{3,19},{4,20},{5,21},{6,22},{7,23},{8,24},{9,... | collective-permute-start | bytes 3145736 | tf_op jit(solution)/shard_map/ppermute | solution.py:43
  14.0 73.7 %collective-permute-start.14 = (bf16[128,2048]{0,1:T(8,128)(2,1)S(1)}, bf16[128,2048]{0,1:T(8,128)(2,1)}, u32[]{:S(2)}, u32[]{:S(2)}) collective-permute-start(bf16[128,2048]{0,1:T(8,128)(2,1)S(1)} %copy.28), channel_id=1, source_target_pairs={{0,16},{1,17},{2,18},{3,19},{4,20},{5,21},{6,22},{7,23},{8,24},{9,... | collective-permute-start | bytes 1572872 | tf_op jit(solution)/shard_map/ppermute | solution.py:43
  16.7 30.5 %collective-permute-start.12 = (f32[4,4096]{1,0:T(4,128)S(1)}, f32[4,4096]{1,0:T(4,128)S(1)}, u32[]{:S(2)}, u32[]{:S(2)}) collective-permute-start(f32[4,4096]{1,0:T(4,128)S(1)} %add.204), channel_id=1, source_target_pairs={{0,8},{1,9},{2,10},{3,11},{4,12},{5,13},{6,14},{7,15},{8,0},{9,1},... | collective-permute-start | bytes 196616 | tf_op jit(solution)/shard_map/ppermute | solution.py:37
  19.2 65.1 %collective-permute-start = (bf16[48,4096]{1,0:T(8,128)(2,1)S(1)}, bf16[48,4096]{1,0:T(8,128)(2,1)S(1)}, u32[]{:S(2)}, u32[]{:S(2)}) collective-permute-start(bf16[48,4096]{1,0:T(8,128)(2,1)S(1)} %get-tuple-element.72), channel_id=1, source_target_pairs={{0,8},{1,9},{2,10},{3,11},{4,12},{5,13},{6,14},{7,15},{8,0},{9,1},... | collective-permute-start | bytes 1179656 | tf_op jit(solution)/shard_map/ppermute | solution.py:37
  47.2 34.8 %collective-permute-start.13 = (f32[4,4096]{1,0:T(4,128)S(1)}, f32[4,4096]{1,0:T(4,128)}, u32[]{:S(2)}, u32[]{:S(2)}) collective-permute-start(f32[4,4096]{1,0:T(4,128)S(1)} %add.205), channel_id=1, source_target_pairs={{0,16},{1,17},{2,18},{3,19},{4,20},{5,21},{6,22},{7,23},{8,24},{9,... | collective-permute-start | bytes 196616 | tf_op jit(solution)/shard_map/ppermute | solution.py:37
  85.4 70.6 %collective-permute-start.1 = (bf16[96,4096]{1,0:T(8,128)(2,1)}, bf16[96,4096]{1,0:T(8,128)(2,1)}, u32[]{:S(2)}, u32[]{:S(2)}) collective-permute-start(bf16[96,4096]{1,0:T(8,128)(2,1)} %pad_maximum_fusion.19), channel_id=1, source_target_pairs={{0,4},{1,5},{2,6},{3,7},{4,0},{5,1},{6,2},{7,3},{8,12},{9,13},{10,... | collective-permute-start | bytes 2359304 | tf_op jit(solution)/shard_map/ppermute | solution.py:37
  90.0 24.4 %collective-permute-start.15 = (bf16[48,2048]{0,1:T(8,128)(2,1)S(1)}, bf16[48,2048]{0,1:T(8,128)(2,1)}, u32[]{:S(2)}, u32[]{:S(2)}) collective-permute-start(bf16[48,2048]{0,1:T(8,128)(2,1)S(1)} %get-tuple-element.75), channel_id=1, source_target_pairs={{0,8},{1,9},{2,10},{3,11},{4,12},{5,13},{6,14},{7,15},{8,0},{9,1},... | collective-permute-start | bytes 589832 | tf_op jit(solution)/shard_map/ppermute | solution.py:37
  91.5 26.6 %collective-permute-start.18 = (bf16[48,2048]{0,1:T(8,128)(2,1)S(1)}, bf16[48,2048]{0,1:T(8,128)(2,1)}, u32[]{:S(2)}, u32[]{:S(2)}) collective-permute-start(bf16[48,2048]{0,1:T(8,128)(2,1)S(1)} %get-tuple-element.74), channel_id=1, source_target_pairs={{0,4},{1,5},{2,6},{3,7},{4,0},{5,1},{6,2},{7,3},{8,12},{9,13},{10,... | collective-permute-start | bytes 589832 | tf_op jit(solution)/shard_map/ppermute | solution.py:37
  95.9 13.2 %collective-permute-start.21 = (bf16[32,2048]{0,1:T(8,128)(2,1)}, bf16[32,2048]{0,1:T(8,128)(2,1)S(1)}, u32[]{:S(2)}, u32[]{:S(2)}) collective-permute-start(bf16[32,2048]{0,1:T(8,128)(2,1)} %slice.392), channel_id=1, source_target_pairs={{0,2},{1,3},{2,0},{3,1},{4,6},{5,7},{6,4},{7,5},{8,10},{9,11},{10,... | collective-permute-start | bytes 393224 | tf_op jit(solution)/shard_map/ppermute | solution.py:37
  112.0 14.1 %collective-permute-start.22 = (bf16[64,2048]{0,1:T(8,128)(2,1)}, bf16[64,2048]{0,1:T(8,128)(2,1)}, u32[]{:S(2)}, u32[]{:S(2)}) collective-permute-start(bf16[64,2048]{0,1:T(8,128)(2,1)} %pad_maximum_fusion.27), channel_id=1, source_target_pairs={{0,8},{1,9},{2,10},{3,11},{4,12},{5,13},{6,14},{7,15},{8,0},{9,1},... | collective-permute-start | bytes 786440 | tf_op jit(solution)/shard_map/ppermute | solution.py:37
  116.5 22.8 %collective-permute-start.16 = (bf16[96,2048]{0,1:T(8,128)(2,1)}, bf16[96,2048]{0,1:T(8,128)(2,1)}, u32[]{:S(2)}, u32[]{:S(2)}) collective-permute-start(bf16[96,2048]{0,1:T(8,128)(2,1)} %pad_maximum_fusion.25), channel_id=1, source_target_pairs={{0,4},{1,5},{2,6},{3,7},{4,0},{5,1},{6,2},{7,3},{8,12},{9,13},{10,... | collective-permute-start | bytes 1179656 | tf_op jit(solution)/shard_map/ppermute | solution.py:37
  120.2 25.8 %collective-permute-start.19 = (bf16[96,2048]{0,1:T(8,128)(2,1)}, bf16[96,2048]{0,1:T(8,128)(2,1)}, u32[]{:S(2)}, u32[]{:S(2)}) collective-permute-start(bf16[96,2048]{0,1:T(8,128)(2,1)} %pad_maximum_fusion.26), channel_id=1, source_target_pairs={{0,2},{1,3},{2,0},{3,1},{4,6},{5,7},{6,4},{7,5},{8,10},{9,11},{10,... | collective-permute-start | bytes 1179656 | tf_op jit(solution)/shard_map/ppermute | solution.py:37
  128.8 116.5 %collective-permute-start.23 = (bf16[128,2048]{0,1:T(8,128)(2,1)}, bf16[128,2048]{0,1:T(8,128)(2,1)}, u32[]{:S(2)}, u32[]{:S(2)}) collective-permute-start(bf16[128,2048]{0,1:T(8,128)(2,1)} %pad_maximum_fusion.28), channel_id=1, source_target_pairs={{0,4},{1,5},{2,6},{3,7},{4,0},{5,1},{6,2},{7,3},{8,12},{9,13},{10,... | collective-permute-start | bytes 1572872 | tf_op jit(solution)/shard_map/ppermute | solution.py:37
  138.0 22.7 %collective-permute-start.25 = (bf16[256,512]{1,0:T(8,128)(2,1)}, bf16[256,512]{1,0:T(8,128)(2,1)}, u32[]{:S(2)}, u32[]{:S(2)}) collective-permute-start(bf16[256,512]{1,0:T(8,128)(2,1)} %get-tuple-element.33), channel_id=1, source_target_pairs={{0,8},{1,9},{2,10},{3,11},{4,12},{5,13},{6,14},{7,15},{8,0},{9,1},... | collective-permute-start | bytes 786440 | tf_op jit(solution)/shard_map/ppermute | solution.py:37
  139.3 24.3 %collective-permute-start.26 = (bf16[256,512]{1,0:T(8,128)(2,1)}, bf16[256,512]{1,0:T(8,128)(2,1)}, u32[]{:S(2)}, u32[]{:S(2)}) collective-permute-start(bf16[256,512]{1,0:T(8,128)(2,1)} %get-tuple-element.32), channel_id=1, source_target_pairs={{0,4},{1,5},{2,6},{3,7},{4,0},{5,1},{6,2},{7,3},{8,12},{9,13},{10,... | collective-permute-start | bytes 786440 | tf_op jit(solution)/shard_map/ppermute | solution.py:37
  146.0 21.6 %collective-permute-start.27 = (bf16[256,512]{1,0:T(8,128)(2,1)}, bf16[256,512]{1,0:T(8,128)(2,1)S(1)}, u32[]{:S(2)}, u32[]{:S(2)}) collective-permute-start(bf16[256,512]{1,0:T(8,128)(2,1)} %get-tuple-element.31), channel_id=1, source_target_pairs={{0,12},{1,13},{2,14},{3,15},{4,8},{5,9},{6,10},{7,11},{8,4},{9,5},... | collective-permute-start | bytes 786440 | tf_op jit(solution)/shard_map/ppermute | solution.py:37
  156.0 18.8 %collective-permute-start.28 = (bf16[256,512]{1,0:T(8,128)(2,1)}, bf16[256,512]{1,0:T(8,128)(2,1)S(1)}, u32[]{:S(2)}, u32[]{:S(2)}) collective-permute-start(bf16[256,512]{1,0:T(8,128)(2,1)} %get-tuple-element.30), channel_id=1, source_target_pairs={{0,2},{1,3},{2,0},{3,1},{4,6},{5,7},{6,4},{7,5},{8,10},{9,11},{10,... | collective-permute-start | bytes 786440 | tf_op jit(solution)/shard_map/ppermute | solution.py:37
  160.6 14.8 %collective-permute-start.29 = (bf16[256,512]{1,0:T(8,128)(2,1)S(1)}, bf16[256,512]{1,0:T(8,128)(2,1)S(1)}, u32[]{:S(2)}, u32[]{:S(2)}) collective-permute-start(bf16[256,512]{1,0:T(8,128)(2,1)S(1)} %copy-done.39), channel_id=1, source_target_pairs={{0,10},{1,11},{2,8},{3,9},{4,14},{5,15},{6,12},{7,13},{8,2},{9,3},... | collective-permute-start | bytes 786440 | tf_op jit(solution)/shard_map/ppermute | solution.py:37
  163.6 18.7 %collective-permute-start.30 = (bf16[256,512]{1,0:T(8,128)(2,1)S(1)}, bf16[256,512]{1,0:T(8,128)(2,1)S(1)}, u32[]{:S(2)}, u32[]{:S(2)}) collective-permute-start(bf16[256,512]{1,0:T(8,128)(2,1)S(1)} %copy-done.38), channel_id=1, source_target_pairs={{0,6},{1,7},{2,4},{3,5},{4,2},{5,3},{6,0},{7,1},{8,14},{9,15},{10,... | collective-permute-start | bytes 786440 | tf_op jit(solution)/shard_map/ppermute | solution.py:37
  167.6 17.1 %collective-permute-start.31 = (bf16[256,512]{1,0:T(8,128)(2,1)S(1)}, bf16[256,512]{1,0:T(8,128)(2,1)S(1)}, u32[]{:S(2)}, u32[]{:S(2)}) collective-permute-start(bf16[256,512]{1,0:T(8,128)(2,1)S(1)} %copy-done.37), channel_id=1, source_target_pairs={{0,14},{1,15},{2,12},{3,13},{4,10},{5,11},{6,8},{7,9},{8,6},{9,7},... | collective-permute-start | bytes 786440 | tf_op jit(solution)/shard_map/ppermute | solution.py:37
  174.8 71.8 %collective-permute-start.17 = (bf16[192,2048]{1,0:T(8,128)(2,1)}, bf16[192,2048]{1,0:T(8,128)(2,1)}, u32[]{:S(2)}, u32[]{:S(2)}) collective-permute-start(bf16[192,2048]{1,0:T(8,128)(2,1)} %copy.13), channel_id=1, source_target_pairs={{0,2},{1,3},{2,0},{3,1},{4,6},{5,7},{6,4},{7,5},{8,10},{9,11},{10,... | collective-permute-start | bytes 2359304 | tf_op jit(solution)/shard_map/ppermute | solution.py:37
  175.4 121.5 %collective-permute-start.20 = (bf16[192,2048]{1,0:T(8,128)(2,1)}, bf16[192,2048]{1,0:T(8,128)(2,1)}, u32[]{:S(2)}, u32[]{:S(2)}) collective-permute-start(bf16[192,2048]{1,0:T(8,128)(2,1)} %copy.14), channel_id=1, source_target_pairs={{0,8},{1,9},{2,10},{3,11},{4,12},{5,13},{6,14},{7,15},{8,0},{9,1},... | collective-permute-start | bytes 2359304 | tf_op jit(solution)/shard_map/ppermute | solution.py:37
  182.3 47.7 %collective-permute-start.2 = (bf16[192,4096]{1,0:T(8,128)(2,1)S(1)}, bf16[192,4096]{1,0:T(8,128)(2,1)S(1)}, u32[]{:S(2)}, u32[]{:S(2)}) collective-permute-start(bf16[192,4096]{1,0:T(8,128)(2,1)S(1)} %pad_maximum_fusion.10), channel_id=1, source_target_pairs={{0,2},{1,3},{2,0},{3,1},{4,6},{5,7},{6,4},{7,5},{8,10},{9,11},{10,... | collective-permute-start | bytes 4718600 | tf_op jit(solution)/shard_map/ppermute | solution.py:37
  232.2 8.8 %collective-permute-start.3 = (bf16[48,4096]{1,0:T(8,128)(2,1)S(1)}, bf16[48,4096]{1,0:T(8,128)(2,1)S(1)}, u32[]{:S(2)}, u32[]{:S(2)}) collective-permute-start(bf16[48,4096]{1,0:T(8,128)(2,1)S(1)} %get-tuple-element.70), channel_id=1, source_target_pairs={{0,4},{1,5},{2,6},{3,7},{4,0},{5,1},{6,2},{7,3},{8,12},{9,13},{10,... | collective-permute-start | bytes 1179656 | tf_op jit(solution)/shard_map/ppermute | solution.py:37
  241.9 17.0 %collective-permute-start.4 = (bf16[96,4096]{1,0:T(8,128)(2,1)}, bf16[96,4096]{1,0:T(8,128)(2,1)}, u32[]{:S(2)}, u32[]{:S(2)}) collective-permute-start(bf16[96,4096]{1,0:T(8,128)(2,1)} %pad_maximum_fusion.20), channel_id=1, source_target_pairs={{0,2},{1,3},{2,0},{3,1},{4,6},{5,7},{6,4},{7,5},{8,10},{9,11},{10,... | collective-permute-start | bytes 2359304 | tf_op jit(solution)/shard_map/ppermute | solution.py:37
  260.2 32.7 %collective-permute-start.5 = (bf16[192,4096]{1,0:T(8,128)(2,1)S(1)}, bf16[192,4096]{1,0:T(8,128)(2,1)S(1)}, u32[]{:S(2)}, u32[]{:S(2)}) collective-permute-start(bf16[192,4096]{1,0:T(8,128)(2,1)S(1)} %pad_maximum_fusion.11), channel_id=1, source_target_pairs={{0,8},{1,9},{2,10},{3,11},{4,12},{5,13},{6,14},{7,15},{8,0},{9,1},... | collective-permute-start | bytes 4718600 | tf_op jit(solution)/shard_map/ppermute | solution.py:37
  301.4 9.2 %collective-permute-start.7 = (bf16[64,4096]{1,0:T(8,128)(2,1)S(1)}, bf16[64,4096]{1,0:T(8,128)(2,1)S(1)}, u32[]{:S(2)}, u32[]{:S(2)}) collective-permute-start(bf16[64,4096]{1,0:T(8,128)(2,1)S(1)} %pad_maximum_fusion.24), channel_id=1, source_target_pairs={{0,8},{1,9},{2,10},{3,11},{4,12},{5,13},{6,14},{7,15},{8,0},{9,1},... | collective-permute-start | bytes 1572872 | tf_op jit(solution)/shard_map/ppermute | solution.py:37
  310.7 18.8 %collective-permute-start.8 = (bf16[128,4096]{1,0:T(8,128)(2,1)S(1)}, bf16[128,4096]{1,0:T(8,128)(2,1)S(1)}, u32[]{:S(2)}, u32[]{:S(2)}) collective-permute-start(bf16[128,4096]{1,0:T(8,128)(2,1)S(1)} %pad_maximum_fusion.15), channel_id=1, source_target_pairs={{0,4},{1,5},{2,6},{3,7},{4,0},{5,1},{6,2},{7,3},{8,12},{9,13},{10,... | collective-permute-start | bytes 3145736 | tf_op jit(solution)/shard_map/ppermute | solution.py:37
  351.2 53.6 %collective-permute-start.38 = (bf16[256,4096]{1,0:T(8,128)(2,1)}, bf16[256,4096]{1,0:T(8,128)(2,1)}, u32[]{:S(2)}, u32[]{:S(2)}) collective-permute-start(bf16[256,4096]{1,0:T(8,128)(2,1)} %constant_dynamic-update-slice_fusion.24), channel_id=1, source_target_pairs={{0,1},{1,0},{2,3},{3,2},{4,5},{5,4},{6,7},{7,6},{8,9},{9,8},{10,11... | collective-permute-start | bytes 6291464 | tf_op jit(solution)/shard_map/ppermute | solution.py:37
  363.3 9.8 %collective-permute-start.45 = (bf16[320,512]{1,0:T(8,128)(2,1)S(1)}, bf16[320,512]{1,0:T(8,128)(2,1)S(1)}, u32[]{:S(2)}, u32[]{:S(2)}) collective-permute-start(bf16[320,512]{1,0:T(8,128)(2,1)S(1)} %slice.439), channel_id=1, source_target_pairs={{0,2},{1,3},{2,0},{3,1},{4,6},{5,7},{6,4},{7,5},{8,10},{9,11},{10,... | collective-permute-start | bytes 983048 | tf_op jit(solution)/shard_map/ppermute | solution.py:37
  366.2 10.2 %collective-permute-start.42 = (bf16[352,512]{1,0:T(8,128)(2,1)S(1)}, bf16[352,512]{1,0:T(8,128)(2,1)S(1)}, u32[]{:S(2)}, u32[]{:S(2)}) collective-permute-start(bf16[352,512]{1,0:T(8,128)(2,1)S(1)} %get-tuple-element.67), channel_id=1, source_target_pairs={{0,4},{1,5},{2,6},{3,7},{4,0},{5,1},{6,2},{7,3},{8,12},{9,13},{10,... | collective-permute-start | bytes 1081352 | tf_op jit(solution)/shard_map/ppermute | solution.py:37
  374.0 25.7 %collective-permute-start.46 = (bf16[320,1024]{1,0:T(8,128)(2,1)}, bf16[320,1024]{1,0:T(8,128)(2,1)}, u32[]{:S(2)}, u32[]{:S(2)}) collective-permute-start(bf16[320,1024]{1,0:T(8,128)(2,1)} %pad_maximum_fusion.23), channel_id=1, source_target_pairs={{0,8},{1,9},{2,10},{3,11},{4,12},{5,13},{6,14},{7,15},{8,0},{9,1},... | collective-permute-start | bytes 1966088 | tf_op jit(solution)/shard_map/ppermute | solution.py:37
  375.0 23.1 %collective-permute-start.39 = (bf16[352,512]{1,0:T(8,128)(2,1)S(1)}, bf16[352,512]{1,0:T(8,128)(2,1)}, u32[]{:S(2)}, u32[]{:S(2)}) collective-permute-start(bf16[352,512]{1,0:T(8,128)(2,1)S(1)} %get-tuple-element.66), channel_id=1, source_target_pairs={{0,8},{1,9},{2,10},{3,11},{4,12},{5,13},{6,14},{7,15},{8,0},{9,1},... | collective-permute-start | bytes 1081352 | tf_op jit(solution)/shard_map/ppermute | solution.py:37
  377.5 25.1 %collective-permute-start.43 = (bf16[352,1024]{1,0:T(8,128)(2,1)}, bf16[352,1024]{1,0:T(8,128)(2,1)}, u32[]{:S(2)}, u32[]{:S(2)}) collective-permute-start(bf16[352,1024]{1,0:T(8,128)(2,1)} %pad_maximum_fusion.22), channel_id=1, source_target_pairs={{0,2},{1,3},{2,0},{3,1},{4,6},{5,7},{6,4},{7,5},{8,10},{9,11},{10,... | collective-permute-start | bytes 2162696 | tf_op jit(solution)/shard_map/ppermute | solution.py:37
  382.3 82.0 %collective-permute-start.48 = (bf16[256,1024]{0,1:T(8,128)(2,1)S(1)}, bf16[256,1024]{0,1:T(8,128)(2,1)S(1)}, u32[]{:S(2)}, u32[]{:S(2)}) collective-permute-start(bf16[256,1024]{0,1:T(8,128)(2,1)S(1)} %get-tuple-element.63), channel_id=1, source_target_pairs={{0,1},{1,0},{2,3},{3,2},{4,5},{5,4},{6,7},{7,6},{8,9},{9,8},{10,11... | collective-permute-start | bytes 1572872 | tf_op jit(solution)/shard_map/ppermute | solution.py:37
  399.1 19.1 %collective-permute-start.40 = (bf16[352,1024]{1,0:T(8,128)(2,1)S(1)}, bf16[352,1024]{1,0:T(8,128)(2,1)S(1)}, u32[]{:S(2)}, u32[]{:S(2)}) collective-permute-start(bf16[352,1024]{1,0:T(8,128)(2,1)S(1)} %pad_maximum_fusion.21), channel_id=1, source_target_pairs={{0,4},{1,5},{2,6},{3,7},{4,0},{5,1},{6,2},{7,3},{8,12},{9,13},{10,... | collective-permute-start | bytes 2162696 | tf_op jit(solution)/shard_map/ppermute | solution.py:37
  401.0 42.7 %collective-permute-start.47 = (bf16[320,2048]{1,0:T(8,128)(2,1)S(1)}, bf16[320,2048]{1,0:T(8,128)(2,1)S(1)}, u32[]{:S(2)}, u32[]{:S(2)}) collective-permute-start(bf16[320,2048]{1,0:T(8,128)(2,1)S(1)} %pad_maximum_fusion.14), channel_id=1, source_target_pairs={{0,4},{1,5},{2,6},{3,7},{4,0},{5,1},{6,2},{7,3},{8,12},{9,13},{10,... | collective-permute-start | bytes 3932168 | tf_op jit(solution)/shard_map/ppermute | solution.py:37
  403.8 53.9 %collective-permute-start.44 = (bf16[352,2048]{1,0:T(8,128)(2,1)S(1)}, bf16[352,2048]{1,0:T(8,128)(2,1)S(1)}, u32[]{:S(2)}, u32[]{:S(2)}) collective-permute-start(bf16[352,2048]{1,0:T(8,128)(2,1)S(1)} %pad_maximum_fusion.13), channel_id=1, source_target_pairs={{0,8},{1,9},{2,10},{3,11},{4,12},{5,13},{6,14},{7,15},{8,0},{9,1},... | collective-permute-start | bytes 4325384 | tf_op jit(solution)/shard_map/ppermute | solution.py:37
  408.0 62.2 %collective-permute-start.54 = (bf16[1024,512]{1,0:T(8,128)(2,1)}, bf16[1024,512]{1,0:T(8,128)(2,1)}, u32[]{:S(2)}, u32[]{:S(2)}) collective-permute-start(bf16[1024,512]{1,0:T(8,128)(2,1)} %get-tuple-element.12), channel_id=1, source_target_pairs={{0,16},{1,17},{2,18},{3,19},{4,20},{5,21},{6,22},{7,23},{8,24},{9,... | collective-permute-start | bytes 3145736 | tf_op jit(solution)/shard_map/ppermute | solution.py:43
  419.4 41.6 %collective-permute-start.41 = (bf16[352,2048]{1,0:T(8,128)(2,1)S(1)}, bf16[352,2048]{1,0:T(8,128)(2,1)S(1)}, u32[]{:S(2)}, u32[]{:S(2)}) collective-permute-start(bf16[352,2048]{1,0:T(8,128)(2,1)S(1)} %pad_maximum_fusion.12), channel_id=1, source_target_pairs={{0,2},{1,3},{2,0},{3,1},{4,6},{5,7},{6,4},{7,5},{8,10},{9,11},{10,... | collective-permute-start | bytes 4325384 | tf_op jit(solution)/shard_map/ppermute | solution.py:37
  471.6 31.5 %collective-permute-start.55 = (bf16[2,1024,512]{2,1,0:T(8,128)(2,1)S(1)}, bf16[2,1024,512]{2,1,0:T(8,128)(2,1)}, u32[]{:S(2)}, u32[]{:S(2)}) collective-permute-start(bf16[2,1024,512]{2,1,0:T(8,128)(2,1)S(1)} %bitcast_dynamic-update-slice_fusion), channel_id=1, source_target_pairs={{0,1},{1,0},{2,3},{3,2},{4,5},{5,4},{6,7},{7,6},{8,9},{9,8},{10,11... | collective-permute-start | bytes 6291464 | tf_op jit(solution)/shard_map/ppermute | solution.py:37
  480.4 22.4 %collective-permute-start.52 = (bf16[256,1024]{0,1:T(8,128)(2,1)}, bf16[256,1024]{0,1:T(8,128)(2,1)S(1)}, u32[]{:S(2)}, u32[]{:S(2)}) collective-permute-start(bf16[256,1024]{0,1:T(8,128)(2,1)} %get-tuple-element.61), channel_id=1, source_target_pairs={{0,1},{1,0},{2,3},{3,2},{4,5},{5,4},{6,7},{7,6},{8,9},{9,8},{10,11... | collective-permute-start | bytes 1572872 | tf_op jit(solution)/shard_map/ppermute | solution.py:37
  515.1 45.8 %collective-permute-start.53 = (bf16[128,2048]{0,1:T(8,128)(2,1)}, bf16[128,2048]{0,1:T(8,128)(2,1)S(1)}, u32[]{:S(2)}, u32[]{:S(2)}) collective-permute-start(bf16[128,2048]{0,1:T(8,128)(2,1)} %get-tuple-element.58), channel_id=1, source_target_pairs={{0,16},{1,17},{2,18},{3,19},{4,20},{5,21},{6,22},{7,23},{8,24},{9,... | collective-permute-start | bytes 1572872 | tf_op jit(solution)/shard_map/ppermute | solution.py:43
  517.5 24.5 %collective-permute-start.57 = (f32[2,512]{1,0:T(2,128)S(1)}, f32[2,512]{1,0:T(2,128)S(1)}, u32[]{:S(2)}, u32[]{:S(2)}) collective-permute-start(f32[2,512]{1,0:T(2,128)S(1)} %fusion.72), channel_id=1, source_target_pairs={{0,16},{1,17},{2,18},{3,19},{4,20},{5,21},{6,22},{7,23},{8,24},{9,... | collective-permute-start | bytes 12296 | tf_op jit(solution)/shard_map/ppermute | solution.py:37
  544.4 8.1 %collective-permute-start.59 = (bf16[128,512]{1,0:T(8,128)(2,1)S(1)}, bf16[128,512]{1,0:T(8,128)(2,1)S(1)}, u32[]{:S(2)}, u32[]{:S(2)}) collective-permute-start(bf16[128,512]{1,0:T(8,128)(2,1)S(1)} %pad_maximum_fusion.30), channel_id=1, source_target_pairs={{0,4},{1,5},{2,6},{3,7},{4,0},{5,1},{6,2},{7,3},{8,12},{9,13},{10,... | collective-permute-start | bytes 393224 | tf_op jit(solution)/shard_map/ppermute | solution.py:37
  546.4 8.4 %collective-permute-start.61 = (bf16[128,512]{1,0:T(8,128)(2,1)S(1)}, bf16[128,512]{1,0:T(8,128)(2,1)S(1)}, u32[]{:S(2)}, u32[]{:S(2)}) collective-permute-start(bf16[128,512]{1,0:T(8,128)(2,1)S(1)} %pad_maximum_fusion.32), channel_id=1, source_target_pairs={{0,8},{1,9},{2,10},{3,11},{4,12},{5,13},{6,14},{7,15},{8,0},{9,1},... | collective-permute-start | bytes 393224 | tf_op jit(solution)/shard_map/ppermute | solution.py:37
  548.3 8.5 %collective-permute-start.62 = (bf16[128,512]{1,0:T(8,128)(2,1)S(1)}, bf16[128,512]{1,0:T(8,128)(2,1)S(1)}, u32[]{:S(2)}, u32[]{:S(2)}) collective-permute-start(bf16[128,512]{1,0:T(8,128)(2,1)S(1)} %pad_maximum_fusion.33), channel_id=1, source_target_pairs={{0,10},{1,11},{2,8},{3,9},{4,14},{5,15},{6,12},{7,13},{8,2},{9,3},... | collective-permute-start | bytes 393224 | tf_op jit(solution)/shard_map/ppermute | solution.py:37
  552.5 8.3 %collective-permute-start.64 = (bf16[128,512]{1,0:T(8,128)(2,1)S(1)}, bf16[128,512]{1,0:T(8,128)(2,1)S(1)}, u32[]{:S(2)}, u32[]{:S(2)}) collective-permute-start(bf16[128,512]{1,0:T(8,128)(2,1)S(1)} %pad_maximum_fusion.35), channel_id=1, source_target_pairs={{0,14},{1,15},{2,12},{3,13},{4,10},{5,11},{6,8},{7,9},{8,6},{9,7},... | collective-permute-start | bytes 393224 | tf_op jit(solution)/shard_map/ppermute | solution.py:37
  (70 other events, 652.2 us)

commit v2 on v1

v2 whole, which is shorter than its diff:
```python
import jax
import jax.numpy as jnp
from jax import lax
from jax.experimental import pallas as pl
from jax.experimental.pallas import tpu as pltpu
from jax.sharding import PartitionSpec as P

lam = 0.0051
eps = 1e-05

cube = 8
orders = ((4, 2, 1), (2, 1, 4), (1, 4, 2))
together = lax.optimization_barrier


def places(order):
    return [
        sum(bit for step, bit in enumerate(order) if place >> step & 1) for place in range(cube)
    ]


def stack_kernel(mean_ref, inv_ref, *refs):
    pieces, (raw_ref, norm_ref) = refs[:cube], refs[cube:]
    rows = pieces[0].shape[0]
    for r, piece in enumerate(pieces):
        raw = piece[...]
        raw_ref[0, r * rows : (r + 1) * rows, :] = raw
        norm_ref[0, r * rows : (r + 1) * rows, :] = (
            (raw.astype(jnp.float32) - mean_ref[...]) * inv_ref[...]
        ).astype(jnp.bfloat16)


def stack_blocks(pieces, rows, mean, inv):
    size, n = pieces[0].shape
    groups = size // rows
    out = jax.ShapeDtypeStruct((groups, cube * rows, n), jnp.bfloat16)
    whole = pl.BlockSpec((1, cube * rows, n), lambda g: (g, 0, 0))
    return pl.pallas_call(
        stack_kernel,
        grid=(groups,),
        out_shape=(out, out),
        in_specs=[pl.BlockSpec((1, n), lambda g: (0, 0))] * 2
        + [pl.BlockSpec((rows, n), lambda g: (g, 0))] * cube,
        out_specs=(whole, whole),
        compiler_params=pltpu.CompilerParams(vmem_limit_bytes=32 << 20),
    )(mean, inv, *pieces)


def place_kernel(k_ref, *refs):
    pieces, out_ref = refs[:cube], refs[cube]
    n = pieces[0].shape[1]
    for r, piece in enumerate(pieces):
        start = pl.multiple_of((k_ref[0] ^ r) * n, n)
        out_ref[:, pl.ds(start, n)] = piece[...]


def place_blocks(pieces, k):
    rows, n = pieces[0].shape
    vmem = pl.BlockSpec(memory_space=pltpu.VMEM)
    return pl.pallas_call(
        place_kernel,
        out_shape=jax.ShapeDtypeStruct((rows, cube * n), jnp.bfloat16),
        in_specs=[pl.BlockSpec(memory_space=pltpu.SMEM)] + [vmem] * cube,
        out_specs=vmem,
        compiler_params=pltpu.CompilerParams(vmem_limit_bytes=32 << 20),
    )(k.reshape(1), *pieces)


def shards(view_a, view_b):
    f32, bf16 = jnp.float32, jnp.bfloat16
    rows, width = view_a.shape
    devices = lax.axis_size("dp")
    count = rows * devices
    cubes = devices // (2 * cube)
    index = lax.axis_index("dp")
    c, k, h = index % 2, index // 2 % cube, index // (2 * cube)
    wide, half, narrow = width // cubes, width // cubes // 2, width // cube

    def swap(x, mask):
        return lax.ppermute(x, "dp", [(i, i ^ mask) for i in range(devices)])

    def swap_k(x, bit):
        return swap(x, 2 * bit)

    def turn(x, step):
        return lax.ppermute(
            x, "dp", [(i, (i + 2 * cube * step) % devices) for i in range(devices)]
        )

    def turns(x):
        return [turn(x, s) for s in range(1, cubes)]

    def columns(x, start, size):
        return lax.dynamic_slice_in_dim(x, start, size, axis=1)

    def pair(mine, other, axis):
        return jnp.where(
            c == 0,
            jnp.concatenate([mine, other], axis),
            jnp.concatenate([other, mine], axis),
        )

    def flat(x, mean, inv):
        return (x.astype(f32) - mean) * inv

    def norm(x, mean, inv):
        return flat(x, mean, inv).astype(bf16)

    def h_masks():
        return [2 * cube << bit for bit in range(cubes.bit_length() - 1)]

    far_raw = [turn(columns(view_a, (h + s) % cubes * wide, wide), s) for s in range(1, cubes)]

    full_a, full_b = view_a.astype(f32), view_b.astype(f32)
    sums = jnp.stack(
        [
            jnp.sum(full_a, axis=0),
            jnp.sum(full_a * full_a, axis=0),
            jnp.sum(full_b, axis=0),
            jnp.sum(full_b * full_b, axis=0),
        ]
    )
    for mask in (1, 2, 4):
        sums = sums + swap(sums, mask)
    sums, own_b = together((sums, view_b))
    own_eighths = [columns(own_b, (k ^ r) * narrow, narrow) for r in range(cube)]
    own_b = [own_eighths[0]] + [swap_k(own_eighths[r], r) for r in range(1, cube)]
    for mask in h_masks() + [8]:
        sums = sums + swap(sums, mask)
    means = sums / count
    mean_a, mean_b = means[0:1], means[2:3]
    inv_a = 1.0 / jnp.sqrt(means[1:2] - mean_a * mean_a + eps)
    inv_b = 1.0 / jnp.sqrt(means[3:4] - mean_b * mean_b + eps)
    mean_aw, inv_aw = columns(mean_a, h * wide, wide), columns(inv_a, h * wide, wide)
    mean_bn, inv_bn = columns(mean_b, k * narrow, narrow), columns(inv_b, k * narrow, narrow)

    near_raw = columns(view_a, h * wide, wide)
    norm_a = norm(view_a, mean_a, inv_a)
    near = columns(norm_a, h * wide, wide)
    rest = jnp.concatenate(
        [columns(norm_a, (h + s) % cubes * wide, wide) for s in range(1, cubes)], 1
    )
    far = jnp.concatenate([norm(x, mean_aw, inv_aw) for x in far_raw], 1)
    moving = [x.reshape(1, 1, 1, *x.shape) for x in (far, near, rest)]
    (moving, raw_b) = together((moving, view_b))
    others_b = turns(raw_b)
    far_eighths = None
    for step in range(3):
        if step == 2:
            others_b, moving = together((others_b, moving))
            pair_b = jnp.concatenate([view_b] + others_b, 0)
            outer = pair_b[rows:]
            far_eighths = [columns(outer, (k ^ r) * narrow, narrow) for r in range(cube)]
            far_b = [far_eighths[0]] + [swap_k(far_eighths[r], r) for r in range(1, cube)]
        arrived = [swap_k(x, order[step]) for x, order in zip(moving, orders)]
        moving, arrived = together((moving, arrived))
        moving = [
            jnp.concatenate([x, y], (4, 2, 1).index(order[step]))
            for x, y, order in zip(moving, arrived, orders)
        ]
    far, near, rest = [x.reshape(cube * rows, -1) for x in moving]

    near_b, right = stack_blocks(own_b, rows, mean_bn, inv_bn)
    _, rights = stack_blocks(far_b, rows, mean_bn, inv_bn)
    near_b = near_b[0]
    partial = 0.0
    for s in range(cubes):
        partial = partial + lax.dot_general(
            near if s == 0 else far[:, (s - 1) * wide : s * wide],
            right[0] if s == 0 else rights[s - 1],
            (((0,), (0,)), ((), ())),
            preferred_element_type=f32,
        )
    corr = (
        lax.dynamic_slice_in_dim(partial, c * half, half, 0)
        + swap(lax.dynamic_slice_in_dim(partial, (1 - c) * half, half, 0), 1)
    ) / count
    first_i, first_j = h * wide + c * half, k * narrow
    diag = (
        lax.broadcasted_iota(jnp.int32, (half, narrow), 0) + first_i
        == lax.broadcasted_iota(jnp.int32, (half, narrow), 1) + first_j
    )
    loss = jnp.sum(jnp.where(diag, (1.0 - corr) ** 2, lam * corr * corr))
    gcorr = jnp.where(diag, 2.0 * (corr - 1.0), 2.0 * lam * corr).astype(bf16)
    loss = jnp.full((1, narrow), loss, f32)

    all_b = jnp.concatenate([pair_b, swap(pair_b, 1)], 0)
    pair_a = jnp.concatenate([near_raw] + far_raw, 0)
    all_a = jnp.concatenate(
        [columns(pair_a, c * half, half), swap(columns(pair_a, (1 - c) * half, half), 1)], 0
    )
    norm_b = norm(all_b, mean_b, inv_b)
    arranged = [
        jnp.concatenate([columns(norm_b, (k ^ r) * narrow, narrow) for r in places(order)], 1)
        for order in orders
    ]

    part = -(-half // 48) * 16
    moving = [gcorr[:part], gcorr[part : 2 * part], gcorr[2 * part :]]
    moving, outgoing = together((moving, gcorr))
    turned = [outgoing] + turns(outgoing)
    out_b = None
    for step in range(3):
        if step == 2:
            turned, moving = together((turned, moving))
            across = jnp.zeros((cubes, half, narrow), bf16)
            for s, block in enumerate(turned):
                across = lax.dynamic_update_slice_in_dim(across, block[None], (h - s) % cubes, 0)
            rows_g = pair(across, swap(across, 1), 1).reshape(cubes, wide, narrow)

            def rows_of(s):
                return lax.dynamic_index_in_dim(rows_g, (h + s) % cubes, 0, keepdims=False)

            grad_nb = jnp.dot(near, rows_of(0), preferred_element_type=f32)
            for s in range(1, cubes):
                grad_nb = grad_nb + jnp.dot(
                    rest[:, (s - 1) * wide : s * wide], rows_of(s), preferred_element_type=f32
                )
            flat_b = flat(near_b, mean_bn, inv_bn)
            stats_b = jnp.concatenate(
                [
                    jnp.sum(grad_nb, axis=0, keepdims=True),
                    jnp.sum(grad_nb * flat_b, axis=0, keepdims=True),
                    loss,
                ]
            )
            for mask in [1] + h_masks():
                stats_b = stats_b + swap(stats_b, mask)
            first, second = stats_b[0:1] / count, stats_b[1:2] / count
            out_b = (inv_bn * (grad_nb - first - flat_b * second)).astype(bf16)
        bit = orders[0][step]
        arrived = [swap_k(x, order[step]) for x, order in zip(moving, orders)]
        if step < 2:
            loss = loss + swap_k(loss, bit)
            moving, arrived, loss = together((moving, arrived, loss))
            moving = [jnp.concatenate([x, y], 1) for x, y in zip(moving, arrived)]
            if step == 1:
                loss = loss + swap_k(loss, orders[0][2])
    moving, arrived, out_b = together((moving, arrived, out_b))
    pieces_b = [out_b[r * rows : (r + 1) * rows] for r in range(cube)]
    pieces_b = [pieces_b[0]] + [swap_k(pieces_b[r], r) for r in range(1, cube)]

    cross = jnp.concatenate(
        [
            sum(
                lax.dot_general(
                    b[:, n * width // 2 : (n + 1) * width // 2],
                    piece,
                    (((1,), (1,)), ((), ())),
                    preferred_element_type=f32,
                )
                for n, piece in enumerate((x, y))
            )
            for b, x, y in zip(arranged, moving, arrived)
        ],
        1,
    )
    mean_ah, inv_ah = columns(mean_a, first_i, half), columns(inv_a, first_i, half)
    flat_a = flat(all_a, mean_ah, inv_ah)
    stats_a = jnp.stack([jnp.sum(cross, axis=0), jnp.sum(cross * flat_a, axis=0)])
    for bit in (1, 2, 4):
        stats_a = stats_a + swap_k(stats_a, bit)
    stats_a = stats_a / count
    out_a = (inv_ah * (cross - stats_a[0:1] - flat_a * stats_a[1:2])).astype(bf16)

    grad_b = place_blocks(pieces_b, k)
    mine = cubes * rows
    both = pair(out_a[:mine], swap(out_a[mine:], 1), 1)
    grad_a = jnp.zeros((rows, width), bf16)
    for s in range(cubes):
        block = both[s * rows : (s + 1) * rows]
        block = turn(block, -s) if s else block
        grad_a = lax.dynamic_update_slice_in_dim(grad_a, block, (h + s) % cubes * wide, 1)
    return (stats_b[2, 0], grad_a, grad_b)


def solution(mesh):
    return jax.shard_map(
        shards,
        mesh=mesh,
        in_specs=(P("dp", None), P("dp", None)),
        out_specs=(P(), P("dp", None), P("dp", None)),
        check_vma=False,
    )
```

time: 572 us -> 404 us (0.71); the launches traced: 563 us -> 403 us
  local copies, waits for them, and re-layouts: 117 us -> 25.1 us
  waiting for transfers between devices: 278 us -> 230 us
  other arithmetic: 64.1 us -> 44 us
    ppermute x61 -> x57, waiting for transfers between devices: 278 us -> 201 us  [swap(): return lax.ppermute(x, 'dp', [(i, i ^ mask) for i in range(devices)])]
    unnamed x175 -> x52, local copies, waits for them, and re-layouts: 71.4 us -> 7.47 us
    ppermute x4, waiting for transfers between devices: 0.01 us -> 29.1 us  [turn(): lax.ppermute(x, 'dp', [(i, (i + 2 * cube * step) % devices) for i in rang...]
    convert_element_type x3 -> x2, other arithmetic: 15.6 us -> 1.4 us  [norm(): return flat(x, mean, inv).astype(bf16)]
    ppermute x7 -> x0, local copies, waits for them, and re-layouts: 12.1 us -> none  [swap(): return lax.ppermute(x, 'dp', [(i, i ^ mask) for i in range(devices)])]
    slice x14 -> x4, local copies, waits for them, and re-layouts: 12.2 us -> 0.65 us  [the longest x1 0.51 us: shards(): return (stats_b[2, 0], grad_a, grad_b)]
    ppermute x61 -> x57, starting transfers between devices: 68.5 us -> 73.8 us  [swap(): return lax.ppermute(x, 'dp', [(i, i ^ mask) for i in range(devices)])]
    concatenate x26 -> x12, other arithmetic: 27.6 us -> 23.5 us  [the longest x6 14.8 us: shards(): jnp.concatenate([x, y], (4, 2, 1).index(order[step]))]
  transfers between devices with their start and end apart: 65 -> 61, of which waited for: 34 -> 42; matrix products, arithmetic and copies ran while one was open for 29% -> 11% of each run, Pallas kernels for 0% -> 1%
where the time goes in v2:
time: 404 us; the launch traced here: 403 us
  waiting for transfers between devices  230 us (57%)
  starting transfers between devices  81 us (20%)
  other arithmetic  44 us (11%)
  local copies, waits for them, and re-layouts  25.1 us (6%)
  matrix products  19.4 us (5%)
    ppermute x57, waiting for transfers between devices, swap(): return lax.ppermute(x, 'dp', [(i, i ^ mask) for i in range(devices)])  201 us
    ppermute x57, starting transfers between devices, swap(): return lax.ppermute(x, 'dp', [(i, i ^ mask) for i in range(devices)])  73.8 us
    ppermute x4, waiting for transfers between devices, turn(): lax.ppermute(x, 'dp', [(i, (i + 2 * cube * step) % devices) for i in rang...  29.1 us
    concatenate x6, other arithmetic, shards(): jnp.concatenate([x, y], (4, 2, 1).index(order[step]))  14.8 us
  transfers between devices with their start and end apart: 61, of which 42 were waited for; matrix products, arithmetic and copies ran while one was open for 11% of the time, Pallas kernels for 1%

profile of v2, /device:TPU:0, one launch (start us, length us, event | category | flops | bytes accessed | tf_op | source)
XLA Modules:
  0.0 403.3 jit_solution(11683069459473975588)
XLA Ops:
  5.4 2.9 collective-permute-start.2
  8.3 2.4 collective-permute-done.2
  12.8 2.4 collective-permute-done.3
  15.2 3.0 collective-permute-start.4
  18.2 2.4 collective-permute-done.4
  23.6 3.4 collective-permute-start
  28.3 18.1 %collective-permute-done = bf16[128,2048]{0,1:T(8,128)(2,1)S(1)} collective-permute-done((bf16[128,2048]{0,1:T(8,128)(2,1)S(1)}, bf16[128,2048]{0,1:T(8,128)(2,1)S(1)}, u32[]{:S(2)}, u32[]{:S(2)}) %collective-permute-start) | collective-permute-done | bytes 524320 | tf_op jit(solution)/shard_map/ppermute | solution.py:86
  50.1 10.1 %collective-permute-done.7 = bf16[1,1,1,128,2048]{3,4,2,1,0:T(8,128)(2,1)S(1)} collective-permute-done((bf16[1,1,1,128,2048]{3,4,2,1,0:T(8,128)(2,1)S(1)}, bf16[1,1,1,128,2048]{3,4,2,1,0:T(8,128)(2,1)S(1)}, u32[]{:S(2)}, u32[]{:S(2)}) %collective-permute-start.7) | collective-permute-done | bytes 524320 | tf_op jit(solution)/shard_map/ppermute | solution.py:80
  66.1 18.9 %collective-permute-done.10 = bf16[2,1,1,128,2048]{3,4,2,1,0:T(8,128)(2,1)S(1)} collective-permute-done((bf16[2,1,1,128,2048]{3,4,2,1,0:T(8,128)(2,1)S(1)}, bf16[2,1,1,128,2048]{3,4,2,1,0:T(8,128)(2,1)S(1)}, u32[]{:S(2)}, u32[]{:S(2)}) %collective-permute-start.10) | collective-permute-done | bytes 1048608 | tf_op jit(solution)/shard_map/ppermute | solution.py:80
  85.3 21.6 %collective-permute-done.12 = bf16[1,1,2,128,2048]{4,3,2,1,0:T(8,128)(2,1)S(1)} collective-permute-done((bf16[1,1,2,128,2048]{4,3,2,1,0:T(8,128)(2,1)S(1)}, bf16[1,1,2,128,2048]{4,3,2,1,0:T(8,128)(2,1)S(1)}, u32[]{:S(2)}, u32[]{:S(2)}) %collective-permute-start.12) | collective-permute-done | bytes 1048608 | tf_op jit(solution)/shard_map/ppermute | solution.py:80
  115.7 44.3 %collective-permute-done.16.refs_1_ = bf16[128,512]{1,0:T(8,128)(2,1)S(1)} collective-permute-done((bf16[128,512]{1,0:T(8,128)(2,1)S(1)}, bf16[128,512]{1,0:T(8,128)(2,1)S(1)}, u32[]{:S(2)}, u32[]{:S(2)}) %collective-permute-start.16) | collective-permute-done | bytes 131104 | tf_op jit(solution)/shard_map/ppermute | solution.py:80
  163.3 2.5 collective-permute-done.18.refs_3_
  167.9 2.3 collective-permute-start.21
  172.2 2.2 collective-permute-start.22
  176.7 2.3 collective-permute-done.22.refs_7_
  179.1 2.7 collective-permute-start.24
  185.1 3.1 collective-permute-done.25.refs_3_
  189.7 2.4 collective-permute-start.28
  194.1 2.2 collective-permute-start.29
  197.2 3.6 collective-permute-done.29.refs_7_
  202.9 4.6 %pad_maximum_fusion.1 = bf16[2,2,2,128,2048]{3,4,2,1,0:T(8,128)(2,1)} fusion(bf16[2,2,1,128,2048]{3,4,2,1,0:T(8,128)(2,1)} %collective-permute-done.13, bf16[2,2,1,128,2048]{3,4,2,1,0:T(8,128)(2,1)} %pad_maximum_fusion.12), kind=kLoop, calls=%fused_computation.2 | loop fusion | flops 2097152 | bytes 8388608 | tf_op jit(solution)/shard_map/concatenate | solution.py:158
  207.5 6.4 %copy.10 = bf16[2,2,2,128,2048]{4,3,2,1,0:T(8,128)(2,1)} copy(bf16[2,2,2,128,2048]{3,4,2,1,0:T(8,128)(2,1)} %pad_maximum_fusion.1) | data formatting | bytes 8388608 | tf_op jit(solution)/shard_map/concatenate | solution.py:158
  213.9 4.6 %fusion.71 = f32[2048,512]{1,0:T(8,128)S(1)} fusion(bf16[1024,2048]{1,0:T(8,128)(2,1)} %bitcast.74, bf16[1,1024,512]{2,1,0:T(8,128)(2,1)S(1)} %copy-done.3), kind=kOutput, calls=%fused_computation.101 | convolution fusion | flops 2147483648 | bytes 9437184 | tf_op jit(solution)/shard_map/dot_general | solution.py:168
  218.5 2.7 pad_maximum_fusion
  221.3 2.6 convolution_add_fusion
  225.9 4.3 %collective-permute-done.30 = f32[1024,512]{1,0:T(8,128)} collective-permute-done((f32[1024,512]{1,0:T(8,128)S(1)}, f32[1024,512]{1,0:T(8,128)}, u32[]{:S(2)}, u32[]{:S(2)}) %collective-permute-start.30) | collective-permute-done | bytes 2097184 | tf_op jit(solution)/shard_map/ppermute | solution.py:80
  230.2 4.1 %fusion.2 = (f32[]{:T(128)}, bf16[1024,512]{1,0:T(8,128)(2,1)S(1)}) fusion(s32[512]{0:T(512)S(1)} %iota_add_fusion.1, s32[1024]{0:T(1024)S(1)} %iota_add_fusion, f32[1024,512]{1,0:T(8,128)} %collective-permute-done.30, f32[2048,512]{1,0:T(8,128)} %copy-done.11, s32[]{:T(128)S(6)} %select_n.174), kind=kLoop, calls=%fused_computation.21 | loop fusion | flops 7340031 | bytes 5249032 | tf_op jit(solution)/shard_map/reduce_sum | solution.py:183
  234.4 2.2 collective-permute-start.32
  240.4 4.9 %collective-permute-done.35 = f32[1,512]{1,0:T(1,128)S(1)} collective-permute-done((f32[1,512]{1,0:T(1,128)S(1)}, f32[1,512]{1,0:T(1,128)S(1)}, u32[]{:S(2)}, u32[]{:S(2)}) %collective-permute-start.35) | collective-permute-done | bytes 2080 | tf_op jit(solution)/shard_map/ppermute | solution.py:80
  255.8 9.0 %collective-permute-done.39 = f32[1,512]{1,0:T(1,128)} collective-permute-done((f32[1,512]{1,0:T(1,128)S(1)}, f32[1,512]{1,0:T(1,128)}, u32[]{:S(2)}, u32[]{:S(2)}) %collective-permute-start.39) | collective-permute-done | bytes 2080 | tf_op jit(solution)/shard_map/ppermute | solution.py:80
  265.5 15.3 %collective-permute-done.38 = bf16[320,1024]{1,0:T(8,128)(2,1)} collective-permute-done((bf16[320,1024]{1,0:T(8,128)(2,1)}, bf16[320,1024]{1,0:T(8,128)(2,1)}, u32[]{:S(2)}, u32[]{:S(2)}) %collective-permute-start.38) | collective-permute-done | bytes 655392 | tf_op jit(solution)/shard_map/ppermute | solution.py:80
  280.9 2.5 pad_maximum_fusion.19
  283.4 2.3 pad_maximum_fusion.17
  285.7 2.4 pad_maximum_fusion.18
  288.1 11.0 %collective-permute-done.31 = bf16[1024,512]{1,0:T(8,128)(2,1)} collective-permute-done((bf16[1024,512]{1,0:T(8,128)(2,1)S(1)}, bf16[1024,512]{1,0:T(8,128)(2,1)}, u32[]{:S(2)}, u32[]{:S(2)}) %collective-permute-start.31) | collective-permute-done | bytes 1048608 | tf_op jit(solution)/shard_map/ppermute | solution.py:86
  301.7 2.4 bitcast_dynamic-update-slice_fusion
  309.8 3.0 pad_maximum_fusion.2
  315.3 5.1 %maximum_select_fusion = bf16[2,2048,512]{2,1,0:T(8,128)(2,1)S(1)} fusion(bf16[2,1024,512]{2,1,0:T(8,128)(2,1)} %collective-permute-done.40, bf16[2,1024,512]{2,1,0:T(8,128)(2,1)} %bitcast_dynamic-update-slice_fusion, pred[]{:T(512)S(6)} %eq.18), kind=kLoop, calls=%fused_computation.3 | loop fusion | flops 18874368 | bytes 8388609 | tf_op jit(solution)/shard_map/jit(_where)/select_n | solution.py:97
  320.4 2.3 fusion.52
  322.7 2.6 fusion.93
  326.6 3.2 collective-permute-start.43
  330.3 14.8 %collective-permute-done.43 = f32[3,512]{1,0:T(4,128)S(1)} collective-permute-done((f32[3,512]{1,0:T(4,128)S(1)}, f32[3,512]{1,0:T(4,128)S(1)}, u32[]{:S(2)}, u32[]{:S(2)}) %collective-permute-start.43) | collective-permute-done | bytes 6176 | tf_op jit(solution)/shard_map/ppermute | solution.py:80
  357.4 2.7 collective-permute-done.49
  361.5 2.4 collective-permute-done.50
  381.2 2.5 collective-permute-start.59
  385.8 2.5 collective-permute-done.57.refs_4_
  388.3 2.8 collective-permute-done.58.refs_5_
  391.1 7.8 %collective-permute-done.59.refs_6_ = bf16[128,512]{1,0:T(8,128)(2,1)S(1)} collective-permute-done((bf16[128,512]{1,0:T(8,128)(2,1)S(1)}, bf16[128,512]{1,0:T(8,128)(2,1)S(1)}, u32[]{:S(2)}, u32[]{:S(2)}) %collective-permute-start.59) | collective-permute-done | bytes 131104 | tf_op jit(solution)/shard_map/ppermute | solution.py:80
  (213 shorter events, 116.1 us)
Async XLA Ops:
  20.6 6.4 %collective-permute-start.5 = (f32[4,4096]{1,0:T(4,128)S(1)}, f32[4,4096]{1,0:T(4,128)S(1)}, u32[]{:S(2)}, u32[]{:S(2)}) collective-permute-start(f32[4,4096]{1,0:T(4,128)S(1)} %add.212), channel_id=1, source_target_pairs={{0,8},{1,9},{2,10},{3,11},{4,12},{5,13},{6,14},{7,15},{8,0},{9,1},... | collective-permute-start | bytes 196616 | tf_op jit(solution)/shard_map/ppermute | solution.py:80
  23.6 22.7 %collective-permute-start = (bf16[128,2048]{0,1:T(8,128)(2,1)S(1)}, bf16[128,2048]{0,1:T(8,128)(2,1)S(1)}, u32[]{:S(2)}, u32[]{:S(2)}) collective-permute-start(bf16[128,2048]{0,1:T(8,128)(2,1)S(1)} %copy.14), channel_id=1, source_target_pairs={{0,16},{1,17},{2,18},{3,19},{4,20},{5,21},{6,22},{7,23},{8,24},{9,... | collective-permute-start | bytes 1572872 | tf_op jit(solution)/shard_map/ppermute | solution.py:86
  47.0 13.2 %collective-permute-start.7 = (bf16[1,1,1,128,2048]{3,4,2,1,0:T(8,128)(2,1)S(1)}, bf16[1,1,1,128,2048]{3,4,2,1,0:T(8,128)(2,1)S(1)}, u32[]{:S(2)}, u32[]{:S(2)}) collective-permute-start(bf16[1,1,1,128,2048]{3,4,2,1,0:T(8,128)(2,1)S(1)} %fusion.75), channel_id=1, source_target_pairs={{0,8},{1,9},{2,10},{3,11},{4,12},{5,13},{6,14},{7,15},{8,0},{9,1},... | collective-permute-start | bytes 1572872 | tf_op jit(solution)/shard_map/ppermute | solution.py:80
  47.0 13.2 %collective-permute-start.8 = (bf16[1,1,1,128,2048]{4,3,2,1,0:T(8,128)(2,1)S(1)}, bf16[1,1,1,128,2048]{4,3,2,1,0:T(8,128)(2,1)S(1)}, u32[]{:S(2)}, u32[]{:S(2)}) collective-permute-start(bf16[1,1,1,128,2048]{4,3,2,1,0:T(8,128)(2,1)S(1)} %get-tuple-element.71), channel_id=1, source_target_pairs={{0,4},{1,5},{2,6},{3,7},{4,0},{5,1},{6,2},{7,3},{8,12},{9,13},{10,... | collective-permute-start | bytes 1572872 | tf_op jit(solution)/shard_map/ppermute | solution.py:80
  48.6 12.9 %collective-permute-start.9 = (bf16[1,1,1,128,2048]{4,3,2,1,0:T(8,128)(2,1)S(1)}, bf16[1,1,1,128,2048]{4,3,2,1,0:T(8,128)(2,1)S(1)}, u32[]{:S(2)}, u32[]{:S(2)}) collective-permute-start(bf16[1,1,1,128,2048]{4,3,2,1,0:T(8,128)(2,1)S(1)} %get-tuple-element.73), channel_id=1, source_target_pairs={{0,2},{1,3},{2,0},{3,1},{4,6},{5,7},{6,4},{7,5},{8,10},{9,11},{10,... | collective-permute-start | bytes 1572872 | tf_op jit(solution)/shard_map/ppermute | solution.py:80
  61.7 23.2 %collective-permute-start.10 = (bf16[2,1,1,128,2048]{3,4,2,1,0:T(8,128)(2,1)S(1)}, bf16[2,1,1,128,2048]{3,4,2,1,0:T(8,128)(2,1)S(1)}, u32[]{:S(2)}, u32[]{:S(2)}) collective-permute-start(bf16[2,1,1,128,2048]{3,4,2,1,0:T(8,128)(2,1)S(1)} %constant_dynamic-update-slice_fusion), channel_id=1, source_target_pairs={{0,4},{1,5},{2,6},{3,7},{4,0},{5,1},{6,2},{7,3},{8,12},{9,13},{10,... | collective-permute-start | bytes 3145736 | tf_op jit(solution)/shard_map/ppermute | solution.py:80
  62.3 23.0 %collective-permute-start.11 = (bf16[1,2,1,128,2048]{4,3,2,1,0:T(8,128)(2,1)S(1)}, bf16[1,2,1,128,2048]{4,3,2,1,0:T(8,128)(2,1)S(1)}, u32[]{:S(2)}, u32[]{:S(2)}) collective-permute-start(bf16[1,2,1,128,2048]{4,3,2,1,0:T(8,128)(2,1)S(1)} %constant_dynamic-update-slice_fusion.2), channel_id=1, source_target_pairs={{0,2},{1,3},{2,0},{3,1},{4,6},{5,7},{6,4},{7,5},{8,10},{9,11},{10,... | collective-permute-start | bytes 3145736 | tf_op jit(solution)/shard_map/ppermute | solution.py:80
  63.9 43.0 %collective-permute-start.12 = (bf16[1,1,2,128,2048]{4,3,2,1,0:T(8,128)(2,1)S(1)}, bf16[1,1,2,128,2048]{4,3,2,1,0:T(8,128)(2,1)S(1)}, u32[]{:S(2)}, u32[]{:S(2)}) collective-permute-start(bf16[1,1,2,128,2048]{4,3,2,1,0:T(8,128)(2,1)S(1)} %constant_dynamic-update-slice_fusion.4), channel_id=1, source_target_pairs={{0,8},{1,9},{2,10},{3,11},{4,12},{5,13},{6,14},{7,15},{8,0},{9,1},... | collective-permute-start | bytes 3145736 | tf_op jit(solution)/shard_map/ppermute | solution.py:80
  65.6 45.8 %collective-permute-start.6 = (bf16[128,4096]{1,0:T(8,128)(2,1)S(1)}, bf16[128,4096]{1,0:T(8,128)(2,1)S(1)}, u32[]{:S(2)}, u32[]{:S(2)}) collective-permute-start(bf16[128,4096]{1,0:T(8,128)(2,1)S(1)} %copy-done.4), channel_id=1, source_target_pairs={{0,16},{1,17},{2,18},{3,19},{4,20},{5,21},{6,22},{7,23},{8,24},{9,... | collective-permute-start | bytes 3145736 | tf_op jit(solution)/shard_map/ppermute | solution.py:86
  111.4 91.5 %collective-permute-start.13 = (bf16[2,2,1,128,2048]{3,4,2,1,0:T(8,128)(2,1)}, bf16[2,2,1,128,2048]{3,4,2,1,0:T(8,128)(2,1)}, u32[]{:S(2)}, u32[]{:S(2)}) collective-permute-start(bf16[2,2,1,128,2048]{3,4,2,1,0:T(8,128)(2,1)} %pad_maximum_fusion.12), channel_id=1, source_target_pairs={{0,2},{1,3},{2,0},{3,1},{4,6},{5,7},{6,4},{7,5},{8,10},{9,11},{10,... | collective-permute-start | bytes 6291464 | tf_op jit(solution)/shard_map/ppermute | solution.py:80
  112.0 90.9 %collective-permute-start.14 = (bf16[1,2,2,128,2048]{4,3,2,1,0:T(8,128)(2,1)}, bf16[1,2,2,128,2048]{4,3,2,1,0:T(8,128)(2,1)}, u32[]{:S(2)}, u32[]{:S(2)}) collective-permute-start(bf16[1,2,2,128,2048]{4,3,2,1,0:T(8,128)(2,1)} %pad_maximum_fusion.13), channel_id=1, source_target_pairs={{0,8},{1,9},{2,10},{3,11},{4,12},{5,13},{6,14},{7,15},{8,0},{9,1},... | collective-permute-start | bytes 6291464 | tf_op jit(solution)/shard_map/ppermute | solution.py:80
  112.0 90.9 %collective-permute-start.15 = (bf16[2,1,2,128,2048]{4,3,2,1,0:T(8,128)(2,1)}, bf16[2,1,2,128,2048]{4,3,2,1,0:T(8,128)(2,1)}, u32[]{:S(2)}, u32[]{:S(2)}) collective-permute-start(bf16[2,1,2,128,2048]{4,3,2,1,0:T(8,128)(2,1)} %pad_maximum_fusion.14), channel_id=1, source_target_pairs={{0,4},{1,5},{2,6},{3,7},{4,0},{5,1},{6,2},{7,3},{8,12},{9,13},{10,... | collective-permute-start | bytes 6291464 | tf_op jit(solution)/shard_map/ppermute | solution.py:80
  113.6 46.4 %collective-permute-start.16 = (bf16[128,512]{1,0:T(8,128)(2,1)S(1)}, bf16[128,512]{1,0:T(8,128)(2,1)S(1)}, u32[]{:S(2)}, u32[]{:S(2)}) collective-permute-start(bf16[128,512]{1,0:T(8,128)(2,1)S(1)} %get-tuple-element.167), channel_id=1, source_target_pairs={{0,2},{1,3},{2,0},{3,1},{4,6},{5,7},{6,4},{7,5},{8,10},{9,11},{10,... | collective-permute-start | bytes 393224 | tf_op jit(solution)/shard_map/ppermute | solution.py:80
  115.1 46.5 %collective-permute-start.17 = (bf16[128,512]{1,0:T(8,128)(2,1)S(1)}, bf16[128,512]{1,0:T(8,128)(2,1)S(1)}, u32[]{:S(2)}, u32[]{:S(2)}) collective-permute-start(bf16[128,512]{1,0:T(8,128)(2,1)S(1)} %get-tuple-element.166), channel_id=1, source_target_pairs={{0,4},{1,5},{2,6},{3,7},{4,0},{5,1},{6,2},{7,3},{8,12},{9,13},{10,... | collective-permute-start | bytes 393224 | tf_op jit(solution)/shard_map/ppermute | solution.py:80
  159.9 5.9 %collective-permute-start.18 = (bf16[128,512]{1,0:T(8,128)(2,1)S(1)}, bf16[128,512]{1,0:T(8,128)(2,1)S(1)}, u32[]{:S(2)}, u32[]{:S(2)}) collective-permute-start(bf16[128,512]{1,0:T(8,128)(2,1)S(1)} %get-tuple-element.165), channel_id=1, source_target_pairs={{0,6},{1,7},{2,4},{3,5},{4,2},{5,3},{6,0},{7,1},{8,14},{9,15},{10,... | collective-permute-start | bytes 393224 | tf_op jit(solution)/shard_map/ppermute | solution.py:80
  161.6 6.3 %collective-permute-start.19 = (bf16[128,512]{1,0:T(8,128)(2,1)S(1)}, bf16[128,512]{1,0:T(8,128)(2,1)S(1)}, u32[]{:S(2)}, u32[]{:S(2)}) collective-permute-start(bf16[128,512]{1,0:T(8,128)(2,1)S(1)} %get-tuple-element.164), channel_id=1, source_target_pairs={{0,8},{1,9},{2,10},{3,11},{4,12},{5,13},{6,14},{7,15},{8,0},{9,1},... | collective-permute-start | bytes 393224 | tf_op jit(solution)/shard_map/ppermute | solution.py:80
  165.8 6.4 %collective-permute-start.20 = (bf16[128,512]{1,0:T(8,128)(2,1)S(1)}, bf16[128,512]{1,0:T(8,128)(2,1)S(1)}, u32[]{:S(2)}, u32[]{:S(2)}) collective-permute-start(bf16[128,512]{1,0:T(8,128)(2,1)S(1)} %get-tuple-element.163), channel_id=1, source_target_pairs={{0,10},{1,11},{2,8},{3,9},{4,14},{5,15},{6,12},{7,13},{8,2},{9,3},... | collective-permute-start | bytes 393224 | tf_op jit(solution)/shard_map/ppermute | solution.py:80
  167.9 7.5 %collective-permute-start.21 = (bf16[128,512]{1,0:T(8,128)(2,1)S(1)}, bf16[128,512]{1,0:T(8,128)(2,1)S(1)}, u32[]{:S(2)}, u32[]{:S(2)}) collective-permute-start(bf16[128,512]{1,0:T(8,128)(2,1)S(1)} %get-tuple-element.162), channel_id=1, source_target_pairs={{0,12},{1,13},{2,14},{3,15},{4,8},{5,9},{6,10},{7,11},{8,4},{9,5},... | collective-permute-start | bytes 393224 | tf_op jit(solution)/shard_map/ppermute | solution.py:80
  172.2 6.9 %collective-permute-start.22 = (bf16[128,512]{1,0:T(8,128)(2,1)S(1)}, bf16[128,512]{1,0:T(8,128)(2,1)S(1)}, u32[]{:S(2)}, u32[]{:S(2)}) collective-permute-start(bf16[128,512]{1,0:T(8,128)(2,1)S(1)} %get-tuple-element.161), channel_id=1, source_target_pairs={{0,14},{1,15},{2,12},{3,13},{4,10},{5,11},{6,8},{7,9},{8,6},{9,7},... | collective-permute-start | bytes 393224 | tf_op jit(solution)/shard_map/ppermute | solution.py:80
  175.4 6.7 %collective-permute-start.23 = (bf16[128,512]{1,0:T(8,128)(2,1)S(1)}, bf16[128,512]{1,0:T(8,128)(2,1)S(1)}, u32[]{:S(2)}, u32[]{:S(2)}) collective-permute-start(bf16[128,512]{1,0:T(8,128)(2,1)S(1)} %get-tuple-element.175), channel_id=1, source_target_pairs={{0,2},{1,3},{2,0},{3,1},{4,6},{5,7},{6,4},{7,5},{8,10},{9,11},{10,... | collective-permute-start | bytes 393224 | tf_op jit(solution)/shard_map/ppermute | solution.py:80
  182.1 6.1 %collective-permute-start.25 = (bf16[128,512]{1,0:T(8,128)(2,1)S(1)}, bf16[128,512]{1,0:T(8,128)(2,1)S(1)}, u32[]{:S(2)}, u32[]{:S(2)}) collective-permute-start(bf16[128,512]{1,0:T(8,128)(2,1)S(1)} %get-tuple-element.173), channel_id=1, source_target_pairs={{0,6},{1,7},{2,4},{3,5},{4,2},{5,3},{6,0},{7,1},{8,14},{9,15},{10,... | collective-permute-start | bytes 393224 | tf_op jit(solution)/shard_map/ppermute | solution.py:80
  188.2 5.9 %collective-permute-start.27 = (bf16[128,512]{1,0:T(8,128)(2,1)S(1)}, bf16[128,512]{1,0:T(8,128)(2,1)S(1)}, u32[]{:S(2)}, u32[]{:S(2)}) collective-permute-start(bf16[128,512]{1,0:T(8,128)(2,1)S(1)} %get-tuple-element.171), channel_id=1, source_target_pairs={{0,10},{1,11},{2,8},{3,9},{4,14},{5,15},{6,12},{7,13},{8,2},{9,3},... | collective-permute-start | bytes 393224 | tf_op jit(solution)/shard_map/ppermute | solution.py:80
  189.7 7.5 %collective-permute-start.28 = (bf16[128,512]{1,0:T(8,128)(2,1)S(1)}, bf16[128,512]{1,0:T(8,128)(2,1)S(1)}, u32[]{:S(2)}, u32[]{:S(2)}) collective-permute-start(bf16[128,512]{1,0:T(8,128)(2,1)S(1)} %get-tuple-element.170), channel_id=1, source_target_pairs={{0,12},{1,13},{2,14},{3,15},{4,8},{5,9},{6,10},{7,11},{8,4},{9,5},... | collective-permute-start | bytes 393224 | tf_op jit(solution)/shard_map/ppermute | solution.py:80
  194.1 6.8 %collective-permute-start.29 = (bf16[128,512]{1,0:T(8,128)(2,1)S(1)}, bf16[128,512]{1,0:T(8,128)(2,1)S(1)}, u32[]{:S(2)}, u32[]{:S(2)}) collective-permute-start(bf16[128,512]{1,0:T(8,128)(2,1)S(1)} %get-tuple-element.169), channel_id=1, source_target_pairs={{0,14},{1,15},{2,12},{3,13},{4,10},{5,11},{6,8},{7,9},{8,6},{9,7},... | collective-permute-start | bytes 393224 | tf_op jit(solution)/shard_map/ppermute | solution.py:80
  234.4 12.2 %collective-permute-start.32 = (bf16[352,512]{1,0:T(8,128)(2,1)S(1)}, bf16[352,512]{1,0:T(8,128)(2,1)S(1)}, u32[]{:S(2)}, u32[]{:S(2)}) collective-permute-start(bf16[352,512]{1,0:T(8,128)(2,1)S(1)} %get-tuple-element.96), channel_id=1, source_target_pairs={{0,8},{1,9},{2,10},{3,11},{4,12},{5,13},{6,14},{7,15},{8,0},{9,1},... | collective-permute-start | bytes 1081352 | tf_op jit(solution)/shard_map/ppermute | solution.py:80
  236.6 10.2 %collective-permute-start.33 = (bf16[352,512]{1,0:T(8,128)(2,1)S(1)}, bf16[352,512]{1,0:T(8,128)(2,1)S(1)}, u32[]{:S(2)}, u32[]{:S(2)}) collective-permute-start(bf16[352,512]{1,0:T(8,128)(2,1)S(1)} %get-tuple-element.98), channel_id=1, source_target_pairs={{0,4},{1,5},{2,6},{3,7},{4,0},{5,1},{6,2},{7,3},{8,12},{9,13},{10,... | collective-permute-start | bytes 1081352 | tf_op jit(solution)/shard_map/ppermute | solution.py:80
  237.4 9.2 %collective-permute-start.34 = (bf16[320,512]{1,0:T(8,128)(2,1)S(1)}, bf16[320,512]{1,0:T(8,128)(2,1)S(1)}, u32[]{:S(2)}, u32[]{:S(2)}) collective-permute-start(bf16[320,512]{1,0:T(8,128)(2,1)S(1)} %slice.114), channel_id=1, source_target_pairs={{0,2},{1,3},{2,0},{3,1},{4,6},{5,7},{6,4},{7,5},{8,10},{9,11},{10,... | collective-permute-start | bytes 983048 | tf_op jit(solution)/shard_map/ppermute | solution.py:80
  238.5 6.9 %collective-permute-start.35 = (f32[1,512]{1,0:T(1,128)S(1)}, f32[1,512]{1,0:T(1,128)S(1)}, u32[]{:S(2)}, u32[]{:S(2)}) collective-permute-start(f32[1,512]{1,0:T(1,128)S(1)} %broadcast_in_dim.22), channel_id=1, source_target_pairs={{0,8},{1,9},{2,10},{3,11},{4,12},{5,13},{6,14},{7,15},{8,0},{9,1},... | collective-permute-start | bytes 6152 | tf_op jit(solution)/shard_map/ppermute | solution.py:80
  247.6 33.2 %collective-permute-start.36 = (bf16[352,1024]{1,0:T(8,128)(2,1)S(1)}, bf16[352,1024]{1,0:T(8,128)(2,1)}, u32[]{:S(2)}, u32[]{:S(2)}) collective-permute-start(bf16[352,1024]{1,0:T(8,128)(2,1)S(1)} %constant_dynamic-update-slice_fusion.6), channel_id=1, source_target_pairs={{0,4},{1,5},{2,6},{3,7},{4,0},{5,1},{6,2},{7,3},{8,12},{9,13},{10,... | collective-permute-start | bytes 2162696 | tf_op jit(solution)/shard_map/ppermute | solution.py:80
  248.8 32.1 %collective-permute-start.37 = (bf16[352,1024]{1,0:T(8,128)(2,1)S(1)}, bf16[352,1024]{1,0:T(8,128)(2,1)}, u32[]{:S(2)}, u32[]{:S(2)}) collective-permute-start(bf16[352,1024]{1,0:T(8,128)(2,1)S(1)} %constant_dynamic-update-slice_fusion.8), channel_id=1, source_target_pairs={{0,2},{1,3},{2,0},{3,1},{4,6},{5,7},{6,4},{7,5},{8,10},{9,11},{10,... | collective-permute-start | bytes 2162696 | tf_op jit(solution)/shard_map/ppermute | solution.py:80
  251.0 29.8 %collective-permute-start.38 = (bf16[320,1024]{1,0:T(8,128)(2,1)}, bf16[320,1024]{1,0:T(8,128)(2,1)}, u32[]{:S(2)}, u32[]{:S(2)}) collective-permute-start(bf16[320,1024]{1,0:T(8,128)(2,1)} %constant_dynamic-update-slice_fusion.10), channel_id=1, source_target_pairs={{0,8},{1,9},{2,10},{3,11},{4,12},{5,13},{6,14},{7,15},{8,0},{9,1},... | collective-permute-start | bytes 1966088 | tf_op jit(solution)/shard_map/ppermute | solution.py:80
  252.7 46.4 %collective-permute-start.31 = (bf16[1024,512]{1,0:T(8,128)(2,1)S(1)}, bf16[1024,512]{1,0:T(8,128)(2,1)}, u32[]{:S(2)}, u32[]{:S(2)}) collective-permute-start(bf16[1024,512]{1,0:T(8,128)(2,1)S(1)} %get-tuple-element.109), channel_id=1, source_target_pairs={{0,16},{1,17},{2,18},{3,19},{4,20},{5,21},{6,22},{7,23},{8,24},{9,... | collective-permute-start | bytes 3145736 | tf_op jit(solution)/shard_map/ppermute | solution.py:86
  254.2 10.7 %collective-permute-start.39 = (f32[1,512]{1,0:T(1,128)S(1)}, f32[1,512]{1,0:T(1,128)}, u32[]{:S(2)}, u32[]{:S(2)}) collective-permute-start(f32[1,512]{1,0:T(1,128)S(1)} %broadcast_add_fusion), channel_id=1, source_target_pairs={{0,4},{1,5},{2,6},{3,7},{4,0},{5,1},{6,2},{7,3},{8,12},{9,13},{10,... | collective-permute-start | bytes 6152 | tf_op jit(solution)/shard_map/ppermute | solution.py:80
  304.1 9.8 %collective-permute-start.40 = (bf16[2,1024,512]{2,1,0:T(8,128)(2,1)}, bf16[2,1024,512]{2,1,0:T(8,128)(2,1)}, u32[]{:S(2)}, u32[]{:S(2)}) collective-permute-start(bf16[2,1024,512]{2,1,0:T(8,128)(2,1)} %bitcast_dynamic-update-slice_fusion), channel_id=1, source_target_pairs={{0,1},{1,0},{2,3},{3,2},{4,5},{5,4},{6,7},{7,6},{8,9},{9,8},{10,11... | collective-permute-start | bytes 6291464 | tf_op jit(solution)/shard_map/ppermute | solution.py:80
  308.3 46.4 %collective-permute-start.48 = (bf16[256,1024]{0,1:T(8,128)(2,1)S(1)}, bf16[256,1024]{0,1:T(8,128)(2,1)S(1)}, u32[]{:S(2)}, u32[]{:S(2)}) collective-permute-start(bf16[256,1024]{0,1:T(8,128)(2,1)S(1)} %get-tuple-element.156), channel_id=1, source_target_pairs={{0,1},{1,0},{2,3},{3,2},{4,5},{5,4},{6,7},{7,6},{8,9},{9,8},{10,11... | collective-permute-start | bytes 1572872 | tf_op jit(solution)/shard_map/ppermute | solution.py:80
  309.0 16.4 %collective-permute-start.44 = (bf16[256,4096]{1,0:T(8,128)(2,1)S(1)}, bf16[256,4096]{1,0:T(8,128)(2,1)S(1)}, u32[]{:S(2)}, u32[]{:S(2)}) collective-permute-start(bf16[256,4096]{1,0:T(8,128)(2,1)S(1)} %pad_maximum_fusion.15), channel_id=1, source_target_pairs={{0,1},{1,0},{2,3},{3,2},{4,5},{5,4},{6,7},{7,6},{8,9},{9,8},{10,11... | collective-permute-start | bytes 6291464 | tf_op jit(solution)/shard_map/ppermute | solution.py:80
  312.8 33.6 %collective-permute-start.45 = (bf16[352,2048]{1,0:T(8,128)(2,1)S(1)}, bf16[352,2048]{1,0:T(8,128)(2,1)S(1)}, u32[]{:S(2)}, u32[]{:S(2)}) collective-permute-start(bf16[352,2048]{1,0:T(8,128)(2,1)S(1)} %copy-done.13), channel_id=1, source_target_pairs={{0,2},{1,3},{2,0},{3,1},{4,6},{5,7},{6,4},{7,5},{8,10},{9,11},{10,... | collective-permute-start | bytes 4325384 | tf_op jit(solution)/shard_map/ppermute | solution.py:80
  313.9 33.5 %collective-permute-start.46 = (bf16[352,2048]{1,0:T(8,128)(2,1)S(1)}, bf16[352,2048]{1,0:T(8,128)(2,1)S(1)}, u32[]{:S(2)}, u32[]{:S(2)}) collective-permute-start(bf16[352,2048]{1,0:T(8,128)(2,1)S(1)} %copy-done.14), channel_id=1, source_target_pairs={{0,8},{1,9},{2,10},{3,11},{4,12},{5,13},{6,14},{7,15},{8,0},{9,1},... | collective-permute-start | bytes 4325384 | tf_op jit(solution)/shard_map/ppermute | solution.py:80
  313.9 31.8 %collective-permute-start.47 = (bf16[320,2048]{1,0:T(8,128)(2,1)S(1)}, bf16[320,2048]{1,0:T(8,128)(2,1)S(1)}, u32[]{:S(2)}, u32[]{:S(2)}) collective-permute-start(bf16[320,2048]{1,0:T(8,128)(2,1)S(1)} %copy-done.15), channel_id=1, source_target_pairs={{0,4},{1,5},{2,6},{3,7},{4,0},{5,1},{6,2},{7,3},{8,12},{9,13},{10,... | collective-permute-start | bytes 3932168 | tf_op jit(solution)/shard_map/ppermute | solution.py:80
  326.6 18.5 %collective-permute-start.43 = (f32[3,512]{1,0:T(4,128)S(1)}, f32[3,512]{1,0:T(4,128)S(1)}, u32[]{:S(2)}, u32[]{:S(2)}) collective-permute-start(f32[3,512]{1,0:T(4,128)S(1)} %fusion.90), channel_id=1, source_target_pairs={{0,16},{1,17},{2,18},{3,19},{4,20},{5,21},{6,22},{7,23},{8,24},{9,... | collective-permute-start | bytes 18440 | tf_op jit(solution)/shard_map/ppermute | solution.py:80
  371.3 30.7 %collective-permute-start.53 = (bf16[128,2048]{0,1:T(8,128)(2,1)S(1)}, bf16[128,2048]{0,1:T(8,128)(2,1)S(1)}, u32[]{:S(2)}, u32[]{:S(2)}) collective-permute-start(bf16[128,2048]{0,1:T(8,128)(2,1)S(1)} %get-tuple-element.151), channel_id=1, source_target_pairs={{0,16},{1,17},{2,18},{3,19},{4,20},{5,21},{6,22},{7,23},{8,24},{9,... | collective-permute-start | bytes 1572872 | tf_op jit(solution)/shard_map/ppermute | solution.py:86
  373.2 6.3 %collective-permute-start.54 = (bf16[128,512]{1,0:T(8,128)(2,1)S(1)}, bf16[128,512]{1,0:T(8,128)(2,1)S(1)}, u32[]{:S(2)}, u32[]{:S(2)}) collective-permute-start(bf16[128,512]{1,0:T(8,128)(2,1)S(1)} %get-tuple-element.149), channel_id=1, source_target_pairs={{0,2},{1,3},{2,0},{3,1},{4,6},{5,7},{6,4},{7,5},{8,10},{9,11},{10,... | collective-permute-start | bytes 393224 | tf_op jit(solution)/shard_map/ppermute | solution.py:80
  374.3 6.9 %collective-permute-start.55 = (bf16[128,512]{1,0:T(8,128)(2,1)S(1)}, bf16[128,512]{1,0:T(8,128)(2,1)S(1)}, u32[]{:S(2)}, u32[]{:S(2)}) collective-permute-start(bf16[128,512]{1,0:T(8,128)(2,1)S(1)} %get-tuple-element.148), channel_id=1, source_target_pairs={{0,4},{1,5},{2,6},{3,7},{4,0},{5,1},{6,2},{7,3},{8,12},{9,13},{10,... | collective-permute-start | bytes 393224 | tf_op jit(solution)/shard_map/ppermute | solution.py:80
  375.1 8.6 %collective-permute-start.56 = (bf16[128,512]{1,0:T(8,128)(2,1)S(1)}, bf16[128,512]{1,0:T(8,128)(2,1)S(1)}, u32[]{:S(2)}, u32[]{:S(2)}) collective-permute-start(bf16[128,512]{1,0:T(8,128)(2,1)S(1)} %get-tuple-element.147), channel_id=1, source_target_pairs={{0,6},{1,7},{2,4},{3,5},{4,2},{5,3},{6,0},{7,1},{8,14},{9,15},{10,... | collective-permute-start | bytes 393224 | tf_op jit(solution)/shard_map/ppermute | solution.py:80
  376.8 11.5 %collective-permute-start.57 = (bf16[128,512]{1,0:T(8,128)(2,1)S(1)}, bf16[128,512]{1,0:T(8,128)(2,1)S(1)}, u32[]{:S(2)}, u32[]{:S(2)}) collective-permute-start(bf16[128,512]{1,0:T(8,128)(2,1)S(1)} %get-tuple-element.146), channel_id=1, source_target_pairs={{0,8},{1,9},{2,10},{3,11},{4,12},{5,13},{6,14},{7,15},{8,0},{9,1},... | collective-permute-start | bytes 393224 | tf_op jit(solution)/shard_map/ppermute | solution.py:80
  379.5 11.6 %collective-permute-start.58 = (bf16[128,512]{1,0:T(8,128)(2,1)S(1)}, bf16[128,512]{1,0:T(8,128)(2,1)S(1)}, u32[]{:S(2)}, u32[]{:S(2)}) collective-permute-start(bf16[128,512]{1,0:T(8,128)(2,1)S(1)} %get-tuple-element.145), channel_id=1, source_target_pairs={{0,10},{1,11},{2,8},{3,9},{4,14},{5,15},{6,12},{7,13},{8,2},{9,3},... | collective-permute-start | bytes 393224 | tf_op jit(solution)/shard_map/ppermute | solution.py:80
  381.2 17.7 %collective-permute-start.59 = (bf16[128,512]{1,0:T(8,128)(2,1)S(1)}, bf16[128,512]{1,0:T(8,128)(2,1)S(1)}, u32[]{:S(2)}, u32[]{:S(2)}) collective-permute-start(bf16[128,512]{1,0:T(8,128)(2,1)S(1)} %get-tuple-element.144), channel_id=1, source_target_pairs={{0,12},{1,13},{2,14},{3,15},{4,8},{5,9},{6,10},{7,11},{8,4},{9,5},... | collective-permute-start | bytes 393224 | tf_op jit(solution)/shard_map/ppermute | solution.py:80
  383.7 16.9 %collective-permute-start.60 = (bf16[128,512]{1,0:T(8,128)(2,1)S(1)}, bf16[128,512]{1,0:T(8,128)(2,1)S(1)}, u32[]{:S(2)}, u32[]{:S(2)}) collective-permute-start(bf16[128,512]{1,0:T(8,128)(2,1)S(1)} %get-tuple-element.143), channel_id=1, source_target_pairs={{0,14},{1,15},{2,12},{3,13},{4,10},{5,11},{6,8},{7,9},{8,6},{9,7},... | collective-permute-start | bytes 393224 | tf_op jit(solution)/shard_map/ppermute | solution.py:80
  (35 other events, 371.6 us)

commit v3 on v0

v3 whole, which is shorter than its diff:
```python
import functools

import jax
import jax.numpy as jnp
from jax import lax
from jax.experimental import pallas as pl
from jax.experimental.pallas import tpu as pltpu
from jax.sharding import PartitionSpec as P

lam = 0.0051
eps = 1e-05

cube = 8
orders = ((4, 2, 1), (1, 4, 2), (2, 1, 4))
together = lax.optimization_barrier
vmem = pl.BlockSpec(memory_space=pltpu.VMEM)
smem = pl.BlockSpec(memory_space=pltpu.SMEM)
roomy = pltpu.CompilerParams(vmem_limit_bytes=32 << 20)


def places(order):
    return [
        sum(bit for step, bit in enumerate(order) if place >> step & 1) for place in range(cube)
    ]


def cuts(width):
    part = -(-width // 384) * 128
    edges = list(range(0, width, part)) + [width]
    return list(zip(edges, edges[1:]))


def prepare_kernel(half, at_ref, a_ref, b_ref, *outs):
    near_ref, rest_ref, eighths_ref, sums_ref = outs[:4]
    rows, width = a_ref.shape
    for n in range(width // half):
        column = a_ref[:, pl.ds(pl.multiple_of(at_ref[n] * half, half), half)]
        if n < 2:
            near_ref[:, n * half : (n + 1) * half] = column
        else:
            rest_ref[:, (n - 2) * half : (n - 1) * half] = column
    parts = iter(outs[4:])
    for full_ref in (near_ref, rest_ref):
        for lo, hi in cuts(full_ref.shape[1]):
            next(parts)[...] = full_ref[:, lo:hi]
    narrow = width // cube
    for i in range(cube):
        here = slice(i * narrow, (i + 1) * narrow)
        eighths_ref[i] = b_ref[:, here]
        for n, ref in enumerate((a_ref, b_ref)):
            x = ref[:, here].astype(jnp.float32)
            sums_ref[2 * n : 2 * n + 1, here] = jnp.sum(x, axis=0, keepdims=True)
            sums_ref[2 * n + 1 : 2 * n + 2, here] = jnp.sum(x * x, axis=0, keepdims=True)


def prepare(view_a, view_b, at, half):
    rows, width = view_a.shape
    widths = [2 * half, width - 2 * half]
    shapes = [(rows, n) for n in widths] + [(cube, rows, width // cube)]
    parts = [(rows, hi - lo) for n in widths for lo, hi in cuts(n)]
    outs = [jax.ShapeDtypeStruct(shape, jnp.bfloat16) for shape in shapes]
    outs += [jax.ShapeDtypeStruct((4, width), jnp.float32)]
    outs += [jax.ShapeDtypeStruct(shape, jnp.bfloat16) for shape in parts]
    near, rest, eighths, sums, *parts = pl.pallas_call(
        functools.partial(prepare_kernel, half),
        out_shape=outs,
        in_specs=[smem, vmem, vmem],
        out_specs=[vmem] * len(outs),
        compiler_params=roomy,
    )(at, view_a, view_b)
    first = len(cuts(widths[0]))
    return near, rest, eighths, sums, parts[:first], parts[first:]


def double_kernel(*refs):
    n = len(refs) // 3
    for x, y, out in zip(refs[:n], refs[n : 2 * n], refs[2 * n :]):
        rows = x.shape[0]
        out[:rows, :] = x[...]
        out[rows:, :] = y[...]


def double(xs, ys):
    return pl.pallas_call(
        double_kernel,
        out_shape=[jax.ShapeDtypeStruct((2 * x.shape[0], x.shape[1]), x.dtype) for x in xs],
        in_specs=[vmem] * (2 * len(xs)),
        out_specs=[vmem] * len(xs),
        compiler_params=roomy,
    )(*xs, *ys)


def merge_kernel(orders, mean_ref, inv_ref, *refs):
    pieces, out_ref = refs[:-1], refs[-1]
    rows = pieces[0].shape[0] * 2 // cube
    start = 0
    for n, order in enumerate(orders[: len(pieces) // 2]):
        size = pieces[2 * n].shape[1]
        mean, inv = mean_ref[:, start : start + size], inv_ref[:, start : start + size]
        for m, r in enumerate(places(order)):
            piece, first = pieces[2 * n + 2 * m // cube], m % (cube // 2) * rows
            raw = piece[first : first + rows, :].astype(jnp.float32)
            out_ref[r * rows : (r + 1) * rows, start : start + size] = (
                (raw - mean) * inv
            ).astype(jnp.bfloat16)
        start += size


def merge(moving, arrived, orders, mean, inv):
    pieces = [x for pair in zip(moving, arrived) for x in pair]
    return pl.pallas_call(
        functools.partial(merge_kernel, orders),
        out_shape=jax.ShapeDtypeStruct((2 * pieces[0].shape[0], mean.shape[1]), jnp.bfloat16),
        in_specs=[vmem] * (2 + len(pieces)),
        out_specs=vmem,
        compiler_params=roomy,
    )(mean, inv, *pieces)


def arrange_kernel(k_ref, blocks_ref, mean_ref, inv_ref, raw_ref, norm_ref):
    rows = blocks_ref.shape[1]
    for r in range(cube):
        raw = blocks_ref[k_ref[0] ^ r]
        raw_ref[r * rows : (r + 1) * rows, :] = raw
        norm_ref[r * rows : (r + 1) * rows, :] = (
            (raw.astype(jnp.float32) - mean_ref[...]) * inv_ref[...]
        ).astype(jnp.bfloat16)


def arrange(blocks, mean, inv, k):
    _, rows, n = blocks.shape
    out = jax.ShapeDtypeStruct((cube * rows, n), jnp.bfloat16)
    return pl.pallas_call(
        arrange_kernel,
        out_shape=(out, out),
        in_specs=[smem] + [vmem] * 3,
        out_specs=(vmem, vmem),
        compiler_params=roomy,
    )(k.reshape(1), blocks, mean, inv)


def finish_kernel(k_ref, grad_ref, raw_ref, mean_ref, inv_ref, first_ref, second_ref, out_ref):
    rows = out_ref.shape[1]
    mean, inv = mean_ref[...], inv_ref[...]
    for r in range(cube):
        here = slice(r * rows, (r + 1) * rows)
        flat = (raw_ref[here, :].astype(jnp.float32) - mean) * inv
        out = inv * (grad_ref[here, :] - first_ref[...] - flat * second_ref[...])
        out_ref[k_ref[0] ^ r] = out.astype(jnp.bfloat16)


def finish(grad, raw, mean, inv, first, second, k):
    size, n = grad.shape
    return pl.pallas_call(
        finish_kernel,
        out_shape=jax.ShapeDtypeStruct((cube, size // cube, n), jnp.bfloat16),
        in_specs=[smem] + [vmem] * 6,
        out_specs=vmem,
        compiler_params=roomy,
    )(k.reshape(1), grad, raw, mean, inv, first, second)


def place_kernel(at_ref, *refs):
    blocks, out_ref = refs[:-1], refs[-1]
    half = blocks[0].shape[1] // 2
    for n, block in enumerate(blocks):
        for side in range(2):
            start = pl.multiple_of(at_ref[2 * n + side] * half, half)
            out_ref[:, pl.ds(start, half)] = block[:, side * half : (side + 1) * half]


def place(blocks, at):
    rows, n = blocks[0].shape
    return pl.pallas_call(
        place_kernel,
        out_shape=jax.ShapeDtypeStruct((rows, n * len(blocks)), jnp.bfloat16),
        in_specs=[smem] + [vmem] * len(blocks),
        out_specs=vmem,
        compiler_params=roomy,
    )(at, *blocks)


def dot(x, y, contract):
    return lax.dot_general(x, y, (contract, ((), ())), preferred_element_type=jnp.float32)


def cross_kernel(orders, k_ref, raw_ref, mean_ref, inv_ref, rows_ref, *refs):
    pieces, (out_ref, sums_ref) = refs[:-2], refs[-2:]
    narrow = rows_ref.shape[1] // cube
    start = 0
    for n, order in enumerate(orders[: len(pieces) // 2]):
        size = pieces[2 * n].shape[1]
        total = 0.0
        for m, r in enumerate(places(order)):
            piece = pieces[2 * n + 2 * m // cube]
            first = m % (cube // 2) * narrow
            at = pl.multiple_of((k_ref[0] ^ r) * narrow, narrow)
            total = total + jnp.dot(
                rows_ref[:, pl.ds(at, narrow)],
                piece[first : first + narrow, :],
                preferred_element_type=jnp.float32,
            )
        out_ref[:, start : start + size] = total
        start += size
    out = out_ref[...]
    flat = (raw_ref[...].astype(jnp.float32) - mean_ref[...]) * inv_ref[...]
    sums = jnp.concatenate(
        [jnp.sum(out, axis=0, keepdims=True), jnp.sum(out * flat, axis=0, keepdims=True)]
    )

    @pl.when(pl.program_id(0) == 0)
    def _():
        sums_ref[...] = sums

    @pl.when(pl.program_id(0) > 0)
    def _():
        sums_ref[...] += sums


def cross_products(rows, pieces, orders, raw, mean, inv, k):
    size, n = raw.shape
    block = min(size, 512)

    def whole(x):
        return pl.BlockSpec(x.shape, lambda i: (0, 0))

    def part(x):
        return pl.BlockSpec((block, x.shape[1]), lambda i: (i, 0))

    return pl.pallas_call(
        functools.partial(cross_kernel, orders),
        grid=(size // block,),
        out_shape=(
            jax.ShapeDtypeStruct((size, n), jnp.float32),
            jax.ShapeDtypeStruct((2, n), jnp.float32),
        ),
        in_specs=[smem, part(raw), whole(mean), whole(inv), part(rows)]
        + [whole(x) for x in pieces],
        out_specs=(part(raw), pl.BlockSpec((2, n), lambda i: (0, 0))),
        compiler_params=pltpu.CompilerParams(vmem_limit_bytes=48 << 20),
    )(k.reshape(1), raw, mean, inv, rows, *pieces)


def shards(view_a, view_b):
    f32, bf16 = jnp.float32, jnp.bfloat16
    rows, width = view_a.shape
    devices = lax.axis_size("dp")
    count = rows * devices
    cubes = devices // (2 * cube)
    index = lax.axis_index("dp")
    c, k, h = index % 2, index // 2 % cube, index // (2 * cube)
    wide, half, narrow = width // cubes, width // cubes // 2, width // cube
    groups = [
        [(g * cube + i) * 2 + core for i in range(cube)] for g in range(cubes) for core in range(2)
    ]

    def swap(x, mask):
        return lax.ppermute(x, "dp", [(i, i ^ mask) for i in range(devices)])

    def swap_k(x, bit):
        return swap(x, 2 * bit)

    def turn(x, step):
        return lax.ppermute(
            x, "dp", [(i, (i + 2 * cube * step) % devices) for i in range(devices)]
        )

    def turns(x):
        return [turn(x, s) for s in range(1, cubes)]

    def exchange(x):
        return lax.all_to_all(
            x, "dp", split_axis=0, concat_axis=0, axis_index_groups=groups, tiled=True
        )

    def columns(x, start, size):
        return lax.dynamic_slice_in_dim(x, start, size, axis=1)

    at = [(h + s) % cubes * 2 + core for s in range(cubes) for core in (c, 1 - c)]

    h_masks = [2 * cube << bit for bit in range(cubes.bit_length() - 1)]

    def by_place(x, sides):
        return jnp.concatenate([columns(x, place * half, half) for place in sides], 1)

    def send(moving, step):
        return [swap_k(x, order[step]) for x, order in zip(moving, orders)]

    whole_near, whole_rest, eighths, sums, near, rest = prepare(view_a, view_b, jnp.stack(at), half)
    parts_a = [whole_near] + [whole_rest[:, s * wide : (s + 1) * wide] for s in range(cubes - 1)]
    cuts_b = (0, 3 * rows // 8, 3 * rows // 4, rows)
    pieces_b = [view_b[lo:hi] for lo, hi in zip(cuts_b, cuts_b[1:])]
    others_b = []

    arrived = send(rest, 0)
    for mask in (1, 2, 4):
        sums = sums + swap(sums, mask)
    rest, arrived, sums, pieces_b, near, eighths = together(
        (rest, arrived, sums, pieces_b, near, eighths)
    )
    rest = double(rest, arrived)
    arrived = send(rest, 1)
    own_b = exchange(eighths)
    others_b.append(turns(pieces_b[0]))
    for mask in h_masks + [8]:
        sums = sums + swap(sums, mask)
    rest, arrived, others_b, sums, pieces_b, own_b = together(
        (rest, arrived, others_b, sums, pieces_b, own_b)
    )
    rest = double(rest, arrived)
    arrived = send(rest, 2)
    others_b.append(turns(pieces_b[1]))
    means = sums / count
    mean_a, mean_b = means[0:1], means[2:3]
    inv_a = 1.0 / jnp.sqrt(means[1:2] - mean_a * mean_a + eps)
    inv_b = 1.0 / jnp.sqrt(means[3:4] - mean_b * mean_b + eps)
    mean_bn = columns(mean_b, k * narrow, narrow)
    inv_bn = columns(inv_b, k * narrow, narrow)
    mean_ap, inv_ap = by_place(mean_a, at), by_place(inv_a, at)
    near_b, right = arrange(own_b, mean_bn, inv_bn, k)
    rest, arrived, others_b, pieces_b, near_b, right, mean_ap, inv_ap = together(
        (rest, arrived, others_b, pieces_b, near_b, right, mean_ap, inv_ap)
    )

    def product(left, s):
        first = dot(right, left[:, s * wide + half : (s + 1) * wide], ((0,), (0,)))
        return swap(first, 1) + dot(right, left[:, s * wide : s * wide + half], ((0,), (0,)))

    def diagonal(s):
        return (
            lax.broadcasted_iota(jnp.int32, (narrow, half), 1) + at[2 * s] * half
            == lax.broadcasted_iota(jnp.int32, (narrow, half), 0) + k * narrow
        )

    rest = merge(rest, arrived, orders, mean_ap[:, wide:], inv_ap[:, wide:])
    others_b.append(turns(pieces_b[2]))
    arrived = send(near, 0)
    partials = [product(rest, s) for s in range(cubes - 1)]
    exact = [
        jnp.sum(jnp.where(diagonal(s + 1), x, 0.0), axis=1).reshape(1, narrow)
        for s, x in enumerate(partials)
    ]
    partials = [x.astype(bf16) for x in partials]
    partials, exact, near, arrived, others_b = together(
        (partials, exact, near, arrived, others_b)
    )
    near = double(near, arrived)

    cuts_p = (0, narrow // 4, 5 * narrow // 8, narrow)
    received = []
    for step in (1, 2):
        arrived = send(near, step)
        received.append(
            [turn(x[cuts_p[step - 1] : cuts_p[step]], s + 1) for s, x in enumerate(partials)]
        )
        if step == 1:
            near, arrived, received, partials, exact = together(
                (near, arrived, received, partials, exact)
            )
            near = double(near, arrived)
        else:
            exact = [turn(x, s + 1) for s, x in enumerate(exact)]
            others_b = [jnp.concatenate(pieces, 0) for pieces in zip(*others_b)]
            pair_b = jnp.concatenate([view_b] + others_b, 0)
            pair_b = ((pair_b.astype(f32) - mean_b) * inv_b).astype(bf16)
            norm_b = jnp.concatenate([pair_b, swap(pair_b, 1)], 0)
            near, arrived, received, partials, exact, norm_b = together(
                (near, arrived, received, partials, exact, norm_b)
            )
    received.append([turn(x[cuts_p[2] :], s + 1) for s, x in enumerate(partials)])
    near = merge(near, arrived, orders, mean_ap[:, :wide], inv_ap[:, :wide])
    corr = product(near, 0)
    corr, received = together((corr, received))
    diag = diagonal(0)
    for blocks, line in zip(zip(*received), exact):
        block = jnp.concatenate(blocks, 0).astype(f32)
        corr = corr + jnp.where(diag, line.reshape(narrow, 1), block)
    corr = corr / count
    loss = jnp.sum(jnp.where(diag, (1.0 - corr) ** 2, lam * corr * corr))
    gcorr = jnp.where(diag, 2.0 * (corr - 1.0), 2.0 * lam * corr).astype(bf16)

    moving = [gcorr[:, lo:hi] for lo, hi in cuts(half)]
    cuts_g = (0, narrow // 4, 5 * narrow // 8, narrow)
    loss = jnp.full((8, 128), loss, f32)
    turned, sibling, far_a = [], [], []
    for step in range(3):
        arrived = send(moving, step)
        turned.append(turns(gcorr[cuts_g[step] : cuts_g[step + 1]]))
        if step > 0:
            sibling.append([swap(x, 1) for x in turned[step - 1]])
            far_a.append(
                [
                    turn(x[:, (2 - step) * half : (3 - step) * half], s + 1)
                    for s, x in enumerate(parts_a[1:])
                ]
            )
        if step == 0:
            own = jnp.concatenate([gcorr, swap(gcorr, 1)], 1)
            loss = loss + swap(loss, 1)
            moving, arrived, turned, gcorr, own, loss, parts_a = together(
                (moving, arrived, turned, gcorr, own, loss, parts_a)
            )
        elif step == 1:
            grad_nb = dot(near, own, ((1,), (1,)))
            moving, arrived, turned, gcorr, sibling, far_a, parts_a, grad_nb = together(
                (moving, arrived, turned, gcorr, sibling, far_a, parts_a, grad_nb)
            )
        else:
            other_a = swap(jnp.concatenate([parts_a[0][:, half:]] + far_a[0], 0), 1)
            moving, arrived, turned, sibling, far_a, other_a, loss = together(
                (moving, arrived, turned, sibling, far_a, other_a, loss)
            )
        if step < 2:
            moving = double(moving, arrived)

    mean_ah, inv_ah = mean_ap[:, :half], inv_ap[:, :half]
    sibling.append([swap(x, 1) for x in turned[2]])
    all_a = jnp.concatenate([parts_a[0][:, :half]] + far_a[1] + [other_a], 0)
    pieces = [x for pair in zip(moving, arrived) for x in pair]
    cross, stats_a = cross_products(norm_b, pieces, orders, all_a, mean_ah, inv_ah, k)
    for mask in h_masks:
        loss = loss + swap(loss, mask)
    cross, stats_a, sibling, loss = together((cross, stats_a, sibling, loss))
    stats_a = jnp.concatenate([stats_a, jnp.full((1, half), loss[0, 0], f32)])
    for bit in (1, 2, 4):
        stats_a = stats_a + swap_k(stats_a, bit)

    for s in range(1, cubes):
        for side, blocks in enumerate((turned, sibling)):
            block = jnp.concatenate([x[cubes - s - 1] for x in blocks], 0)
            start = (s - 1) * wide + side * half
            grad_nb = grad_nb + dot(rest[:, start : start + half], block, ((1,), (1,)))
    flat_b = (near_b.astype(f32) - mean_bn) * inv_bn
    stats_b = jnp.stack([jnp.sum(grad_nb, axis=0), jnp.sum(grad_nb * flat_b, axis=0)])
    for mask in [1] + h_masks:
        stats_b = stats_b + swap(stats_b, mask)
    stats_a, stats_b, grad_nb = together((stats_a, stats_b, grad_nb))
    loss = stats_a[2, 0]
    stats_a, stats_b = stats_a / count, stats_b / count

    flat_a = (all_a.astype(f32) - mean_ah) * inv_ah
    out_a = (inv_ah * (cross - stats_a[0:1] - flat_a * stats_a[1:2])).astype(bf16)
    mine = cubes * rows
    both = jnp.concatenate([out_a[:mine], swap(out_a[mine:], 1)], 1)
    blocks = [both[s * rows : (s + 1) * rows] for s in range(cubes)]
    blocks = [blocks[0]] + [turn(blocks[s], -s) for s in range(1, cubes)]
    grad_a = place(blocks, jnp.stack(at))
    out_b = exchange(finish(grad_nb, near_b, mean_bn, inv_bn, stats_b[0:1], stats_b[1:2], k))
    grad_b = jnp.concatenate([out_b[r] for r in range(cube)], 1)
    return (loss, grad_a, grad_b)


def solution(mesh):
    return jax.shard_map(
        shards,
        mesh=mesh,
        in_specs=(P("dp", None), P("dp", None)),
        out_specs=(P(), P("dp", None), P("dp", None)),
        check_vma=False,
    )
```

time: 1160 us -> 340 us (0.29)
  waiting for transfers between devices: 1030 us -> 193 us
  starting transfers between devices: 0.3 us -> 81.7 us
  matrix products: 57.6 us -> 14.6 us
  blocking collectives: 39.5 us -> 0 us
  Pallas kernels: 0 us -> 20.2 us
  between operations: 15.8 us -> 1.42 us
  local copies, waits for them, and re-layouts: 0.01 us -> 12.4 us
    reduce_scatter x1 -> x0, waiting for transfers between devices: 704 us -> none  [shards(): lax.psum_scatter(lax.dot_general(block, norm_b, (((0,), (0,)), ((), ())),...]
    all_gather x1 -> x0, waiting for transfers between devices: 201 us -> none  [shards(): piece = lax.all_gather(gcorr, 'dp', axis=0, tiled=True)]
    ppermute x0 -> x61, waiting for transfers between devices: none -> 193 us  [the longest x13 142 us: turn(): lax.ppermute(x, 'dp', [(i, (i + 2 * cube * step) % devices) for i in rang...]
    psum x1 -> x0, waiting for transfers between devices: 125 us -> none  [shards(): lax.psum((jnp.sum(full_a, axis=0), jnp.sum(full_a * full_a, axis=0), jnp....]
    ppermute x0 -> x61, starting transfers between devices: none -> 73.9 us  [the longest x48 49.8 us: swap(): return lax.ppermute(x, 'dp', [(i, i ^ mask) for i in range(devices)])]
    dot_general x3 -> x7, matrix products: 57.6 us -> 14.6 us  [dot(): lax.dot_general(x, y, (contract, ((), ())), preferred_element_type=jnp.fl...]
    psum x1 -> x0, blocking collectives: 39.5 us -> none  [shards(): loss = lax.psum(loss_part, 'dp')]
    pallas_call x0 -> x13, Pallas kernels: none -> 20.2 us  [the longest x1 10.8 us: cross_products(): pl.pallas_call(functools.partial(cross_kernel, orders), grid=(size // blo...]
  transfers between devices with their start and end apart: 3 -> 63, of which waited for: 3 -> 28; matrix products, arithmetic and copies ran while one was open for 0% -> 8% of each run, Pallas kernels for 0% -> 4%
where the time goes in v3:
time: 340 us
  waiting for transfers between devices  193 us (57%)
  starting transfers between devices  81.7 us (24%)
  Pallas kernels  20.2 us (6%)
  other arithmetic  16.6 us (5%)
  matrix products  14.6 us (4%)
  local copies, waits for them, and re-layouts  12.4 us (4%)
    ppermute x13, waiting for transfers between devices, turn(): lax.ppermute(x, 'dp', [(i, (i + 2 * cube * step) % devices) for i in rang...  142 us
    ppermute x48, waiting for transfers between devices, swap(): return lax.ppermute(x, 'dp', [(i, i ^ mask) for i in range(devices)])  50.5 us
    ppermute x48, starting transfers between devices, swap(): return lax.ppermute(x, 'dp', [(i, i ^ mask) for i in range(devices)])  49.8 us
    ppermute x13, starting transfers between devices, turn(): lax.ppermute(x, 'dp', [(i, (i + 2 * cube * step) % devices) for i in rang...  24.1 us
    dot_general x7, matrix products, dot(): lax.dot_general(x, y, (contract, ((), ())), preferred_element_type=jnp.fl...  14.6 us
    pallas_call x1, Pallas kernels, cross_products(): pl.pallas_call(functools.partial(cross_kernel, orders), grid=(size // blo...  10.8 us
    unnamed x57, local copies, waits for them, and re-layouts  7.98 us
    all_to_all x2, starting transfers between devices, exchange(): lax.all_to_all(x, 'dp', split_axis=0, concat_axis=0, axis_index_groups=gr...  7.86 us
  transfers between devices with their start and end apart: 63, of which 28 were waited for; matrix products, arithmetic and copies ran while one was open for 8% of the time, Pallas kernels for 4%

profile of v3, /device:TPU:0, one launch (start us, length us, event | category | flops | bytes accessed | tf_op | source)
XLA Modules:
  0.0 339.6 jit_solution(17979662277183326124)
XLA Ops:
  3.2 2.1 shard_map.49
  6.8 2.9 collective-permute-start.4
  15.7 2.2 collective-permute-done.5
  19.4 4.3 %all-to-all-start = ((bf16[8,128,512]{2,1,0:T(8,128)(2,1)}), bf16[8,128,512]{2,1,0:T(8,128)(2,1)S(1)}, u32[]{:S(2)}, u32[]{:S(2)}) async-start(bf16[8,128,512]{2,1,0:T(8,128)(2,1)} %get-tuple-element.178), calls=%async_computation | async-start | bytes 2097152 | tf_op jit(solution)/shard_map/all_to_all | solution.py:272
  27.4 2.1 collective-permute-start.6
  31.0 2.6 collective-permute-start.9
  35.4 16.4 %collective-permute-done.10 = f32[4,4096]{1,0:T(4,128)S(1)} collective-permute-done((f32[4,4096]{1,0:T(4,128)}, f32[4,4096]{1,0:T(4,128)S(1)}, u32[]{:S(2)}, u32[]{:S(2)}) %collective-permute-start.10) | collective-permute-done | bytes 65568 | tf_op jit(solution)/shard_map/ppermute | solution.py:258
  53.3 4.7 %collective-permute-start.11 = (f32[4,4096]{1,0:T(4,128)}, f32[4,4096]{1,0:T(4,128)}, u32[]{:S(2)}, u32[]{:S(2)}) collective-permute-start(f32[4,4096]{1,0:T(4,128)} %add.152), channel_id=1, source_target_pairs={{0,8},{1,9},{2,10},{3,11},{4,12},{5,13},{6,14},{7,15},{8,0},{9,1},... | collective-permute-start | bytes 196616 | tf_op jit(solution)/shard_map/ppermute | solution.py:258
  58.0 2.6 collective-permute-done.11
  63.3 1.8 collective-permute-start.12
  66.8 2.0 collective-permute-start.14
  69.3 15.0 %collective-permute-done.15 = bf16[48,4096]{1,0:T(8,128)(2,1)S(1)} collective-permute-done((bf16[48,4096]{1,0:T(8,128)(2,1)S(1)}, bf16[48,4096]{1,0:T(8,128)(2,1)S(1)}, u32[]{:S(2)}, u32[]{:S(2)}) %collective-permute-start.15) | collective-permute-done | bytes 393248 | tf_op jit(solution)/shard_map/ppermute | solution.py:264
  89.0 2.0 collective-permute-start.20
  93.8 5.8 %collective-permute-done.17.refs_3_ = bf16[128,768]{1,0:T(8,128)(2,1)S(1)} collective-permute-done((bf16[128,768]{1,0:T(8,128)(2,1)S(1)}, bf16[128,768]{1,0:T(8,128)(2,1)S(1)}, u32[]{:S(2)}, u32[]{:S(2)}) %collective-permute-start.17) | collective-permute-done | bytes 196640 | tf_op jit(solution)/shard_map/ppermute | solution.py:258
  99.6 3.8 %collective-permute-done.20 = bf16[32,4096]{1,0:T(8,128)(2,1)S(1)} collective-permute-done((bf16[32,4096]{1,0:T(8,128)(2,1)S(1)}, bf16[32,4096]{1,0:T(8,128)(2,1)S(1)}, u32[]{:S(2)}, u32[]{:S(2)}) %collective-permute-start.20) | collective-permute-done | bytes 262176 | tf_op jit(solution)/shard_map/ppermute | solution.py:264
  103.4 2.3 multiply_convert_fusion
  109.6 3.4 %collective-permute-start.24 = (bf16[128,1024]{1,0:T(8,128)(2,1)S(1)}, bf16[128,1024]{1,0:T(8,128)(2,1)S(1)}, u32[]{:S(2)}, u32[]{:S(2)}) collective-permute-start(bf16[128,1024]{1,0:T(8,128)(2,1)S(1)} %slice.159), channel_id=1, source_target_pairs={{0,16},{1,17},{2,18},{3,19},{4,20},{5,21},{6,22},{7,23},{8,24},{9,... | collective-permute-start | bytes 786440 | tf_op jit(solution)/shard_map/ppermute | solution.py:264
  113.1 3.2 collective-permute-done.23.refs_5_
  116.3 6.3 %collective-permute-done.24 = bf16[128,1024]{1,0:T(8,128)(2,1)S(1)} collective-permute-done((bf16[128,1024]{1,0:T(8,128)(2,1)S(1)}, bf16[128,1024]{1,0:T(8,128)(2,1)S(1)}, u32[]{:S(2)}, u32[]{:S(2)}) %collective-permute-start.24) | collective-permute-done | bytes 262176 | tf_op jit(solution)/shard_map/ppermute | solution.py:264
  122.5 1.8 collective-permute-done.22.refs_4_
  124.4 1.7 collective-permute-start.25
  126.7 2.1 collective-permute-start.27
  128.9 1.8 collective-permute-start.28
  131.9 2.3 pad_maximum_fusion.rows_ref
  134.1 13.7 %collective-permute-done.29 = f32[1,512]{1,0:T(1,128)S(1)} collective-permute-done((f32[1,512]{1,0:T(1,128)S(1)}, f32[1,512]{1,0:T(1,128)S(1)}, u32[]{:S(2)}, u32[]{:S(2)}) %collective-permute-start.29) | collective-permute-done | bytes 2080 | tf_op jit(solution)/shard_map/ppermute | solution.py:264
  150.9 2.7 collective-permute-start.32
  155.4 16.4 %collective-permute-done.32 = bf16[192,1024]{1,0:T(8,128)(2,1)S(1)} collective-permute-done((bf16[192,1024]{1,0:T(8,128)(2,1)S(1)}, bf16[192,1024]{1,0:T(8,128)(2,1)S(1)}, u32[]{:S(2)}, u32[]{:S(2)}) %collective-permute-start.32) | collective-permute-done | bytes 393248 | tf_op jit(solution)/shard_map/ppermute | solution.py:264
  171.8 3.3 fusion.2
  178.7 2.9 collective-permute-start.36
  182.4 2.6 collective-permute-done.35.refs_5_
  185.0 6.0 %collective-permute-done.36 = bf16[128,1024]{1,0:T(8,128)(2,1)S(1)} collective-permute-done((bf16[128,1024]{1,0:T(8,128)(2,1)S(1)}, bf16[128,1024]{1,0:T(8,128)(2,1)S(1)}, u32[]{:S(2)}, u32[]{:S(2)}) %collective-permute-start.36) | collective-permute-done | bytes 262176 | tf_op jit(solution)/shard_map/ppermute | solution.py:264
  191.0 2.2 collective-permute-done.33.refs_3_
  196.8 1.8 collective-permute-start.42
  199.9 3.7 %fusion.53 = f32[1024,512]{1,0:T(8,128)} fusion(bf16[1024,2048]{1,0:T(8,128)(2,1)S(1)} %shard_map.56, bf16[512,2048]{1,0:T(8,128)(2,1)S(1)} %pad_maximum_fusion.1), kind=kOutput, calls=%fused_computation.101 | convolution fusion | flops 2147483648 | bytes 8388608 | tf_op jit(solution)/shard_map/dot_general | solution.py:184
  203.5 24.1 %collective-permute-done.44 = bf16[128,1024]{1,0:T(8,128)(2,1)S(1)} collective-permute-done((bf16[128,1024]{1,0:T(8,128)(2,1)S(1)}, bf16[128,1024]{1,0:T(8,128)(2,1)S(1)}, u32[]{:S(2)}, u32[]{:S(2)}) %collective-permute-start.44) | collective-permute-done | bytes 262176 | tf_op jit(solution)/shard_map/ppermute | solution.py:264
  232.3 1.8 collective-permute-start.48
  235.4 32.6 %collective-permute-done.50 = bf16[128,1024]{1,0:T(8,128)(2,1)S(1)} collective-permute-done((bf16[128,1024]{1,0:T(8,128)(2,1)S(1)}, bf16[128,1024]{1,0:T(8,128)(2,1)S(1)}, u32[]{:S(2)}, u32[]{:S(2)}) %collective-permute-start.50) | collective-permute-done | bytes 262176 | tf_op jit(solution)/shard_map/ppermute | solution.py:264
  268.5 2.0 collective-permute-done.49
  270.7 3.4 collective-permute-start.53
  274.1 2.6 fusion.8
  276.8 10.8 %shard_map.59 = (f32[512,1024]{1,0:T(8,128)}, f32[2,1024]{1,0:T(2,128)S(1)}) custom-call(s32[1]{0:T(128)} %bitcast.k_ref, bf16[512,1024]{1,0:T(8,128)(2,1)S(1)} %pad_maximum_fusion.3.raw_ref, f32[1,1024]{1,0:T(1,128)S(1)} %slice.174.mean_ref, f32[1,1024]{1,0:T(1,128)S(1)} %slice.175.inv_ref, bf16[512,4096]{1,0:T(8,128)(2,1)} %pad_maximum_fusion.rows_ref, ...), custom_call_target="tpu_custom_call" | custom-call | tf_op jit(solution)/shard_map/pallas_call | solution.py:230
  289.6 3.3 fusion.44
  295.4 2.1 collective-permute-done.55
  298.1 1.7 collective-permute-done.58
  302.8 3.6 %all-to-all-start.1 = ((bf16[8,128,512]{2,1,0:T(8,128)(2,1)}), bf16[8,128,512]{2,1,0:T(8,128)(2,1)S(1)}, u32[]{:S(2)}, u32[]{:S(2)}) async-start(bf16[8,128,512]{2,1,0:T(8,128)(2,1)} %shard_map.61), calls=%async_computation.1 | async-start | bytes 2097152 | tf_op jit(solution)/shard_map/all_to_all | solution.py:272
  306.4 2.2 multiply_convert_fusion.1
  308.7 1.9 collective-permute-done.59
  312.6 24.3 %collective-permute-done.60.refs_1_ = bf16[128,2048]{1,0:T(8,128)(2,1)S(1)} collective-permute-done((bf16[128,2048]{1,0:T(8,128)(2,1)S(1)}, bf16[128,2048]{1,0:T(8,128)(2,1)S(1)}, u32[]{:S(2)}, u32[]{:S(2)}) %collective-permute-start.60) | collective-permute-done | bytes 524320 | tf_op jit(solution)/shard_map/ppermute | solution.py:264
  (215 shorter events, 71.5 us)
Async XLA Ops:
  6.8 6.5 %collective-permute-start.4 = (f32[4,4096]{1,0:T(4,128)S(1)}, f32[4,4096]{1,0:T(4,128)S(1)}, u32[]{:S(2)}, u32[]{:S(2)}) collective-permute-start(f32[4,4096]{1,0:T(4,128)S(1)} %add.149), channel_id=1, source_target_pairs={{0,2},{1,3},{2,0},{3,1},{4,6},{5,7},{6,4},{7,5},{8,10},{9,11},{10,... | collective-permute-start | bytes 196616 | tf_op jit(solution)/shard_map/ppermute | solution.py:258
  9.7 8.9 %collective-permute-start = (bf16[128,768]{1,0:T(8,128)(2,1)S(1)}, bf16[128,768]{1,0:T(8,128)(2,1)S(1)}, u32[]{:S(2)}, u32[]{:S(2)}) collective-permute-start(bf16[128,768]{1,0:T(8,128)(2,1)S(1)} %get-tuple-element.165.refs_0_), channel_id=1, source_target_pairs={{0,8},{1,9},{2,10},{3,11},{4,12},{5,13},{6,14},{7,15},{8,0},{9,1},... | collective-permute-start | bytes 589832 | tf_op jit(solution)/shard_map/ppermute | solution.py:258
  11.3 7.3 %collective-permute-start.1 = (bf16[128,768]{1,0:T(8,128)(2,1)S(1)}, bf16[128,768]{1,0:T(8,128)(2,1)S(1)}, u32[]{:S(2)}, u32[]{:S(2)}) collective-permute-start(bf16[128,768]{1,0:T(8,128)(2,1)S(1)} %get-tuple-element.166.refs_1_), channel_id=1, source_target_pairs={{0,2},{1,3},{2,0},{3,1},{4,6},{5,7},{6,4},{7,5},{8,10},{9,11},{10,... | collective-permute-start | bytes 589832 | tf_op jit(solution)/shard_map/ppermute | solution.py:258
  11.8 6.8 %collective-permute-start.2 = (bf16[128,512]{1,0:T(8,128)(2,1)S(1)}, bf16[128,512]{1,0:T(8,128)(2,1)S(1)}, u32[]{:S(2)}, u32[]{:S(2)}) collective-permute-start(bf16[128,512]{1,0:T(8,128)(2,1)S(1)} %get-tuple-element.167.refs_2_), channel_id=1, source_target_pairs={{0,4},{1,5},{2,6},{3,7},{4,0},{5,1},{6,2},{7,3},{8,12},{9,13},{10,... | collective-permute-start | bytes 393224 | tf_op jit(solution)/shard_map/ppermute | solution.py:258
  19.4 42.7 %all-to-all-start = ((bf16[8,128,512]{2,1,0:T(8,128)(2,1)}), bf16[8,128,512]{2,1,0:T(8,128)(2,1)S(1)}, u32[]{:S(2)}, u32[]{:S(2)}) async-start(bf16[8,128,512]{2,1,0:T(8,128)(2,1)} %get-tuple-element.178), calls=%async_computation | async-start | bytes 2097152 | tf_op jit(solution)/shard_map/all_to_all | solution.py:272
  27.4 34.6 %collective-permute-start.6 = (bf16[256,768]{1,0:T(8,128)(2,1)S(1)}, bf16[256,768]{1,0:T(8,128)(2,1)S(1)}, u32[]{:S(2)}, u32[]{:S(2)}) collective-permute-start(bf16[256,768]{1,0:T(8,128)(2,1)S(1)} %get-tuple-element.179.refs_0_), channel_id=1, source_target_pairs={{0,4},{1,5},{2,6},{3,7},{4,0},{5,1},{6,2},{7,3},{8,12},{9,13},{10,... | collective-permute-start | bytes 1179656 | tf_op jit(solution)/shard_map/ppermute | solution.py:258
  29.5 32.5 %collective-permute-start.7 = (bf16[256,768]{1,0:T(8,128)(2,1)S(1)}, bf16[256,768]{1,0:T(8,128)(2,1)}, u32[]{:S(2)}, u32[]{:S(2)}) collective-permute-start(bf16[256,768]{1,0:T(8,128)(2,1)S(1)} %get-tuple-element.180.refs_1_), channel_id=1, source_target_pairs={{0,8},{1,9},{2,10},{3,11},{4,12},{5,13},{6,14},{7,15},{8,0},{9,1},... | collective-permute-start | bytes 1179656 | tf_op jit(solution)/shard_map/ppermute | solution.py:258
  31.0 31.1 %collective-permute-start.9 = (bf16[48,4096]{1,0:T(8,128)(2,1)}, bf16[48,4096]{1,0:T(8,128)(2,1)}, u32[]{:S(2)}, u32[]{:S(2)}) collective-permute-start(bf16[48,4096]{1,0:T(8,128)(2,1)} %get-tuple-element.174), channel_id=1, source_target_pairs={{0,16},{1,17},{2,18},{3,19},{4,20},{5,21},{6,22},{7,23},{8,24},{9,... | collective-permute-start | bytes 1179656 | tf_op jit(solution)/shard_map/ppermute | solution.py:264
  33.6 28.5 %collective-permute-start.8 = (bf16[256,512]{1,0:T(8,128)(2,1)S(1)}, bf16[256,512]{1,0:T(8,128)(2,1)}, u32[]{:S(2)}, u32[]{:S(2)}) collective-permute-start(bf16[256,512]{1,0:T(8,128)(2,1)S(1)} %get-tuple-element.181.refs_2_), channel_id=1, source_target_pairs={{0,2},{1,3},{2,0},{3,1},{4,6},{5,7},{6,4},{7,5},{8,10},{9,11},{10,... | collective-permute-start | bytes 786440 | tf_op jit(solution)/shard_map/ppermute | solution.py:258
  35.0 16.8 %collective-permute-start.10 = (f32[4,4096]{1,0:T(4,128)}, f32[4,4096]{1,0:T(4,128)S(1)}, u32[]{:S(2)}, u32[]{:S(2)}) collective-permute-start(f32[4,4096]{1,0:T(4,128)} %add.151), channel_id=1, source_target_pairs={{0,16},{1,17},{2,18},{3,19},{4,20},{5,21},{6,22},{7,23},{8,24},{9,... | collective-permute-start | bytes 196616 | tf_op jit(solution)/shard_map/ppermute | solution.py:258
  53.3 7.2 %collective-permute-start.11 = (f32[4,4096]{1,0:T(4,128)}, f32[4,4096]{1,0:T(4,128)}, u32[]{:S(2)}, u32[]{:S(2)}) collective-permute-start(f32[4,4096]{1,0:T(4,128)} %add.152), channel_id=1, source_target_pairs={{0,8},{1,9},{2,10},{3,11},{4,12},{5,13},{6,14},{7,15},{8,0},{9,1},... | collective-permute-start | bytes 196616 | tf_op jit(solution)/shard_map/ppermute | solution.py:258
  63.3 21.7 %collective-permute-start.12 = (bf16[512,768]{1,0:T(8,128)(2,1)S(1)}, bf16[512,768]{1,0:T(8,128)(2,1)S(1)}, u32[]{:S(2)}, u32[]{:S(2)}) collective-permute-start(bf16[512,768]{1,0:T(8,128)(2,1)S(1)} %get-tuple-element.198.refs_0_), channel_id=1, source_target_pairs={{0,2},{1,3},{2,0},{3,1},{4,6},{5,7},{6,4},{7,5},{8,10},{9,11},{10,... | collective-permute-start | bytes 2359304 | tf_op jit(solution)/shard_map/ppermute | solution.py:258
  65.2 19.9 %collective-permute-start.13 = (bf16[512,768]{1,0:T(8,128)(2,1)S(1)}, bf16[512,768]{1,0:T(8,128)(2,1)S(1)}, u32[]{:S(2)}, u32[]{:S(2)}) collective-permute-start(bf16[512,768]{1,0:T(8,128)(2,1)S(1)} %get-tuple-element.200.refs_2_), channel_id=1, source_target_pairs={{0,4},{1,5},{2,6},{3,7},{4,0},{5,1},{6,2},{7,3},{8,12},{9,13},{10,... | collective-permute-start | bytes 2359304 | tf_op jit(solution)/shard_map/ppermute | solution.py:258
  66.8 18.2 %collective-permute-start.14 = (bf16[512,512]{1,0:T(8,128)(2,1)S(1)}, bf16[512,512]{1,0:T(8,128)(2,1)S(1)}, u32[]{:S(2)}, u32[]{:S(2)}) collective-permute-start(bf16[512,512]{1,0:T(8,128)(2,1)S(1)} %get-tuple-element.202.refs_4_), channel_id=1, source_target_pairs={{0,8},{1,9},{2,10},{3,11},{4,12},{5,13},{6,14},{7,15},{8,0},{9,1},... | collective-permute-start | bytes 1572872 | tf_op jit(solution)/shard_map/ppermute | solution.py:258
  68.8 15.5 %collective-permute-start.15 = (bf16[48,4096]{1,0:T(8,128)(2,1)S(1)}, bf16[48,4096]{1,0:T(8,128)(2,1)S(1)}, u32[]{:S(2)}, u32[]{:S(2)}) collective-permute-start(bf16[48,4096]{1,0:T(8,128)(2,1)S(1)} %copy-done.20), channel_id=1, source_target_pairs={{0,16},{1,17},{2,18},{3,19},{4,20},{5,21},{6,22},{7,23},{8,24},{9,... | collective-permute-start | bytes 1179656 | tf_op jit(solution)/shard_map/ppermute | solution.py:264
  87.4 12.1 %collective-permute-start.17 = (bf16[128,768]{1,0:T(8,128)(2,1)S(1)}, bf16[128,768]{1,0:T(8,128)(2,1)S(1)}, u32[]{:S(2)}, u32[]{:S(2)}) collective-permute-start(bf16[128,768]{1,0:T(8,128)(2,1)S(1)} %copy-done.5), channel_id=1, source_target_pairs={{0,8},{1,9},{2,10},{3,11},{4,12},{5,13},{6,14},{7,15},{8,0},{9,1},... | collective-permute-start | bytes 589832 | tf_op jit(solution)/shard_map/ppermute | solution.py:258
  88.1 11.5 %collective-permute-start.18 = (bf16[128,768]{1,0:T(8,128)(2,1)S(1)}, bf16[128,768]{1,0:T(8,128)(2,1)S(1)}, u32[]{:S(2)}, u32[]{:S(2)}) collective-permute-start(bf16[128,768]{1,0:T(8,128)(2,1)S(1)} %copy-done.7), channel_id=1, source_target_pairs={{0,2},{1,3},{2,0},{3,1},{4,6},{5,7},{6,4},{7,5},{8,10},{9,11},{10,... | collective-permute-start | bytes 589832 | tf_op jit(solution)/shard_map/ppermute | solution.py:258
  89.0 14.4 %collective-permute-start.20 = (bf16[32,4096]{1,0:T(8,128)(2,1)S(1)}, bf16[32,4096]{1,0:T(8,128)(2,1)S(1)}, u32[]{:S(2)}, u32[]{:S(2)}) collective-permute-start(bf16[32,4096]{1,0:T(8,128)(2,1)S(1)} %copy-done.22), channel_id=1, source_target_pairs={{0,16},{1,17},{2,18},{3,19},{4,20},{5,21},{6,22},{7,23},{8,24},{9,... | collective-permute-start | bytes 786440 | tf_op jit(solution)/shard_map/ppermute | solution.py:264
  105.8 24.9 %collective-permute-start.30 = (bf16[256,4096]{1,0:T(8,128)(2,1)S(1)}, bf16[256,4096]{1,0:T(8,128)(2,1)S(1)}, u32[]{:S(2)}, u32[]{:S(2)}) collective-permute-start(bf16[256,4096]{1,0:T(8,128)(2,1)S(1)} %multiply_convert_fusion), channel_id=1, source_target_pairs={{0,1},{1,0},{2,3},{3,2},{4,5},{5,4},{6,7},{7,6},{8,9},{9,8},{10,11... | collective-permute-start | bytes 6291464 | tf_op jit(solution)/shard_map/ppermute | solution.py:258
  105.9 16.6 %collective-permute-start.21 = (bf16[256,768]{1,0:T(8,128)(2,1)S(1)}, bf16[256,768]{1,0:T(8,128)(2,1)S(1)}, u32[]{:S(2)}, u32[]{:S(2)}) collective-permute-start(bf16[256,768]{1,0:T(8,128)(2,1)S(1)} %get-tuple-element.221.refs_0_), channel_id=1, source_target_pairs={{0,4},{1,5},{2,6},{3,7},{4,0},{5,1},{6,2},{7,3},{8,12},{9,13},{10,... | collective-permute-start | bytes 1179656 | tf_op jit(solution)/shard_map/ppermute | solution.py:258
  107.4 16.8 %collective-permute-start.22 = (bf16[256,768]{1,0:T(8,128)(2,1)S(1)}, bf16[256,768]{1,0:T(8,128)(2,1)S(1)}, u32[]{:S(2)}, u32[]{:S(2)}) collective-permute-start(bf16[256,768]{1,0:T(8,128)(2,1)S(1)} %get-tuple-element.222.refs_1_), channel_id=1, source_target_pairs={{0,8},{1,9},{2,10},{3,11},{4,12},{5,13},{6,14},{7,15},{8,0},{9,1},... | collective-permute-start | bytes 1179656 | tf_op jit(solution)/shard_map/ppermute | solution.py:258
  108.1 8.1 %collective-permute-start.23 = (bf16[256,512]{1,0:T(8,128)(2,1)S(1)}, bf16[256,512]{1,0:T(8,128)(2,1)S(1)}, u32[]{:S(2)}, u32[]{:S(2)}) collective-permute-start(bf16[256,512]{1,0:T(8,128)(2,1)S(1)} %get-tuple-element.223.refs_2_), channel_id=1, source_target_pairs={{0,2},{1,3},{2,0},{3,1},{4,6},{5,7},{6,4},{7,5},{8,10},{9,11},{10,... | collective-permute-start | bytes 786440 | tf_op jit(solution)/shard_map/ppermute | solution.py:258
  109.6 12.9 %collective-permute-start.24 = (bf16[128,1024]{1,0:T(8,128)(2,1)S(1)}, bf16[128,1024]{1,0:T(8,128)(2,1)S(1)}, u32[]{:S(2)}, u32[]{:S(2)}) collective-permute-start(bf16[128,1024]{1,0:T(8,128)(2,1)S(1)} %slice.159), channel_id=1, source_target_pairs={{0,16},{1,17},{2,18},{3,19},{4,20},{5,21},{6,22},{7,23},{8,24},{9,... | collective-permute-start | bytes 786440 | tf_op jit(solution)/shard_map/ppermute | solution.py:264
  124.4 24.1 %collective-permute-start.25 = (bf16[512,768]{1,0:T(8,128)(2,1)S(1)}, bf16[512,768]{1,0:T(8,128)(2,1)S(1)}, u32[]{:S(2)}, u32[]{:S(2)}) collective-permute-start(bf16[512,768]{1,0:T(8,128)(2,1)S(1)} %get-tuple-element.236.refs_0_), channel_id=1, source_target_pairs={{0,2},{1,3},{2,0},{3,1},{4,6},{5,7},{6,4},{7,5},{8,10},{9,11},{10,... | collective-permute-start | bytes 2359304 | tf_op jit(solution)/shard_map/ppermute | solution.py:258
  126.2 22.4 %collective-permute-start.26 = (bf16[512,768]{1,0:T(8,128)(2,1)S(1)}, bf16[512,768]{1,0:T(8,128)(2,1)S(1)}, u32[]{:S(2)}, u32[]{:S(2)}) collective-permute-start(bf16[512,768]{1,0:T(8,128)(2,1)S(1)} %get-tuple-element.238.refs_2_), channel_id=1, source_target_pairs={{0,4},{1,5},{2,6},{3,7},{4,0},{5,1},{6,2},{7,3},{8,12},{9,13},{10,... | collective-permute-start | bytes 2359304 | tf_op jit(solution)/shard_map/ppermute | solution.py:258
  126.7 21.8 %collective-permute-start.27 = (bf16[512,512]{1,0:T(8,128)(2,1)S(1)}, bf16[512,512]{1,0:T(8,128)(2,1)S(1)}, u32[]{:S(2)}, u32[]{:S(2)}) collective-permute-start(bf16[512,512]{1,0:T(8,128)(2,1)S(1)} %get-tuple-element.240.refs_4_), channel_id=1, source_target_pairs={{0,8},{1,9},{2,10},{3,11},{4,12},{5,13},{6,14},{7,15},{8,0},{9,1},... | collective-permute-start | bytes 1572872 | tf_op jit(solution)/shard_map/ppermute | solution.py:258
  128.9 18.9 %collective-permute-start.28 = (bf16[192,1024]{1,0:T(8,128)(2,1)S(1)}, bf16[192,1024]{1,0:T(8,128)(2,1)S(1)}, u32[]{:S(2)}, u32[]{:S(2)}) collective-permute-start(bf16[192,1024]{1,0:T(8,128)(2,1)S(1)} %slice.160), channel_id=1, source_target_pairs={{0,16},{1,17},{2,18},{3,19},{4,20},{5,21},{6,22},{7,23},{8,24},{9,... | collective-permute-start | bytes 1179656 | tf_op jit(solution)/shard_map/ppermute | solution.py:264
  130.7 17.1 %collective-permute-start.29 = (f32[1,512]{1,0:T(1,128)S(1)}, f32[1,512]{1,0:T(1,128)S(1)}, u32[]{:S(2)}, u32[]{:S(2)}) collective-permute-start(f32[1,512]{1,0:T(1,128)S(1)} %bitcast.71), channel_id=1, source_target_pairs={{0,16},{1,17},{2,18},{3,19},{4,20},{5,21},{6,22},{7,23},{8,24},{9,... | collective-permute-start | bytes 6152 | tf_op jit(solution)/shard_map/ppermute | solution.py:264
  150.9 20.9 %collective-permute-start.32 = (bf16[192,1024]{1,0:T(8,128)(2,1)S(1)}, bf16[192,1024]{1,0:T(8,128)(2,1)S(1)}, u32[]{:S(2)}, u32[]{:S(2)}) collective-permute-start(bf16[192,1024]{1,0:T(8,128)(2,1)S(1)} %slice.163), channel_id=1, source_target_pairs={{0,16},{1,17},{2,18},{3,19},{4,20},{5,21},{6,22},{7,23},{8,24},{9,... | collective-permute-start | bytes 1179656 | tf_op jit(solution)/shard_map/ppermute | solution.py:264
  175.1 7.1 %collective-permute-start.37 = (bf16[512,1024]{1,0:T(8,128)(2,1)S(1)}, bf16[512,1024]{1,0:T(8,128)(2,1)S(1)}, u32[]{:S(2)}, u32[]{:S(2)}) collective-permute-start(bf16[512,1024]{1,0:T(8,128)(2,1)S(1)} %get-tuple-element.278), channel_id=1, source_target_pairs={{0,1},{1,0},{2,3},{3,2},{4,5},{5,4},{6,7},{7,6},{8,9},{9,8},{10,11... | collective-permute-start | bytes 3145736 | tf_op jit(solution)/shard_map/ppermute | solution.py:258
  176.5 16.7 %collective-permute-start.33 = (bf16[512,384]{1,0:T(8,128)(2,1)S(1)}, bf16[512,384]{1,0:T(8,128)(2,1)S(1)}, u32[]{:S(2)}, u32[]{:S(2)}) collective-permute-start(bf16[512,384]{1,0:T(8,128)(2,1)S(1)} %get-tuple-element.252.refs_0_), channel_id=1, source_target_pairs={{0,8},{1,9},{2,10},{3,11},{4,12},{5,13},{6,14},{7,15},{8,0},{9,1},... | collective-permute-start | bytes 1179656 | tf_op jit(solution)/shard_map/ppermute | solution.py:258
  176.6 16.6 %collective-permute-start.34 = (bf16[512,384]{1,0:T(8,128)(2,1)S(1)}, bf16[512,384]{1,0:T(8,128)(2,1)S(1)}, u32[]{:S(2)}, u32[]{:S(2)}) collective-permute-start(bf16[512,384]{1,0:T(8,128)(2,1)S(1)} %get-tuple-element.253.refs_1_), channel_id=1, source_target_pairs={{0,2},{1,3},{2,0},{3,1},{4,6},{5,7},{6,4},{7,5},{8,10},{9,11},{10,... | collective-permute-start | bytes 1179656 | tf_op jit(solution)/shard_map/ppermute | solution.py:258
  177.1 8.0 %collective-permute-start.35 = (bf16[512,256]{1,0:T(8,128)(2,1)S(1)}, bf16[512,256]{1,0:T(8,128)(2,1)S(1)}, u32[]{:S(2)}, u32[]{:S(2)}) collective-permute-start(bf16[512,256]{1,0:T(8,128)(2,1)S(1)} %slice.204.refs_2_), channel_id=1, source_target_pairs={{0,4},{1,5},{2,6},{3,7},{4,0},{5,1},{6,2},{7,3},{8,12},{9,13},{10,... | collective-permute-start | bytes 786440 | tf_op jit(solution)/shard_map/ppermute | solution.py:258
  178.7 12.3 %collective-permute-start.36 = (bf16[128,1024]{1,0:T(8,128)(2,1)S(1)}, bf16[128,1024]{1,0:T(8,128)(2,1)S(1)}, u32[]{:S(2)}, u32[]{:S(2)}) collective-permute-start(bf16[128,1024]{1,0:T(8,128)(2,1)S(1)} %slice.205), channel_id=1, source_target_pairs={{0,16},{1,17},{2,18},{3,19},{4,20},{5,21},{6,22},{7,23},{8,24},{9,... | collective-permute-start | bytes 786440 | tf_op jit(solution)/shard_map/ppermute | solution.py:264
  193.4 34.2 %collective-permute-start.39 = (bf16[1024,384]{1,0:T(8,128)(2,1)S(1)}, bf16[1024,384]{1,0:T(8,128)(2,1)S(1)}, u32[]{:S(2)}, u32[]{:S(2)}) collective-permute-start(bf16[1024,384]{1,0:T(8,128)(2,1)S(1)} %get-tuple-element.267.refs_0_), channel_id=1, source_target_pairs={{0,4},{1,5},{2,6},{3,7},{4,0},{5,1},{6,2},{7,3},{8,12},{9,13},{10,... | collective-permute-start | bytes 2359304 | tf_op jit(solution)/shard_map/ppermute | solution.py:258
  195.0 33.7 %collective-permute-start.40 = (bf16[1024,384]{1,0:T(8,128)(2,1)S(1)}, bf16[1024,384]{1,0:T(8,128)(2,1)S(1)}, u32[]{:S(2)}, u32[]{:S(2)}) collective-permute-start(bf16[1024,384]{1,0:T(8,128)(2,1)S(1)} %get-tuple-element.268.refs_1_), channel_id=1, source_target_pairs={{0,8},{1,9},{2,10},{3,11},{4,12},{5,13},{6,14},{7,15},{8,0},{9,1},... | collective-permute-start | bytes 2359304 | tf_op jit(solution)/shard_map/ppermute | solution.py:258
  196.4 31.2 %collective-permute-start.41 = (bf16[1024,256]{1,0:T(8,128)(2,1)S(1)}, bf16[1024,256]{1,0:T(8,128)(2,1)S(1)}, u32[]{:S(2)}, u32[]{:S(2)}) collective-permute-start(bf16[1024,256]{1,0:T(8,128)(2,1)S(1)} %get-tuple-element.269.refs_2_), channel_id=1, source_target_pairs={{0,2},{1,3},{2,0},{3,1},{4,6},{5,7},{6,4},{7,5},{8,10},{9,11},{10,... | collective-permute-start | bytes 1572872 | tf_op jit(solution)/shard_map/ppermute | solution.py:258
  196.8 30.8 %collective-permute-start.42 = (bf16[192,1024]{1,0:T(8,128)(2,1)S(1)}, bf16[192,1024]{1,0:T(8,128)(2,1)S(1)}, u32[]{:S(2)}, u32[]{:S(2)}) collective-permute-start(bf16[192,1024]{1,0:T(8,128)(2,1)S(1)} %slice.168), channel_id=1, source_target_pairs={{0,16},{1,17},{2,18},{3,19},{4,20},{5,21},{6,22},{7,23},{8,24},{9,... | collective-permute-start | bytes 1179656 | tf_op jit(solution)/shard_map/ppermute | solution.py:264
  198.6 29.0 %collective-permute-start.44 = (bf16[128,1024]{1,0:T(8,128)(2,1)S(1)}, bf16[128,1024]{1,0:T(8,128)(2,1)S(1)}, u32[]{:S(2)}, u32[]{:S(2)}) collective-permute-start(bf16[128,1024]{1,0:T(8,128)(2,1)S(1)} %slice.169), channel_id=1, source_target_pairs={{0,16},{1,17},{2,18},{3,19},{4,20},{5,21},{6,22},{7,23},{8,24},{9,... | collective-permute-start | bytes 786440 | tf_op jit(solution)/shard_map/ppermute | solution.py:264
  229.0 41.5 %collective-permute-start.45 = (bf16[2048,384]{1,0:T(8,128)(2,1)S(1)}, bf16[2048,384]{1,0:T(8,128)(2,1)S(1)}, u32[]{:S(2)}, u32[]{:S(2)}) collective-permute-start(bf16[2048,384]{1,0:T(8,128)(2,1)S(1)} %get-tuple-element.286.refs_0_), channel_id=1, source_target_pairs={{0,2},{1,3},{2,0},{3,1},{4,6},{5,7},{6,4},{7,5},{8,10},{9,11},{10,... | collective-permute-start | bytes 4718600 | tf_op jit(solution)/shard_map/ppermute | solution.py:258
  229.7 40.9 %collective-permute-start.46 = (bf16[2048,384]{1,0:T(8,128)(2,1)S(1)}, bf16[2048,384]{1,0:T(8,128)(2,1)S(1)}, u32[]{:S(2)}, u32[]{:S(2)}) collective-permute-start(bf16[2048,384]{1,0:T(8,128)(2,1)S(1)} %get-tuple-element.288.refs_2_), channel_id=1, source_target_pairs={{0,4},{1,5},{2,6},{3,7},{4,0},{5,1},{6,2},{7,3},{8,12},{9,13},{10,... | collective-permute-start | bytes 4718600 | tf_op jit(solution)/shard_map/ppermute | solution.py:258
  231.0 39.5 %collective-permute-start.47 = (bf16[2048,256]{1,0:T(8,128)(2,1)S(1)}, bf16[2048,256]{1,0:T(8,128)(2,1)S(1)}, u32[]{:S(2)}, u32[]{:S(2)}) collective-permute-start(bf16[2048,256]{1,0:T(8,128)(2,1)S(1)} %get-tuple-element.290.refs_4_), channel_id=1, source_target_pairs={{0,8},{1,9},{2,10},{3,11},{4,12},{5,13},{6,14},{7,15},{8,0},{9,1},... | collective-permute-start | bytes 3145736 | tf_op jit(solution)/shard_map/ppermute | solution.py:258
  232.3 35.8 %collective-permute-start.48 = (bf16[192,1024]{1,0:T(8,128)(2,1)S(1)}, bf16[192,1024]{1,0:T(8,128)(2,1)S(1)}, u32[]{:S(2)}, u32[]{:S(2)}) collective-permute-start(bf16[192,1024]{1,0:T(8,128)(2,1)S(1)} %slice.171), channel_id=1, source_target_pairs={{0,16},{1,17},{2,18},{3,19},{4,20},{5,21},{6,22},{7,23},{8,24},{9,... | collective-permute-start | bytes 1179656 | tf_op jit(solution)/shard_map/ppermute | solution.py:264
  234.1 34.0 %collective-permute-start.50 = (bf16[128,1024]{1,0:T(8,128)(2,1)S(1)}, bf16[128,1024]{1,0:T(8,128)(2,1)S(1)}, u32[]{:S(2)}, u32[]{:S(2)}) collective-permute-start(bf16[128,1024]{1,0:T(8,128)(2,1)S(1)} %slice.172), channel_id=1, source_target_pairs={{0,16},{1,17},{2,18},{3,19},{4,20},{5,21},{6,22},{7,23},{8,24},{9,... | collective-permute-start | bytes 786440 | tf_op jit(solution)/shard_map/ppermute | solution.py:264
  270.5 17.1 %collective-permute-start.52 = (bf16[192,1024]{1,0:T(8,128)(2,1)S(1)}, bf16[192,1024]{1,0:T(8,128)(2,1)S(1)}, u32[]{:S(2)}, u32[]{:S(2)}) collective-permute-start(bf16[192,1024]{1,0:T(8,128)(2,1)S(1)} %collective-permute-done.48), channel_id=1, source_target_pairs={{0,1},{1,0},{2,3},{3,2},{4,5},{5,4},{6,7},{7,6},{8,9},{9,8},{10,11... | collective-permute-start | bytes 1179656 | tf_op jit(solution)/shard_map/ppermute | solution.py:258
  270.7 16.9 %collective-permute-start.53 = (f32[8,128]{1,0:T(8,128)S(1)}, f32[8,128]{1,0:T(8,128)S(1)}, u32[]{:S(2)}, u32[]{:S(2)}) collective-permute-start(f32[8,128]{1,0:T(8,128)S(1)} %broadcast_add_fusion), channel_id=1, source_target_pairs={{0,16},{1,17},{2,18},{3,19},{4,20},{5,21},{6,22},{7,23},{8,24},{9,... | collective-permute-start | bytes 12296 | tf_op jit(solution)/shard_map/ppermute | solution.py:258
  302.8 35.7 %all-to-all-start.1 = ((bf16[8,128,512]{2,1,0:T(8,128)(2,1)}), bf16[8,128,512]{2,1,0:T(8,128)(2,1)S(1)}, u32[]{:S(2)}, u32[]{:S(2)}) async-start(bf16[8,128,512]{2,1,0:T(8,128)(2,1)} %shard_map.61), calls=%async_computation.1 | async-start | bytes 2097152 | tf_op jit(solution)/shard_map/all_to_all | solution.py:272
  310.7 26.2 %collective-permute-start.60 = (bf16[128,2048]{1,0:T(8,128)(2,1)S(1)}, bf16[128,2048]{1,0:T(8,128)(2,1)S(1)}, u32[]{:S(2)}, u32[]{:S(2)}) collective-permute-start(bf16[128,2048]{1,0:T(8,128)(2,1)S(1)} %get-tuple-element.317), channel_id=1, source_target_pairs={{0,16},{1,17},{2,18},{3,19},{4,20},{5,21},{6,22},{7,23},{8,24},{9,... | collective-permute-start | bytes 1572872 | tf_op jit(solution)/shard_map/ppermute | solution.py:264
  (40 other events, 219.6 us)

commit v4 on v3

--- a/solution.py
+++ b/solution.py
@@ -1,4 +1,5 @@
 import functools
+import math
 
 import jax
 import jax.numpy as jnp
@@ -15,7 +16,11 @@
 together = lax.optimization_barrier
 vmem = pl.BlockSpec(memory_space=pltpu.VMEM)
 smem = pl.BlockSpec(memory_space=pltpu.SMEM)
-roomy = pltpu.CompilerParams(vmem_limit_bytes=32 << 20)
+
+
+def room(*arrays):
+    sizes = [math.prod(x.shape) * x.dtype.itemsize for x in arrays]
+    return pltpu.CompilerParams(vmem_limit_bytes=sum(sizes) + max(sizes) + (4 << 20))
 
 
 def places(order):
@@ -66,7 +71,7 @@
         out_shape=outs,
         in_specs=[smem, vmem, vmem],
         out_specs=[vmem] * len(outs),
-        compiler_params=roomy,
+        compiler_params=room(view_a, view_b, *outs),
     )(at, view_a, view_b)
     first = len(cuts(widths[0]))
     return near, rest, eighths, sums, parts[:first], parts[first:]
@@ -86,7 +91,7 @@
         out_shape=[jax.ShapeDtypeStruct((2 * x.shape[0], x.shape[1]), x.dtype) for x in xs],
         in_specs=[vmem] * (2 * len(xs)),
         out_specs=[vmem] * len(xs),
-        compiler_params=roomy,
+        compiler_params=room(*xs, *ys, *xs, *ys),
     )(*xs, *ys)
 
 
@@ -113,7 +118,7 @@
         out_shape=jax.ShapeDtypeStruct((2 * pieces[0].shape[0], mean.shape[1]), jnp.bfloat16),
         in_specs=[vmem] * (2 + len(pieces)),
         out_specs=vmem,
-        compiler_params=roomy,
+        compiler_params=room(*pieces, *pieces),
     )(mean, inv, *pieces)
 
 
@@ -135,7 +140,7 @@
         out_shape=(out, out),
         in_specs=[smem] + [vmem] * 3,
         out_specs=(vmem, vmem),
-        compiler_params=roomy,
+        compiler_params=room(blocks, out, out),
     )(k.reshape(1), blocks, mean, inv)
 
 
@@ -156,7 +161,7 @@
         out_shape=jax.ShapeDtypeStruct((cube, size // cube, n), jnp.bfloat16),
         in_specs=[smem] + [vmem] * 6,
         out_specs=vmem,
-        compiler_params=roomy,
+        compiler_params=room(grad, raw, raw),
     )(k.reshape(1), grad, raw, mean, inv, first, second)
 
 
@@ -176,7 +181,7 @@
         out_shape=jax.ShapeDtypeStruct((rows, n * len(blocks)), jnp.bfloat16),
         in_specs=[smem] + [vmem] * len(blocks),
         out_specs=vmem,
-        compiler_params=roomy,
+        compiler_params=room(*blocks, *blocks),
     )(at, *blocks)
 
 
@@ -184,41 +189,34 @@
     return lax.dot_general(x, y, (contract, ((), ())), preferred_element_type=jnp.float32)
 
 
-def cross_kernel(orders, k_ref, raw_ref, mean_ref, inv_ref, rows_ref, *refs):
-    pieces, (out_ref, sums_ref) = refs[:-2], refs[-2:]
+def cross_kernel(side, orders, k_ref, rows_ref, *refs):
+    if side == 0:
+        pieces, out_ref = refs[:-1], refs[-1]
+    else:
+        total_ref, raw_ref, mean_ref, inv_ref, *pieces, out_ref, sums_ref = refs
     narrow = rows_ref.shape[1] // cube
     start = 0
-    for n, order in enumerate(orders[: len(pieces) // 2]):
-        size = pieces[2 * n].shape[1]
-        total = 0.0
-        for m, r in enumerate(places(order)):
-            piece = pieces[2 * n + 2 * m // cube]
-            first = m % (cube // 2) * narrow
+    for order, piece in zip(orders, pieces):
+        here = slice(start, start + piece.shape[1])
+        start += piece.shape[1]
+        total = 0.0 if side == 0 else total_ref[:, here]
+        for m in range(cube // 2):
+            r = places(order)[side * cube // 2 + m]
             at = pl.multiple_of((k_ref[0] ^ r) * narrow, narrow)
             total = total + jnp.dot(
                 rows_ref[:, pl.ds(at, narrow)],
-                piece[first : first + narrow, :],
+                piece[m * narrow : (m + 1) * narrow, :],
                 preferred_element_type=jnp.float32,
             )
-        out_ref[:, start : start + size] = total
-        start += size
-    out = out_ref[...]
-    flat = (raw_ref[...].astype(jnp.float32) - mean_ref[...]) * inv_ref[...]
-    sums = jnp.concatenate(
-        [jnp.sum(out, axis=0, keepdims=True), jnp.sum(out * flat, axis=0, keepdims=True)]
-    )
-
-    @pl.when(pl.program_id(0) == 0)
-    def _():
-        sums_ref[...] = sums
-
-    @pl.when(pl.program_id(0) > 0)
-    def _():
-        sums_ref[...] += sums
-
-
-def cross_products(rows, pieces, orders, raw, mean, inv, k):
-    size, n = raw.shape
+        out_ref[:, here] = total
+        if side == 1:
+            flat = (raw_ref[:, here].astype(jnp.float32) - mean_ref[:, here]) * inv_ref[:, here]
+            sums_ref[0, 0:1, here] = jnp.sum(total, axis=0, keepdims=True)
+            sums_ref[0, 1:2, here] = jnp.sum(total * flat, axis=0, keepdims=True)
+
+
+def cross_products(side, rows, pieces, orders, k, *more):
+    size, n = rows.shape[0], sum(x.shape[1] for x in pieces)
     block = min(size, 512)
 
     def whole(x):
@@ -227,18 +225,17 @@
     def part(x):
         return pl.BlockSpec((block, x.shape[1]), lambda i: (i, 0))
 
-    return pl.pallas_call(
-        functools.partial(cross_kernel, orders),
+    out = jax.ShapeDtypeStruct((size, n), jnp.float32)
+    sums = jax.ShapeDtypeStruct((size // block, 2, n), jnp.float32)
+    specs = [part(x) if x.shape[0] == size else whole(x) for x in more]
+    return pl.pallas_call(
+        functools.partial(cross_kernel, side, orders),
         grid=(size // block,),
-        out_shape=(
-            jax.ShapeDtypeStruct((size, n), jnp.float32),
-            jax.ShapeDtypeStruct((2, n), jnp.float32),
-        ),
-        in_specs=[smem, part(raw), whole(mean), whole(inv), part(rows)]
-        + [whole(x) for x in pieces],
-        out_specs=(part(raw), pl.BlockSpec((2, n), lambda i: (0, 0))),
+        out_shape=(out, sums) if side else out,
+        in_specs=[smem, part(rows)] + specs + [whole(x) for x in pieces],
+        out_specs=(part(out), pl.BlockSpec((1, 2, n), lambda i: (i, 0, 0))) if side else part(out),
         compiler_params=pltpu.CompilerParams(vmem_limit_bytes=48 << 20),
-    )(k.reshape(1), raw, mean, inv, rows, *pieces)
+    )(k.reshape(1), rows, *more, *pieces)
 
 
 def shards(view_a, view_b):
@@ -288,28 +285,31 @@
 
     whole_near, whole_rest, eighths, sums, near, rest = prepare(view_a, view_b, jnp.stack(at), half)
     parts_a = [whole_near] + [whole_rest[:, s * wide : (s + 1) * wide] for s in range(cubes - 1)]
-    cuts_b = (0, 3 * rows // 8, 3 * rows // 4, rows)
+    cuts_b = (0, rows // 2, rows)
     pieces_b = [view_b[lo:hi] for lo, hi in zip(cuts_b, cuts_b[1:])]
     others_b = []
 
     arrived = send(rest, 0)
-    for mask in (1, 2, 4):
+
+    own_b = exchange(eighths)
+    far_1 = [turn(x[:, half:], s + 1) for s, x in enumerate(parts_a[1:])]
+    for mask in [1] + h_masks:
         sums = sums + swap(sums, mask)
-    rest, arrived, sums, pieces_b, near, eighths = together(
-        (rest, arrived, sums, pieces_b, near, eighths)
+    rest, arrived, sums, pieces_b, near, parts_a, far_1 = together(
+        (rest, arrived, sums, pieces_b, near, parts_a, far_1)
     )
     rest = double(rest, arrived)
     arrived = send(rest, 1)
-    own_b = exchange(eighths)
     others_b.append(turns(pieces_b[0]))
-    for mask in h_masks + [8]:
+    for mask in (2, 4):
         sums = sums + swap(sums, mask)
-    rest, arrived, others_b, sums, pieces_b, own_b = together(
-        (rest, arrived, others_b, sums, pieces_b, own_b)
+    rest, arrived, others_b, sums, pieces_b, own_b, parts_a, far_1 = together(
+        (rest, arrived, others_b, sums, pieces_b, own_b, parts_a, far_1)
     )
     rest = double(rest, arrived)
     arrived = send(rest, 2)
     others_b.append(turns(pieces_b[1]))
+    sums = sums + swap(sums, 8)
     means = sums / count
     mean_a, mean_b = means[0:1], means[2:3]
     inv_a = 1.0 / jnp.sqrt(means[1:2] - mean_a * mean_a + eps)
@@ -318,8 +318,8 @@
     inv_bn = columns(inv_b, k * narrow, narrow)
     mean_ap, inv_ap = by_place(mean_a, at), by_place(inv_a, at)
     near_b, right = arrange(own_b, mean_bn, inv_bn, k)
-    rest, arrived, others_b, pieces_b, near_b, right, mean_ap, inv_ap = together(
-        (rest, arrived, others_b, pieces_b, near_b, right, mean_ap, inv_ap)
+    rest, arrived, others_b, near_b, right, mean_ap, inv_ap, parts_a, far_1 = together(
+        (rest, arrived, others_b, near_b, right, mean_ap, inv_ap, parts_a, far_1)
     )
 
     def product(left, s):
@@ -333,7 +333,6 @@
         )
 
     rest = merge(rest, arrived, orders, mean_ap[:, wide:], inv_ap[:, wide:])
-    others_b.append(turns(pieces_b[2]))
     arrived = send(near, 0)
     partials = [product(rest, s) for s in range(cubes - 1)]
     exact = [
@@ -346,7 +345,7 @@
     )
     near = double(near, arrived)
 
-    cuts_p = (0, narrow // 4, 5 * narrow // 8, narrow)
+    cuts_p = (0, 3 * narrow // 8, 7 * narrow // 8, narrow)
     received = []
     for step in (1, 2):
         arrived = send(near, step)
@@ -354,23 +353,23 @@
             [turn(x[cuts_p[step - 1] : cuts_p[step]], s + 1) for s, x in enumerate(partials)]
         )
         if step == 1:
-            near, arrived, received, partials, exact = together(
-                (near, arrived, received, partials, exact)
+            other_a = swap(jnp.concatenate([parts_a[0][:, half:]] + far_1, 0), 1)
+            near, arrived, received, partials, exact, others_b, other_a = together(
+                (near, arrived, received, partials, exact, others_b, other_a)
             )
             near = double(near, arrived)
         else:
-            exact = [turn(x, s + 1) for s, x in enumerate(exact)]
             others_b = [jnp.concatenate(pieces, 0) for pieces in zip(*others_b)]
             pair_b = jnp.concatenate([view_b] + others_b, 0)
             pair_b = ((pair_b.astype(f32) - mean_b) * inv_b).astype(bf16)
-            norm_b = jnp.concatenate([pair_b, swap(pair_b, 1)], 0)
-            near, arrived, received, partials, exact, norm_b = together(
-                (near, arrived, received, partials, exact, norm_b)
+            near, arrived, received, partials, exact, pair_b = together(
+                (near, arrived, received, partials, exact, pair_b)
             )
     received.append([turn(x[cuts_p[2] :], s + 1) for s, x in enumerate(partials)])
+    exact = [turn(x, s + 1) for s, x in enumerate(exact)]
     near = merge(near, arrived, orders, mean_ap[:, :wide], inv_ap[:, :wide])
     corr = product(near, 0)
-    corr, received = together((corr, received))
+    corr, received, exact = together((corr, received, exact))
     diag = diagonal(0)
     for blocks, line in zip(zip(*received), exact):
         block = jnp.concatenate(blocks, 0).astype(f32)
@@ -380,50 +379,55 @@
     gcorr = jnp.where(diag, 2.0 * (corr - 1.0), 2.0 * lam * corr).astype(bf16)
 
     moving = [gcorr[:, lo:hi] for lo, hi in cuts(half)]
-    cuts_g = (0, narrow // 4, 5 * narrow // 8, narrow)
     loss = jnp.full((8, 128), loss, f32)
-    turned, sibling, far_a = [], [], []
+    cuts_g = (0, narrow // 4, 3 * narrow // 4, narrow)
+    mean_ah, inv_ah = mean_ap[:, :half], inv_ap[:, :half]
+    turned, sibling = [], []
     for step in range(3):
         arrived = send(moving, step)
-        turned.append(turns(gcorr[cuts_g[step] : cuts_g[step + 1]]))
+        piece = gcorr[cuts_g[step] : cuts_g[step + 1]]
+        if step < 2:
+            turned.append(turns(piece))
+        else:
+            both = [
+                turn(jnp.concatenate([piece, x[:, :half]], 0), s + 1)
+                for s, x in enumerate(parts_a[1:])
+            ]
+            turned.append([x[: narrow // 4] for x in both])
+            far_0 = [x[narrow // 4 :] for x in both]
         if step > 0:
             sibling.append([swap(x, 1) for x in turned[step - 1]])
-            far_a.append(
-                [
-                    turn(x[:, (2 - step) * half : (3 - step) * half], s + 1)
-                    for s, x in enumerate(parts_a[1:])
-                ]
-            )
         if step == 0:
+            for mask in [1] + h_masks:
+                loss = loss + swap(loss, mask)
+            moving, arrived, turned, gcorr, parts_a, pair_b, loss = together(
+                (moving, arrived, turned, gcorr, parts_a, pair_b, loss)
+            )
+        elif step == 1:
+            norm_b = jnp.concatenate([pair_b, swap(pair_b, 1)], 0)
             own = jnp.concatenate([gcorr, swap(gcorr, 1)], 1)
-            loss = loss + swap(loss, 1)
-            moving, arrived, turned, gcorr, own, loss, parts_a = together(
-                (moving, arrived, turned, gcorr, own, loss, parts_a)
-            )
-        elif step == 1:
+            moving, arrived, turned, gcorr, sibling, parts_a, norm_b, own = together(
+                (moving, arrived, turned, gcorr, sibling, parts_a, norm_b, own)
+            )
+        else:
+            cross = cross_products(0, norm_b, moving, orders, k)
             grad_nb = dot(near, own, ((1,), (1,)))
-            moving, arrived, turned, gcorr, sibling, far_a, parts_a, grad_nb = together(
-                (moving, arrived, turned, gcorr, sibling, far_a, parts_a, grad_nb)
-            )
-        else:
-            other_a = swap(jnp.concatenate([parts_a[0][:, half:]] + far_a[0], 0), 1)
-            moving, arrived, turned, sibling, far_a, other_a, loss = together(
-                (moving, arrived, turned, sibling, far_a, other_a, loss)
+            arrived, turned, sibling, far_0, cross, mean_ah, inv_ah, grad_nb = together(
+                (arrived, turned, sibling, far_0, cross, mean_ah, inv_ah, grad_nb)
             )
         if step < 2:
             moving = double(moving, arrived)
 
-    mean_ah, inv_ah = mean_ap[:, :half], inv_ap[:, :half]
     sibling.append([swap(x, 1) for x in turned[2]])
-    all_a = jnp.concatenate([parts_a[0][:, :half]] + far_a[1] + [other_a], 0)
-    pieces = [x for pair in zip(moving, arrived) for x in pair]
-    cross, stats_a = cross_products(norm_b, pieces, orders, all_a, mean_ah, inv_ah, k)
-    for mask in h_masks:
-        loss = loss + swap(loss, mask)
-    cross, stats_a, sibling, loss = together((cross, stats_a, sibling, loss))
-    stats_a = jnp.concatenate([stats_a, jnp.full((1, half), loss[0, 0], f32)])
-    for bit in (1, 2, 4):
-        stats_a = stats_a + swap_k(stats_a, bit)
+    all_a = jnp.concatenate([parts_a[0][:, :half]] + far_0 + [other_a], 0)
+    cross, stats_a = cross_products(
+        1, norm_b, arrived, orders, k, cross, all_a, mean_ah, inv_ah
+    )
+    cross, stats_a, sibling, rest = together((cross, stats_a, sibling, rest))
+    stats_a = jnp.concatenate(
+        [jnp.sum(stats_a, axis=0), jnp.broadcast_to(loss[0:1, 0:1], (1, half))]
+    )
+    stats_a = stats_a + swap_k(stats_a, 1)
 
     for s in range(1, cubes):
         for side, blocks in enumerate((turned, sibling)):
@@ -432,9 +436,12 @@
             grad_nb = grad_nb + dot(rest[:, start : start + half], block, ((1,), (1,)))
     flat_b = (near_b.astype(f32) - mean_bn) * inv_bn
     stats_b = jnp.stack([jnp.sum(grad_nb, axis=0), jnp.sum(grad_nb * flat_b, axis=0)])
+    stats_a, stats_b, grad_nb = together((stats_a, stats_b, grad_nb))
+    for bit in (2, 4):
+        stats_a = stats_a + swap_k(stats_a, bit)
     for mask in [1] + h_masks:
         stats_b = stats_b + swap(stats_b, mask)
-    stats_a, stats_b, grad_nb = together((stats_a, stats_b, grad_nb))
+    stats_a, stats_b = together((stats_a, stats_b))
     loss = stats_a[2, 0]
     stats_a, stats_b = stats_a / count, stats_b / count
 
@@ -442,6 +449,7 @@
     out_a = (inv_ah * (cross - stats_a[0:1] - flat_a * stats_a[1:2])).astype(bf16)
     mine = cubes * rows
     both = jnp.concatenate([out_a[:mine], swap(out_a[mine:], 1)], 1)
+    both, stats_b, grad_nb = together((both, stats_b, grad_nb))
     blocks = [both[s * rows : (s + 1) * rows] for s in range(cubes)]
     blocks = [blocks[0]] + [turn(blocks[s], -s) for s in range(1, cubes)]
     grad_a = place(blocks, jnp.stack(at))

time: 340 us -> 319 us (0.938)
  waiting for transfers between devices: 193 us -> 181 us
  starting transfers between devices: 81.7 us -> 72.4 us
    ppermute x13 -> x11, waiting for transfers between devices: 142 us -> 71.7 us  [turn(): lax.ppermute(x, 'dp', [(i, (i + 2 * cube * step) % devices) for i in rang...]
    ppermute x48, waiting for transfers between devices: 50.5 us -> 110 us  [swap(): return lax.ppermute(x, 'dp', [(i, i ^ mask) for i in range(devices)])]
    ppermute x48, starting transfers between devices: 49.8 us -> 43.2 us  [swap(): return lax.ppermute(x, 'dp', [(i, i ^ mask) for i in range(devices)])]
    ppermute x13 -> x11, starting transfers between devices: 24.1 us -> 19.5 us  [turn(): lax.ppermute(x, 'dp', [(i, (i + 2 * cube * step) % devices) for i in rang...]
    pallas_call x1 -> x2, Pallas kernels: 10.8 us -> 13.7 us  [cross_products(): pl.pallas_call(functools.partial(cross_kernel, side, orders), grid=(size...]
    unnamed x57 -> x79, local copies, waits for them, and re-layouts: 7.98 us -> 10.8 us
  transfers between devices with their start and end apart: 63 -> 61, of which waited for: 28 -> 27; matrix products, arithmetic and copies ran while one was open for 8% -> 7% of each run, Pallas kernels for 4% -> 5%
where the time goes in v4:
time: 319 us
  waiting for transfers between devices  181 us (57%)
  starting transfers between devices  72.4 us (23%)
  Pallas kernels  22 us (7%)
  local copies, waits for them, and re-layouts  14.6 us (5%)
  other arithmetic  13.9 us (4%)
  matrix products  12.9 us (4%)
    ppermute x48, waiting for transfers between devices, swap(): return lax.ppermute(x, 'dp', [(i, i ^ mask) for i in range(devices)])  110 us
    ppermute x11, waiting for transfers between devices, turn(): lax.ppermute(x, 'dp', [(i, (i + 2 * cube * step) % devices) for i in rang...  71.7 us
    ppermute x48, starting transfers between devices, swap(): return lax.ppermute(x, 'dp', [(i, i ^ mask) for i in range(devices)])  43.2 us
    ppermute x11, starting transfers between devices, turn(): lax.ppermute(x, 'dp', [(i, (i + 2 * cube * step) % devices) for i in rang...  19.5 us
    pallas_call x2, Pallas kernels, cross_products(): pl.pallas_call(functools.partial(cross_kernel, side, orders), grid=(size...  13.7 us
    dot_general x7, matrix products, dot(): lax.dot_general(x, y, (contract, ((), ())), preferred_element_type=jnp.fl...  12.9 us
    unnamed x79, local copies, waits for them, and re-layouts  10.8 us
    all_to_all x2, starting transfers between devices, exchange(): lax.all_to_all(x, 'dp', split_axis=0, concat_axis=0, axis_index_groups=gr...  9.74 us
  transfers between devices with their start and end apart: 61, of which 27 were waited for; matrix products, arithmetic and copies ran while one was open for 7% of the time, Pallas kernels for 5%

profile of v4, /device:TPU:0, one launch (start us, length us, event | category | flops | bytes accessed | tf_op | source)
XLA Modules:
  0.0 318.9 jit_solution(7895428335157980256)
XLA Ops:
  3.2 2.1 shard_map.49
  7.5 6.2 %all-to-all-start = ((bf16[8,128,512]{2,1,0:T(8,128)(2,1)}), bf16[8,128,512]{2,1,0:T(8,128)(2,1)S(1)}, u32[]{:S(2)}, u32[]{:S(2)}) async-start(bf16[8,128,512]{2,1,0:T(8,128)(2,1)} %get-tuple-element.190), calls=%async_computation | async-start | bytes 2097152 | tf_op jit(solution)/shard_map/all_to_all | solution.py:269
  13.7 2.7 collective-permute-start.5
  16.4 2.0 collective-permute-start
  22.6 13.7 %collective-permute-done.4 = f32[4,4096]{1,0:T(4,128)S(1)} collective-permute-done((f32[4,4096]{1,0:T(4,128)S(1)}, f32[4,4096]{1,0:T(4,128)S(1)}, u32[]{:S(2)}, u32[]{:S(2)}) %collective-permute-start.4) | collective-permute-done | bytes 65568 | tf_op jit(solution)/shard_map/ppermute | solution.py:255
  36.4 2.2 collective-permute-done.refs_3_
  38.6 2.0 collective-permute-start.9
  41.5 1.5 collective-permute-start.6
  46.3 5.4 %collective-permute-done.10 = f32[4,4096]{1,0:T(4,128)S(1)} collective-permute-done((f32[4,4096]{1,0:T(4,128)S(1)}, f32[4,4096]{1,0:T(4,128)S(1)}, u32[]{:S(2)}, u32[]{:S(2)}) %collective-permute-start.10) | collective-permute-done | bytes 65568 | tf_op jit(solution)/shard_map/ppermute | solution.py:255
  52.4 3.7 %collective-permute-done.11 = f32[4,4096]{1,0:T(4,128)S(1)} collective-permute-done((f32[4,4096]{1,0:T(4,128)S(1)}, f32[4,4096]{1,0:T(4,128)S(1)}, u32[]{:S(2)}, u32[]{:S(2)}) %collective-permute-start.11) | collective-permute-done | bytes 65568 | tf_op jit(solution)/shard_map/ppermute | solution.py:255
  59.1 4.3 %collective-permute-done.9 = bf16[64,4096]{1,0:T(8,128)(2,1)} collective-permute-done((bf16[64,4096]{1,0:T(8,128)(2,1)S(1)}, bf16[64,4096]{1,0:T(8,128)(2,1)}, u32[]{:S(2)}, u32[]{:S(2)}) %collective-permute-start.9) | collective-permute-done | bytes 524320 | tf_op jit(solution)/shard_map/ppermute | solution.py:261
  65.5 1.5 collective-permute-start.12
  68.5 2.0 collective-permute-start.14
  72.5 19.4 %collective-permute-done.14.refs_5_ = bf16[512,512]{1,0:T(8,128)(2,1)S(1)} collective-permute-done((bf16[512,512]{1,0:T(8,128)(2,1)S(1)}, bf16[512,512]{1,0:T(8,128)(2,1)S(1)}, u32[]{:S(2)}, u32[]{:S(2)}) %collective-permute-start.14) | collective-permute-done | bytes 524320 | tf_op jit(solution)/shard_map/ppermute | solution.py:255
  94.3 3.5 %collective-permute-start.18 = (bf16[128,768]{1,0:T(8,128)(2,1)S(1)}, bf16[128,768]{1,0:T(8,128)(2,1)S(1)}, u32[]{:S(2)}, u32[]{:S(2)}) collective-permute-start(bf16[128,768]{1,0:T(8,128)(2,1)S(1)} %copy-done.12), channel_id=1, source_target_pairs={{0,8},{1,9},{2,10},{3,11},{4,12},{5,13},{6,14},{7,15},{8,0},{9,1},... | collective-permute-start | bytes 589832 | tf_op jit(solution)/shard_map/ppermute | solution.py:255
  101.0 2.7 collective-permute-done.20.refs_5_
  106.0 2.8 collective-permute-start.24
  109.3 6.5 %collective-permute-done.23.refs_5_ = bf16[256,512]{1,0:T(8,128)(2,1)S(1)} collective-permute-done((bf16[256,512]{1,0:T(8,128)(2,1)S(1)}, bf16[256,512]{1,0:T(8,128)(2,1)S(1)}, u32[]{:S(2)}, u32[]{:S(2)}) %collective-permute-start.23) | collective-permute-done | bytes 262176 | tf_op jit(solution)/shard_map/ppermute | solution.py:255
  115.8 8.3 %collective-permute-done.22.refs_4_ = bf16[256,768]{1,0:T(8,128)(2,1)S(1)} collective-permute-done((bf16[256,768]{1,0:T(8,128)(2,1)S(1)}, bf16[256,768]{1,0:T(8,128)(2,1)S(1)}, u32[]{:S(2)}, u32[]{:S(2)}) %collective-permute-start.22) | collective-permute-done | bytes 393248 | tf_op jit(solution)/shard_map/ppermute | solution.py:255
  126.3 2.7 collective-permute-start.28
  129.1 2.9 collective-permute-start.29
  131.9 1.6 multiply_convert_fusion
  133.5 16.0 %collective-permute-done.28.refs_5_ = bf16[512,512]{1,0:T(8,128)(2,1)S(1)} collective-permute-done((bf16[512,512]{1,0:T(8,128)(2,1)S(1)}, bf16[512,512]{1,0:T(8,128)(2,1)S(1)}, u32[]{:S(2)}, u32[]{:S(2)}) %collective-permute-start.28) | collective-permute-done | bytes 524320 | tf_op jit(solution)/shard_map/ppermute | solution.py:255
  149.5 2.9 collective-permute-done.29
  155.1 2.7 collective-permute-start.32
  159.6 4.5 %collective-permute-done.32 = f32[1,512]{1,0:T(1,128)S(1)} collective-permute-done((f32[1,512]{1,0:T(1,128)S(1)}, f32[1,512]{1,0:T(1,128)S(1)}, u32[]{:S(2)}, u32[]{:S(2)}) %collective-permute-start.32) | collective-permute-done | bytes 2080 | tf_op jit(solution)/shard_map/ppermute | solution.py:261
  164.2 3.3 %fusion.2 = (f32[]{:T(128)}, bf16[512,1024]{1,0:T(8,128)(2,1)S(1)}) fusion(f32[512,1024]{1,0:T(8,128)S(1)} %add.164, f32[512]{0:T(512)S(1)} %bitcast.69, s32[1024]{0:T(1024)S(1)} %iota_add_fusion.1, s32[512]{0:T(512)S(1)} %iota_add_fusion.2, bf16[64,1024]{1,0:T(8,128)(2,1)S(1)} %collective-permute-done.31, bf16[256,1024]{1,0:T(8,128)(2,1)S(1)} %collective-permute-done.29, ...), kind=kLoop, calls=%fused_computation.7 | loop fusion | flops 11010047 | bytes 4202500 | tf_op jit(solution)/shard_map/reduce_sum | solution.py:378
  170.6 2.0 collective-permute-start.36
  174.3 9.2 %collective-permute-done.38 = f32[8,128]{1,0:T(8,128)S(1)} collective-permute-done((f32[8,128]{1,0:T(8,128)S(1)}, f32[8,128]{1,0:T(8,128)S(1)}, u32[]{:S(2)}, u32[]{:S(2)}) %collective-permute-start.38) | collective-permute-done | bytes 4128 | tf_op jit(solution)/shard_map/ppermute | solution.py:255
  186.4 2.1 collective-permute-start.39
  189.7 1.6 collective-permute-done.45
  191.3 2.0 collective-permute-start.42
  193.5 2.5 pad_maximum_fusion.rows_ref
  196.1 6.0 %collective-permute-done.41.refs_5_ = bf16[1024,256]{1,0:T(8,128)(2,1)S(1)} collective-permute-done((bf16[1024,256]{1,0:T(8,128)(2,1)S(1)}, bf16[1024,256]{1,0:T(8,128)(2,1)S(1)}, u32[]{:S(2)}, u32[]{:S(2)}) %collective-permute-start.41) | collective-permute-done | bytes 524320 | tf_op jit(solution)/shard_map/ppermute | solution.py:255
  202.1 14.6 %collective-permute-done.42 = bf16[256,1024]{1,0:T(8,128)(2,1)S(1)} collective-permute-done((bf16[256,1024]{1,0:T(8,128)(2,1)S(1)}, bf16[256,1024]{1,0:T(8,128)(2,1)S(1)}, u32[]{:S(2)}, u32[]{:S(2)}) %collective-permute-start.42) | collective-permute-done | bytes 524320 | tf_op jit(solution)/shard_map/ppermute | solution.py:261
  220.8 2.8 collective-permute-start.48
  224.6 3.8 %fusion.54 = f32[1024,512]{1,0:T(8,128)} fusion(bf16[1024,2048]{1,0:T(8,128)(2,1)S(1)} %shard_map.56, bf16[512,2048]{1,0:T(8,128)(2,1)S(1)} %pad_maximum_fusion.1), kind=kOutput, calls=%fused_computation.99 | convolution fusion | flops 2147483648 | bytes 8388608 | tf_op jit(solution)/shard_map/dot_general | solution.py:189
  228.3 6.5 %shard_map.59.refs_0_ = f32[512,1024]{1,0:T(8,128)} custom-call(s32[1]{0:T(128)} %bitcast.k_ref, bf16[512,4096]{1,0:T(8,128)(2,1)} %pad_maximum_fusion.rows_ref, bf16[2048,384]{1,0:T(8,128)(2,1)S(1)} %get-tuple-element.293.refs_0_, bf16[2048,384]{1,0:T(8,128)(2,1)S(1)} %get-tuple-element.294.refs_1_, bf16[2048,256]{1,0:T(8,128)(2,1)S(1)} %get-tuple-element.295.refs_2_), custom_call_target="tpu_custom_call" | custom-call | tf_op jit(solution)/shard_map/pallas_call | solution.py:231
  234.8 21.0 %collective-permute-done.49 = bf16[256,1024]{1,0:T(8,128)(2,1)S(1)} collective-permute-done((bf16[256,1024]{1,0:T(8,128)(2,1)}, bf16[256,1024]{1,0:T(8,128)(2,1)S(1)}, u32[]{:S(2)}, u32[]{:S(2)}) %collective-permute-start.49) | collective-permute-done | bytes 524320 | tf_op jit(solution)/shard_map/ppermute | solution.py:261
  257.1 7.2 %shard_map.60 = (f32[512,1024]{1,0:T(8,128)}, f32[1,2,1024]{2,1,0:T(2,128)S(1)}) custom-call(s32[1]{0:T(128)} %bitcast.k_ref, bf16[512,4096]{1,0:T(8,128)(2,1)} %pad_maximum_fusion.rows_ref, f32[512,1024]{1,0:T(8,128)} %shard_map.59.refs_0_, bf16[512,1024]{1,0:T(8,128)(2,1)S(1)} %pad_maximum_fusion.3.refs_1_, f32[1,1024]{1,0:T(1,128)S(1)} %slice.181.refs_2_, ...), custom_call_target="tpu_custom_call" | custom-call | tf_op jit(solution)/shard_map/pallas_call | solution.py:231
  267.0 2.8 fusion.44
  271.5 2.8 collective-permute-done.53
  274.3 2.0 collective-permute-start.54
  278.3 3.6 %collective-permute-done.56 = f32[2,512]{1,0:T(2,128)S(1)} collective-permute-done((f32[2,512]{1,0:T(2,128)S(1)}, f32[2,512]{1,0:T(2,128)S(1)}, u32[]{:S(2)}, u32[]{:S(2)}) %collective-permute-start.56) | collective-permute-done | bytes 4128 | tf_op jit(solution)/shard_map/ppermute | solution.py:255
  282.8 1.9 collective-permute-done.57
  286.3 3.6 %all-to-all-start.1 = ((bf16[8,128,512]{2,1,0:T(8,128)(2,1)}), bf16[8,128,512]{2,1,0:T(8,128)(2,1)S(1)}, u32[]{:S(2)}, u32[]{:S(2)}) async-start(bf16[8,128,512]{2,1,0:T(8,128)(2,1)} %shard_map.62), calls=%async_computation.1 | async-start | bytes 2097152 | tf_op jit(solution)/shard_map/all_to_all | solution.py:269
  292.0 24.2 %collective-permute-done.58.refs_1_ = bf16[128,2048]{1,0:T(8,128)(2,1)S(1)} collective-permute-done((bf16[128,2048]{1,0:T(8,128)(2,1)S(1)}, bf16[128,2048]{1,0:T(8,128)(2,1)S(1)}, u32[]{:S(2)}, u32[]{:S(2)}) %collective-permute-start.58) | collective-permute-done | bytes 524320 | tf_op jit(solution)/shard_map/ppermute | solution.py:261
  316.2 1.6 shard_map.61
  (236 shorter events, 64.6 us)
Async XLA Ops:
  7.5 55.9 %all-to-all-start = ((bf16[8,128,512]{2,1,0:T(8,128)(2,1)}), bf16[8,128,512]{2,1,0:T(8,128)(2,1)S(1)}, u32[]{:S(2)}, u32[]{:S(2)}) async-start(bf16[8,128,512]{2,1,0:T(8,128)(2,1)} %get-tuple-element.190), calls=%async_computation | async-start | bytes 2097152 | tf_op jit(solution)/shard_map/all_to_all | solution.py:269
  13.7 7.6 %collective-permute-start.3 = (f32[4,4096]{1,0:T(4,128)S(1)}, f32[4,4096]{1,0:T(4,128)S(1)}, u32[]{:S(2)}, u32[]{:S(2)}) collective-permute-start(f32[4,4096]{1,0:T(4,128)S(1)} %get-tuple-element.172), channel_id=1, source_target_pairs={{0,1},{1,0},{2,3},{3,2},{4,5},{5,4},{6,7},{7,6},{8,9},{9,8},{10,11... | collective-permute-start | bytes 196616 | tf_op jit(solution)/shard_map/ppermute | solution.py:255
  13.7 24.8 %collective-permute-start.5 = (bf16[128,1024]{1,0:T(8,128)(2,1)S(1)}, bf16[128,1024]{1,0:T(8,128)(2,1)S(1)}, u32[]{:S(2)}, u32[]{:S(2)}) collective-permute-start(bf16[128,1024]{1,0:T(8,128)(2,1)S(1)} %slice.155), channel_id=1, source_target_pairs={{0,16},{1,17},{2,18},{3,19},{4,20},{5,21},{6,22},{7,23},{8,24},{9,... | collective-permute-start | bytes 786440 | tf_op jit(solution)/shard_map/ppermute | solution.py:261
  16.4 22.2 %collective-permute-start = (bf16[128,768]{1,0:T(8,128)(2,1)S(1)}, bf16[128,768]{1,0:T(8,128)(2,1)S(1)}, u32[]{:S(2)}, u32[]{:S(2)}) collective-permute-start(bf16[128,768]{1,0:T(8,128)(2,1)S(1)} %get-tuple-element.178.refs_0_), channel_id=1, source_target_pairs={{0,8},{1,9},{2,10},{3,11},{4,12},{5,13},{6,14},{7,15},{8,0},{9,1},... | collective-permute-start | bytes 589832 | tf_op jit(solution)/shard_map/ppermute | solution.py:255
  18.4 20.2 %collective-permute-start.1 = (bf16[128,768]{1,0:T(8,128)(2,1)S(1)}, bf16[128,768]{1,0:T(8,128)(2,1)S(1)}, u32[]{:S(2)}, u32[]{:S(2)}) collective-permute-start(bf16[128,768]{1,0:T(8,128)(2,1)S(1)} %get-tuple-element.179.refs_1_), channel_id=1, source_target_pairs={{0,2},{1,3},{2,0},{3,1},{4,6},{5,7},{6,4},{7,5},{8,10},{9,11},{10,... | collective-permute-start | bytes 589832 | tf_op jit(solution)/shard_map/ppermute | solution.py:255
  19.9 16.5 %collective-permute-start.2 = (bf16[128,512]{1,0:T(8,128)(2,1)S(1)}, bf16[128,512]{1,0:T(8,128)(2,1)S(1)}, u32[]{:S(2)}, u32[]{:S(2)}) collective-permute-start(bf16[128,512]{1,0:T(8,128)(2,1)S(1)} %get-tuple-element.180.refs_2_), channel_id=1, source_target_pairs={{0,4},{1,5},{2,6},{3,7},{4,0},{5,1},{6,2},{7,3},{8,12},{9,13},{10,... | collective-permute-start | bytes 393224 | tf_op jit(solution)/shard_map/ppermute | solution.py:255
  21.4 15.0 %collective-permute-start.4 = (f32[4,4096]{1,0:T(4,128)S(1)}, f32[4,4096]{1,0:T(4,128)S(1)}, u32[]{:S(2)}, u32[]{:S(2)}) collective-permute-start(f32[4,4096]{1,0:T(4,128)S(1)} %add.149), channel_id=1, source_target_pairs={{0,16},{1,17},{2,18},{3,19},{4,20},{5,21},{6,22},{7,23},{8,24},{9,... | collective-permute-start | bytes 196616 | tf_op jit(solution)/shard_map/ppermute | solution.py:255
  38.6 24.8 %collective-permute-start.9 = (bf16[64,4096]{1,0:T(8,128)(2,1)S(1)}, bf16[64,4096]{1,0:T(8,128)(2,1)}, u32[]{:S(2)}, u32[]{:S(2)}) collective-permute-start(bf16[64,4096]{1,0:T(8,128)(2,1)S(1)} %get-tuple-element.187), channel_id=1, source_target_pairs={{0,16},{1,17},{2,18},{3,19},{4,20},{5,21},{6,22},{7,23},{8,24},{9,... | collective-permute-start | bytes 1572872 | tf_op jit(solution)/shard_map/ppermute | solution.py:261
  41.5 15.9 %collective-permute-start.6 = (bf16[256,768]{1,0:T(8,128)(2,1)S(1)}, bf16[256,768]{1,0:T(8,128)(2,1)S(1)}, u32[]{:S(2)}, u32[]{:S(2)}) collective-permute-start(bf16[256,768]{1,0:T(8,128)(2,1)S(1)} %get-tuple-element.194.refs_0_), channel_id=1, source_target_pairs={{0,4},{1,5},{2,6},{3,7},{4,0},{5,1},{6,2},{7,3},{8,12},{9,13},{10,... | collective-permute-start | bytes 1179656 | tf_op jit(solution)/shard_map/ppermute | solution.py:255
  43.0 15.3 %collective-permute-start.7 = (bf16[256,768]{1,0:T(8,128)(2,1)S(1)}, bf16[256,768]{1,0:T(8,128)(2,1)S(1)}, u32[]{:S(2)}, u32[]{:S(2)}) collective-permute-start(bf16[256,768]{1,0:T(8,128)(2,1)S(1)} %get-tuple-element.195.refs_1_), channel_id=1, source_target_pairs={{0,8},{1,9},{2,10},{3,11},{4,12},{5,13},{6,14},{7,15},{8,0},{9,1},... | collective-permute-start | bytes 1179656 | tf_op jit(solution)/shard_map/ppermute | solution.py:255
  44.3 12.4 %collective-permute-start.8 = (bf16[256,512]{1,0:T(8,128)(2,1)S(1)}, bf16[256,512]{1,0:T(8,128)(2,1)S(1)}, u32[]{:S(2)}, u32[]{:S(2)}) collective-permute-start(bf16[256,512]{1,0:T(8,128)(2,1)S(1)} %get-tuple-element.196.refs_2_), channel_id=1, source_target_pairs={{0,2},{1,3},{2,0},{3,1},{4,6},{5,7},{6,4},{7,5},{8,10},{9,11},{10,... | collective-permute-start | bytes 786440 | tf_op jit(solution)/shard_map/ppermute | solution.py:255
  63.4 7.8 %collective-permute-start.16 = (f32[4,4096]{1,0:T(4,128)}, f32[4,4096]{1,0:T(4,128)}, u32[]{:S(2)}, u32[]{:S(2)}) collective-permute-start(f32[4,4096]{1,0:T(4,128)} %add.152), channel_id=1, source_target_pairs={{0,8},{1,9},{2,10},{3,11},{4,12},{5,13},{6,14},{7,15},{8,0},{9,1},... | collective-permute-start | bytes 196616 | tf_op jit(solution)/shard_map/ppermute | solution.py:255
  65.5 26.4 %collective-permute-start.12 = (bf16[512,768]{1,0:T(8,128)(2,1)S(1)}, bf16[512,768]{1,0:T(8,128)(2,1)S(1)}, u32[]{:S(2)}, u32[]{:S(2)}) collective-permute-start(bf16[512,768]{1,0:T(8,128)(2,1)S(1)} %get-tuple-element.215.refs_0_), channel_id=1, source_target_pairs={{0,2},{1,3},{2,0},{3,1},{4,6},{5,7},{6,4},{7,5},{8,10},{9,11},{10,... | collective-permute-start | bytes 2359304 | tf_op jit(solution)/shard_map/ppermute | solution.py:255
  67.0 24.9 %collective-permute-start.13 = (bf16[512,768]{1,0:T(8,128)(2,1)S(1)}, bf16[512,768]{1,0:T(8,128)(2,1)S(1)}, u32[]{:S(2)}, u32[]{:S(2)}) collective-permute-start(bf16[512,768]{1,0:T(8,128)(2,1)S(1)} %get-tuple-element.217.refs_2_), channel_id=1, source_target_pairs={{0,4},{1,5},{2,6},{3,7},{4,0},{5,1},{6,2},{7,3},{8,12},{9,13},{10,... | collective-permute-start | bytes 2359304 | tf_op jit(solution)/shard_map/ppermute | solution.py:255
  68.5 23.4 %collective-permute-start.14 = (bf16[512,512]{1,0:T(8,128)(2,1)S(1)}, bf16[512,512]{1,0:T(8,128)(2,1)S(1)}, u32[]{:S(2)}, u32[]{:S(2)}) collective-permute-start(bf16[512,512]{1,0:T(8,128)(2,1)S(1)} %get-tuple-element.219.refs_4_), channel_id=1, source_target_pairs={{0,8},{1,9},{2,10},{3,11},{4,12},{5,13},{6,14},{7,15},{8,0},{9,1},... | collective-permute-start | bytes 1572872 | tf_op jit(solution)/shard_map/ppermute | solution.py:255
  70.5 21.4 %collective-permute-start.15 = (bf16[64,4096]{1,0:T(8,128)(2,1)S(1)}, bf16[64,4096]{1,0:T(8,128)(2,1)S(1)}, u32[]{:S(2)}, u32[]{:S(2)}) collective-permute-start(bf16[64,4096]{1,0:T(8,128)(2,1)S(1)} %copy-done.24), channel_id=1, source_target_pairs={{0,16},{1,17},{2,18},{3,19},{4,20},{5,21},{6,22},{7,23},{8,24},{9,... | collective-permute-start | bytes 1572872 | tf_op jit(solution)/shard_map/ppermute | solution.py:261
  94.3 9.4 %collective-permute-start.18 = (bf16[128,768]{1,0:T(8,128)(2,1)S(1)}, bf16[128,768]{1,0:T(8,128)(2,1)S(1)}, u32[]{:S(2)}, u32[]{:S(2)}) collective-permute-start(bf16[128,768]{1,0:T(8,128)(2,1)S(1)} %copy-done.12), channel_id=1, source_target_pairs={{0,8},{1,9},{2,10},{3,11},{4,12},{5,13},{6,14},{7,15},{8,0},{9,1},... | collective-permute-start | bytes 589832 | tf_op jit(solution)/shard_map/ppermute | solution.py:255
  97.9 7.0 %collective-permute-start.19 = (bf16[128,768]{1,0:T(8,128)(2,1)S(1)}, bf16[128,768]{1,0:T(8,128)(2,1)S(1)}, u32[]{:S(2)}, u32[]{:S(2)}) collective-permute-start(bf16[128,768]{1,0:T(8,128)(2,1)S(1)} %copy-done.14), channel_id=1, source_target_pairs={{0,2},{1,3},{2,0},{3,1},{4,6},{5,7},{6,4},{7,5},{8,10},{9,11},{10,... | collective-permute-start | bytes 589832 | tf_op jit(solution)/shard_map/ppermute | solution.py:255
  99.1 10.2 %collective-permute-start.25 = (bf16[256,1024]{1,0:T(8,128)(2,1)S(1)}, bf16[256,1024]{1,0:T(8,128)(2,1)S(1)}, u32[]{:S(2)}, u32[]{:S(2)}) collective-permute-start(bf16[256,1024]{1,0:T(8,128)(2,1)S(1)} %pad_maximum_fusion.5), channel_id=1, source_target_pairs={{0,1},{1,0},{2,3},{3,2},{4,5},{5,4},{6,7},{7,6},{8,9},{9,8},{10,11... | collective-permute-start | bytes 1572872 | tf_op jit(solution)/shard_map/ppermute | solution.py:255
  104.9 10.9 %collective-permute-start.21 = (bf16[256,768]{1,0:T(8,128)(2,1)S(1)}, bf16[256,768]{1,0:T(8,128)(2,1)S(1)}, u32[]{:S(2)}, u32[]{:S(2)}) collective-permute-start(bf16[256,768]{1,0:T(8,128)(2,1)S(1)} %get-tuple-element.241.refs_0_), channel_id=1, source_target_pairs={{0,4},{1,5},{2,6},{3,7},{4,0},{5,1},{6,2},{7,3},{8,12},{9,13},{10,... | collective-permute-start | bytes 1179656 | tf_op jit(solution)/shard_map/ppermute | solution.py:255
  105.6 18.5 %collective-permute-start.22 = (bf16[256,768]{1,0:T(8,128)(2,1)S(1)}, bf16[256,768]{1,0:T(8,128)(2,1)S(1)}, u32[]{:S(2)}, u32[]{:S(2)}) collective-permute-start(bf16[256,768]{1,0:T(8,128)(2,1)S(1)} %get-tuple-element.242.refs_1_), channel_id=1, source_target_pairs={{0,8},{1,9},{2,10},{3,11},{4,12},{5,13},{6,14},{7,15},{8,0},{9,1},... | collective-permute-start | bytes 1179656 | tf_op jit(solution)/shard_map/ppermute | solution.py:255
  106.0 18.1 %collective-permute-start.24 = (bf16[192,1024]{1,0:T(8,128)(2,1)S(1)}, bf16[192,1024]{1,0:T(8,128)(2,1)S(1)}, u32[]{:S(2)}, u32[]{:S(2)}) collective-permute-start(bf16[192,1024]{1,0:T(8,128)(2,1)S(1)} %slice.166), channel_id=1, source_target_pairs={{0,16},{1,17},{2,18},{3,19},{4,20},{5,21},{6,22},{7,23},{8,24},{9,... | collective-permute-start | bytes 1179656 | tf_op jit(solution)/shard_map/ppermute | solution.py:261
  108.8 7.1 %collective-permute-start.23 = (bf16[256,512]{1,0:T(8,128)(2,1)S(1)}, bf16[256,512]{1,0:T(8,128)(2,1)S(1)}, u32[]{:S(2)}, u32[]{:S(2)}) collective-permute-start(bf16[256,512]{1,0:T(8,128)(2,1)S(1)} %get-tuple-element.243.refs_2_), channel_id=1, source_target_pairs={{0,2},{1,3},{2,0},{3,1},{4,6},{5,7},{6,4},{7,5},{8,10},{9,11},{10,... | collective-permute-start | bytes 786440 | tf_op jit(solution)/shard_map/ppermute | solution.py:255
  124.3 28.2 %collective-permute-start.26 = (bf16[512,768]{1,0:T(8,128)(2,1)S(1)}, bf16[512,768]{1,0:T(8,128)(2,1)S(1)}, u32[]{:S(2)}, u32[]{:S(2)}) collective-permute-start(bf16[512,768]{1,0:T(8,128)(2,1)S(1)} %get-tuple-element.255.refs_0_), channel_id=1, source_target_pairs={{0,2},{1,3},{2,0},{3,1},{4,6},{5,7},{6,4},{7,5},{8,10},{9,11},{10,... | collective-permute-start | bytes 2359304 | tf_op jit(solution)/shard_map/ppermute | solution.py:255
  124.9 27.6 %collective-permute-start.27 = (bf16[512,768]{1,0:T(8,128)(2,1)S(1)}, bf16[512,768]{1,0:T(8,128)(2,1)S(1)}, u32[]{:S(2)}, u32[]{:S(2)}) collective-permute-start(bf16[512,768]{1,0:T(8,128)(2,1)S(1)} %get-tuple-element.257.refs_2_), channel_id=1, source_target_pairs={{0,4},{1,5},{2,6},{3,7},{4,0},{5,1},{6,2},{7,3},{8,12},{9,13},{10,... | collective-permute-start | bytes 2359304 | tf_op jit(solution)/shard_map/ppermute | solution.py:255
  126.3 23.2 %collective-permute-start.28 = (bf16[512,512]{1,0:T(8,128)(2,1)S(1)}, bf16[512,512]{1,0:T(8,128)(2,1)S(1)}, u32[]{:S(2)}, u32[]{:S(2)}) collective-permute-start(bf16[512,512]{1,0:T(8,128)(2,1)S(1)} %get-tuple-element.259.refs_4_), channel_id=1, source_target_pairs={{0,8},{1,9},{2,10},{3,11},{4,12},{5,13},{6,14},{7,15},{8,0},{9,1},... | collective-permute-start | bytes 1572872 | tf_op jit(solution)/shard_map/ppermute | solution.py:255
  129.1 23.4 %collective-permute-start.29 = (bf16[256,1024]{1,0:T(8,128)(2,1)S(1)}, bf16[256,1024]{1,0:T(8,128)(2,1)S(1)}, u32[]{:S(2)}, u32[]{:S(2)}) collective-permute-start(bf16[256,1024]{1,0:T(8,128)(2,1)S(1)} %slice.168), channel_id=1, source_target_pairs={{0,16},{1,17},{2,18},{3,19},{4,20},{5,21},{6,22},{7,23},{8,24},{9,... | collective-permute-start | bytes 1572872 | tf_op jit(solution)/shard_map/ppermute | solution.py:261
  154.8 9.4 %collective-permute-start.31 = (bf16[64,1024]{1,0:T(8,128)(2,1)S(1)}, bf16[64,1024]{1,0:T(8,128)(2,1)S(1)}, u32[]{:S(2)}, u32[]{:S(2)}) collective-permute-start(bf16[64,1024]{1,0:T(8,128)(2,1)S(1)} %slice.171), channel_id=1, source_target_pairs={{0,16},{1,17},{2,18},{3,19},{4,20},{5,21},{6,22},{7,23},{8,24},{9,... | collective-permute-start | bytes 393224 | tf_op jit(solution)/shard_map/ppermute | solution.py:261
  155.1 9.1 %collective-permute-start.32 = (f32[1,512]{1,0:T(1,128)S(1)}, f32[1,512]{1,0:T(1,128)S(1)}, u32[]{:S(2)}, u32[]{:S(2)}) collective-permute-start(f32[1,512]{1,0:T(1,128)S(1)} %bitcast.68), channel_id=1, source_target_pairs={{0,16},{1,17},{2,18},{3,19},{4,20},{5,21},{6,22},{7,23},{8,24},{9,... | collective-permute-start | bytes 6152 | tf_op jit(solution)/shard_map/ppermute | solution.py:261
  168.4 17.2 %collective-permute-start.33 = (bf16[512,384]{1,0:T(8,128)(2,1)S(1)}, bf16[512,384]{1,0:T(8,128)(2,1)S(1)}, u32[]{:S(2)}, u32[]{:S(2)}) collective-permute-start(bf16[512,384]{1,0:T(8,128)(2,1)S(1)} %get-tuple-element.272.refs_0_), channel_id=1, source_target_pairs={{0,8},{1,9},{2,10},{3,11},{4,12},{5,13},{6,14},{7,15},{8,0},{9,1},... | collective-permute-start | bytes 1179656 | tf_op jit(solution)/shard_map/ppermute | solution.py:255
  168.5 17.2 %collective-permute-start.34 = (bf16[512,384]{1,0:T(8,128)(2,1)S(1)}, bf16[512,384]{1,0:T(8,128)(2,1)S(1)}, u32[]{:S(2)}, u32[]{:S(2)}) collective-permute-start(bf16[512,384]{1,0:T(8,128)(2,1)S(1)} %get-tuple-element.273.refs_1_), channel_id=1, source_target_pairs={{0,2},{1,3},{2,0},{3,1},{4,6},{5,7},{6,4},{7,5},{8,10},{9,11},{10,... | collective-permute-start | bytes 1179656 | tf_op jit(solution)/shard_map/ppermute | solution.py:255
  170.0 14.1 %collective-permute-start.35 = (bf16[512,256]{1,0:T(8,128)(2,1)S(1)}, bf16[512,256]{1,0:T(8,128)(2,1)S(1)}, u32[]{:S(2)}, u32[]{:S(2)}) collective-permute-start(bf16[512,256]{1,0:T(8,128)(2,1)S(1)} %slice.214.refs_2_), channel_id=1, source_target_pairs={{0,4},{1,5},{2,6},{3,7},{4,0},{5,1},{6,2},{7,3},{8,12},{9,13},{10,... | collective-permute-start | bytes 786440 | tf_op jit(solution)/shard_map/ppermute | solution.py:255
  170.6 13.5 %collective-permute-start.36 = (bf16[128,1024]{1,0:T(8,128)(2,1)S(1)}, bf16[128,1024]{1,0:T(8,128)(2,1)S(1)}, u32[]{:S(2)}, u32[]{:S(2)}) collective-permute-start(bf16[128,1024]{1,0:T(8,128)(2,1)S(1)} %slice.215), channel_id=1, source_target_pairs={{0,16},{1,17},{2,18},{3,19},{4,20},{5,21},{6,22},{7,23},{8,24},{9,... | collective-permute-start | bytes 786440 | tf_op jit(solution)/shard_map/ppermute | solution.py:261
  173.3 10.1 %collective-permute-start.38 = (f32[8,128]{1,0:T(8,128)S(1)}, f32[8,128]{1,0:T(8,128)S(1)}, u32[]{:S(2)}, u32[]{:S(2)}) collective-permute-start(f32[8,128]{1,0:T(8,128)S(1)} %broadcast_add_fusion), channel_id=1, source_target_pairs={{0,16},{1,17},{2,18},{3,19},{4,20},{5,21},{6,22},{7,23},{8,24},{9,... | collective-permute-start | bytes 12296 | tf_op jit(solution)/shard_map/ppermute | solution.py:255
  185.6 7.8 %collective-permute-start.44 = (bf16[256,4096]{1,0:T(8,128)(2,1)S(1)}, bf16[256,4096]{1,0:T(8,128)(2,1)S(1)}, u32[]{:S(2)}, u32[]{:S(2)}) collective-permute-start(bf16[256,4096]{1,0:T(8,128)(2,1)S(1)} %multiply_convert_fusion), channel_id=1, source_target_pairs={{0,1},{1,0},{2,3},{3,2},{4,5},{5,4},{6,7},{7,6},{8,9},{9,8},{10,11... | collective-permute-start | bytes 6291464 | tf_op jit(solution)/shard_map/ppermute | solution.py:255
  186.4 30.4 %collective-permute-start.39 = (bf16[1024,384]{1,0:T(8,128)(2,1)S(1)}, bf16[1024,384]{1,0:T(8,128)(2,1)S(1)}, u32[]{:S(2)}, u32[]{:S(2)}) collective-permute-start(bf16[1024,384]{1,0:T(8,128)(2,1)S(1)} %get-tuple-element.287.refs_0_), channel_id=1, source_target_pairs={{0,4},{1,5},{2,6},{3,7},{4,0},{5,1},{6,2},{7,3},{8,12},{9,13},{10,... | collective-permute-start | bytes 2359304 | tf_op jit(solution)/shard_map/ppermute | solution.py:255
  188.4 30.5 %collective-permute-start.40 = (bf16[1024,384]{1,0:T(8,128)(2,1)S(1)}, bf16[1024,384]{1,0:T(8,128)(2,1)S(1)}, u32[]{:S(2)}, u32[]{:S(2)}) collective-permute-start(bf16[1024,384]{1,0:T(8,128)(2,1)S(1)} %get-tuple-element.288.refs_1_), channel_id=1, source_target_pairs={{0,8},{1,9},{2,10},{3,11},{4,12},{5,13},{6,14},{7,15},{8,0},{9,1},... | collective-permute-start | bytes 2359304 | tf_op jit(solution)/shard_map/ppermute | solution.py:255
  188.4 13.6 %collective-permute-start.41 = (bf16[1024,256]{1,0:T(8,128)(2,1)S(1)}, bf16[1024,256]{1,0:T(8,128)(2,1)S(1)}, u32[]{:S(2)}, u32[]{:S(2)}) collective-permute-start(bf16[1024,256]{1,0:T(8,128)(2,1)S(1)} %get-tuple-element.289.refs_2_), channel_id=1, source_target_pairs={{0,2},{1,3},{2,0},{3,1},{4,6},{5,7},{6,4},{7,5},{8,10},{9,11},{10,... | collective-permute-start | bytes 1572872 | tf_op jit(solution)/shard_map/ppermute | solution.py:255
  191.3 25.4 %collective-permute-start.42 = (bf16[256,1024]{1,0:T(8,128)(2,1)S(1)}, bf16[256,1024]{1,0:T(8,128)(2,1)S(1)}, u32[]{:S(2)}, u32[]{:S(2)}) collective-permute-start(bf16[256,1024]{1,0:T(8,128)(2,1)S(1)} %slice.176), channel_id=1, source_target_pairs={{0,16},{1,17},{2,18},{3,19},{4,20},{5,21},{6,22},{7,23},{8,24},{9,... | collective-permute-start | bytes 1572872 | tf_op jit(solution)/shard_map/ppermute | solution.py:261
  219.3 37.2 %collective-permute-start.46 = (bf16[2048,384]{1,0:T(8,128)(2,1)S(1)}, bf16[2048,384]{1,0:T(8,128)(2,1)S(1)}, u32[]{:S(2)}, u32[]{:S(2)}) collective-permute-start(bf16[2048,384]{1,0:T(8,128)(2,1)S(1)} %get-tuple-element.293.refs_0_), channel_id=1, source_target_pairs={{0,2},{1,3},{2,0},{3,1},{4,6},{5,7},{6,4},{7,5},{8,10},{9,11},{10,... | collective-permute-start | bytes 4718600 | tf_op jit(solution)/shard_map/ppermute | solution.py:255
  219.4 37.1 %collective-permute-start.47 = (bf16[2048,384]{1,0:T(8,128)(2,1)S(1)}, bf16[2048,384]{1,0:T(8,128)(2,1)S(1)}, u32[]{:S(2)}, u32[]{:S(2)}) collective-permute-start(bf16[2048,384]{1,0:T(8,128)(2,1)S(1)} %get-tuple-element.294.refs_1_), channel_id=1, source_target_pairs={{0,4},{1,5},{2,6},{3,7},{4,0},{5,1},{6,2},{7,3},{8,12},{9,13},{10,... | collective-permute-start | bytes 4718600 | tf_op jit(solution)/shard_map/ppermute | solution.py:255
  220.8 35.7 %collective-permute-start.48 = (bf16[2048,256]{1,0:T(8,128)(2,1)S(1)}, bf16[2048,256]{1,0:T(8,128)(2,1)S(1)}, u32[]{:S(2)}, u32[]{:S(2)}) collective-permute-start(bf16[2048,256]{1,0:T(8,128)(2,1)S(1)} %get-tuple-element.295.refs_2_), channel_id=1, source_target_pairs={{0,8},{1,9},{2,10},{3,11},{4,12},{5,13},{6,14},{7,15},{8,0},{9,1},... | collective-permute-start | bytes 3145736 | tf_op jit(solution)/shard_map/ppermute | solution.py:255
  224.5 31.4 %collective-permute-start.49 = (bf16[256,1024]{1,0:T(8,128)(2,1)}, bf16[256,1024]{1,0:T(8,128)(2,1)S(1)}, u32[]{:S(2)}, u32[]{:S(2)}) collective-permute-start(bf16[256,1024]{1,0:T(8,128)(2,1)} %pad_maximum_fusion.6), channel_id=1, source_target_pairs={{0,16},{1,17},{2,18},{3,19},{4,20},{5,21},{6,22},{7,23},{8,24},{9,... | collective-permute-start | bytes 1572872 | tf_op jit(solution)/shard_map/ppermute | solution.py:261
  224.6 31.3 %collective-permute-start.50 = (bf16[256,1024]{1,0:T(8,128)(2,1)S(1)}, bf16[256,1024]{1,0:T(8,128)(2,1)}, u32[]{:S(2)}, u32[]{:S(2)}) collective-permute-start(bf16[256,1024]{1,0:T(8,128)(2,1)S(1)} %copy-done.30), channel_id=1, source_target_pairs={{0,1},{1,0},{2,3},{3,2},{4,5},{5,4},{6,7},{7,6},{8,9},{9,8},{10,11... | collective-permute-start | bytes 1572872 | tf_op jit(solution)/shard_map/ppermute | solution.py:255
  256.5 7.9 %collective-permute-start.51 = (bf16[128,1024]{1,0:T(8,128)(2,1)S(1)}, bf16[128,1024]{1,0:T(8,128)(2,1)S(1)}, u32[]{:S(2)}, u32[]{:S(2)}) collective-permute-start(bf16[128,1024]{1,0:T(8,128)(2,1)S(1)} %get-tuple-element.315), channel_id=1, source_target_pairs={{0,1},{1,0},{2,3},{3,2},{4,5},{5,4},{6,7},{7,6},{8,9},{9,8},{10,11... | collective-permute-start | bytes 786440 | tf_op jit(solution)/shard_map/ppermute | solution.py:255
  274.3 7.7 %collective-permute-start.54 = (f32[3,1024]{1,0:T(4,128)S(1)}, f32[3,1024]{1,0:T(4,128)S(1)}, u32[]{:S(2)}, u32[]{:S(2)}) collective-permute-start(f32[3,1024]{1,0:T(4,128)S(1)} %add.171), channel_id=1, source_target_pairs={{0,8},{1,9},{2,10},{3,11},{4,12},{5,13},{6,14},{7,15},{8,0},{9,1},... | collective-permute-start | bytes 36872 | tf_op jit(solution)/shard_map/ppermute | solution.py:255
  286.3 31.5 %all-to-all-start.1 = ((bf16[8,128,512]{2,1,0:T(8,128)(2,1)}), bf16[8,128,512]{2,1,0:T(8,128)(2,1)S(1)}, u32[]{:S(2)}, u32[]{:S(2)}) async-start(bf16[8,128,512]{2,1,0:T(8,128)(2,1)} %shard_map.62), calls=%async_computation.1 | async-start | bytes 2097152 | tf_op jit(solution)/shard_map/all_to_all | solution.py:269
  290.0 26.2 %collective-permute-start.58 = (bf16[128,2048]{1,0:T(8,128)(2,1)S(1)}, bf16[128,2048]{1,0:T(8,128)(2,1)S(1)}, u32[]{:S(2)}, u32[]{:S(2)}) collective-permute-start(bf16[128,2048]{1,0:T(8,128)(2,1)S(1)} %get-tuple-element.341), channel_id=1, source_target_pairs={{0,16},{1,17},{2,18},{3,19},{4,20},{5,21},{6,22},{7,23},{8,24},{9,... | collective-permute-start | bytes 1572872 | tf_op jit(solution)/shard_map/ppermute | solution.py:261
  (49 other events, 376.0 us)
